TPU v7x, 32 devices: a whole 2x2x4 slice. The times are simulated.
32 devices in a mesh: req: 4 (over y, x), hid: 8 (over z, core).
Axes of the slice: x: 2, y: 2, z: 4, core: 2. Of those that a mesh axis runs over, the one named last changes fastest.
Arguments:
- input_activations: bfloat16 [4, 512, 4096], P('req'), may hold values from -6 to 6
- prompt_extents: int32 [4], P('req'), may hold values from 1 to 512, as said below
- continuing_flags: int32 [4], P('req'), may hold values from 0 to 1, as said below
- owning_index: int32 [4], P('req'), may hold values from 0 to 7
- partition_arrangement: int32 [32], replicated, may hold values from 0 to 31, each once
- training_accept_pieces: float32 [4096, 4096], P(('req', 'hid')), may hold values from -0.09375 to 0.09375
- training_lookup_pieces: float32 [4096, 4096], P(('req', 'hid')), may hold values from -0.09375 to 0.09375
- training_content_pieces: float32 [4096, 4096], P(('req', 'hid')), may hold values from -0.09375 to 0.09375
- normalizer_scales: bfloat16 [2, 4096], replicated, may hold values from 0.5 to 1.5
- prior_step_blends: bfloat16 [7, 4096], replicated, may hold values from 0.049804688 to 0.94921875
- forgetting_bias_vector: float32 [4096], P('hid'), may hold values from -7 to -3
- forgetting_left_lowrank: bfloat16 [4096, 128], replicated, may hold values from -0.09375 to 0.09375
- forgetting_right_lowrank: bfloat16 [128, 4096], P(None, 'hid'), may hold values from -0.5 to 0.5
- instant_emphasis: float32 [4096], P('hid'), may hold values from -3 to 3
- group_normalizer_scale: float32 [4096], P('hid'), may hold values from 0.5 to 1.5
- gating_projection: bfloat16 [4096, 4096], P(None, 'hid'), may hold values from -0.09375 to 0.09375
- mixing_exit_projection: bfloat16 [4096, 4096], P('hid'), may hold values from -0.09375 to 0.09375
- kept_summary_places: float32 [4, 8, 64, 64, 64], P('req', 'hid'), may hold values from -6 to 6
- previous_normed_entries: bfloat16 [4, 2, 4096], P('req'), may hold values from -6 to 6
- feedforward_entry_proj: bfloat16 [14336, 4096], P(('req', 'hid')), may hold values from -0.09375 to 0.09375
- feedforward_exit_proj: bfloat16 [14336, 4096], P(('req', 'hid')), may hold values from -0.046875 to 0.046875
- feedforward_accept_proj: bfloat16 [4096, 4096], P(None, 'hid'), may hold values from -0.09375 to 0.09375
Outputs:
- layer_out: bfloat16 [4, 512, 4096], P('req', None, 'hid')
- new_states: float32 [4, 64, 64, 64], P('req', 'hid')
- new_shift: bfloat16 [4, 2, 4096], P('req')
Inputs may be any that keep to these rules, and one draw needn't show every extreme that they name: `prompt_extents`: in every draw some request has length 512. `continuing_flags`: at least one request has 1 and at least one has 0. `owning_index`: read only where continuing_flags is 1. `partition_arrangement`: each of 0 to 31 appears once.
All inputs are finite; a program needn't handle non-finite values.
Results may differ from a plain program's by a relative error of at most 0.02.
Values may be sent and summed in bfloat16 or wider, within the bound.
No kernel may reach another device: no remote copies, remote signals or barrier semaphores. Data moves between devices by JAX's collectives and lax.ppermute only.
A program may use at most 256 MiB of HBM per device.

v0:
```python
from functools import partial

import jax
import jax.numpy as jnp
from jax import lax
from jax.sharding import PartitionSpec as P

GROUP_DIMENSION = 64


def layer_norm(values, gain):
    center = values - jnp.mean(values, axis=-1, keepdims=True)
    spread = jnp.mean(center * center, axis=-1, keepdims=True)
    return center / jnp.sqrt(spread + 1e-05) * gain


def head_norm(outputs, gain_rows):
    center = outputs - jnp.mean(outputs, axis=-1, keepdims=True)
    spread = jnp.mean(center * center, axis=-1, keepdims=True)
    return center / jnp.sqrt(spread + 0.00064) * gain_rows


def shifted(values, first_row):
    return jnp.concatenate([first_row[None, :], values[:-1]], axis=0)


def segment_step(extra_diagonal_term, carried_summary, piece_sequence):
    acceptance_vectors, present_lookup_vectors, content_vectors, decays = piece_sequence
    inclusive = jnp.cumsum(decays, axis=0)
    exclusive = inclusive - decays
    closing = inclusive[-1]
    resulting_activations = jnp.einsum(
        "thi,hij->thj",
        acceptance_vectors * jnp.exp(exclusive),
        carried_summary,
        precision=lax.Precision.HIGHEST,
    )
    distance = exclusive[:, None] - inclusive[None, :]
    sizing = decays.shape[0]
    earlier = (jnp.arange(sizing)[:, None] > jnp.arange(sizing)[None, :]).astype(jnp.float32)
    factor = jnp.exp(jnp.minimum(distance, 0.0)) * earlier[:, :, None, None]
    scores = jnp.sum(
        acceptance_vectors[:, None] * factor * present_lookup_vectors[None, :], axis=-1
    )
    resulting_activations = resulting_activations + jnp.einsum(
        "tsh,shj->thj", scores, content_vectors, precision=lax.Precision.HIGHEST
    )
    resulting_activations = (
        resulting_activations
        + jnp.sum(
            acceptance_vectors * extra_diagonal_term * present_lookup_vectors,
            axis=-1,
            keepdims=True,
        )
        * content_vectors
    )
    weighted = present_lookup_vectors * jnp.exp(closing[None] - inclusive)
    carried_summary = jnp.exp(closing)[:, :, None] * carried_summary + jnp.einsum(
        "shi,shj->hij", weighted, content_vectors, precision=lax.Precision.HIGHEST
    )
    return (carried_summary, resulting_activations)


def local(
    input_activations,
    prompt_extents,
    continuing_flags,
    owning_index,
    partition_arrangement,
    training_accept_pieces,
    training_lookup_pieces,
    training_content_pieces,
    normalizer_scales,
    prior_step_blends,
    forgetting_bias_vector,
    forgetting_left_lowrank,
    forgetting_right_lowrank,
    instant_emphasis,
    group_normalizer_scale,
    gating_projection,
    mixing_exit_projection,
    kept_summary_places,
    previous_normed_entries,
    feedforward_entry_proj,
    feedforward_exit_proj,
    feedforward_accept_proj,
):
    token_rows = input_activations[0]
    seq_len, width = token_rows.shape
    local_width = mixing_exit_projection.shape[0]
    groups_on_device = local_width // GROUP_DIMENSION
    shards = partition_arrangement.shape[0]
    shard_rows = width // shards
    length = prompt_extents[0]
    resuming = continuing_flags[0]
    present = jnp.arange(seq_len) < length
    gain_rows = normalizer_scales.astype(jnp.float32)
    mix_rows = prior_step_blends.astype(jnp.float32)
    carried = previous_normed_entries[0].astype(jnp.float32)
    normed_in = layer_norm(token_rows.astype(jnp.float32), gain_rows[0])
    before = shifted(normed_in, jnp.where(resuming == 1, carried[0], 0.0))
    blended = (normed_in[None] + (before - normed_in)[None] * mix_rows[:5, None, :]).astype(
        jnp.bfloat16
    )
    permuted = jnp.take(
        blended[:3].reshape(3, seq_len, shards, shard_rows), partition_arrangement, axis=2
    ).reshape(3, seq_len, width)
    local_rows = jnp.stack(
        [training_accept_pieces, training_lookup_pieces, training_content_pieces]
    ).astype(jnp.bfloat16)
    collected = lax.all_gather(local_rows, "req", axis=1, tiled=True)
    swapped = lax.all_to_all(collected, "hid", split_axis=2, concat_axis=1, tiled=True)
    hid_count = lax.axis_size("hid")
    req_count = lax.axis_size("req")
    ordered = (
        swapped.reshape(3, hid_count, req_count, shard_rows, local_width)
        .transpose(0, 2, 1, 3, 4)
        .reshape(3, width, local_width)
    )
    projected = jnp.einsum("mtd,mdc->mtc", permuted, ordered, preferred_element_type=jnp.float32)
    low_rank = jnp.tanh(
        jnp.dot(blended[3], forgetting_left_lowrank, preferred_element_type=jnp.float32)
    ).astype(jnp.bfloat16)
    log_decay = -jnp.exp(
        forgetting_bias_vector
        + jnp.dot(low_rank, forgetting_right_lowrank, preferred_element_type=jnp.float32)
    )
    log_decay = jnp.where(present[:, None], log_decay, 0.0)
    gate = jax.nn.silu(jnp.dot(blended[4], gating_projection, preferred_element_type=jnp.float32))
    present_lookup_vectors = jnp.where(present[:, None], projected[1], 0.0)
    fetched = lax.all_to_all(
        kept_summary_places.astype(jnp.bfloat16), "hid", split_axis=2, concat_axis=1, tiled=True
    ).astype(kept_summary_places.dtype)
    chosen = lax.dynamic_index_in_dim(fetched[0], owning_index[0], 0, keepdims=False)
    carried_summary = jnp.where(resuming == 1, chosen, 0.0)
    block_len = min(64, seq_len)
    count_blocks = seq_len // block_len

    def by_blocks(values):
        return values.reshape(count_blocks, block_len, groups_on_device, GROUP_DIMENSION)

    sequences = (
        by_blocks(projected[0]),
        by_blocks(present_lookup_vectors),
        by_blocks(projected[2]),
        by_blocks(log_decay),
    )
    segment_cursor = partial(
        segment_step, instant_emphasis.reshape(groups_on_device, GROUP_DIMENSION)
    )
    carried_summary, outputs = lax.scan(segment_cursor, carried_summary, sequences)
    outputs = outputs.reshape(seq_len, groups_on_device, GROUP_DIMENSION)
    grouped = head_norm(
        outputs, group_normalizer_scale.reshape(groups_on_device, GROUP_DIMENSION)
    ).reshape(seq_len, local_width)
    gated = (grouped * gate).astype(jnp.bfloat16)
    head_terms = jnp.dot(gated, mixing_exit_projection, preferred_element_type=jnp.float32)
    attended = lax.psum(head_terms.astype(jnp.bfloat16), "hid").astype(jnp.float32)
    middle = (token_rows.astype(jnp.float32) + attended).astype(jnp.bfloat16)
    mid_share = lax.dynamic_slice_in_dim(
        middle, lax.axis_index("hid") * local_width, local_width, 1
    )
    chan_in = layer_norm(middle.astype(jnp.float32), gain_rows[1])
    chan_before = shifted(chan_in, jnp.where(resuming == 1, carried[1], 0.0))
    chan_mixed = (chan_in[None] + (chan_before - chan_in)[None] * mix_rows[5:, None, :]).astype(
        jnp.bfloat16
    )
    key_rows = lax.all_gather(feedforward_entry_proj, "req", axis=0, tiled=True)
    value_rows = lax.all_gather(feedforward_exit_proj, "req", axis=0, tiled=True)
    inner = lax.dot_general(
        chan_mixed[0], key_rows, (((1,), (1,)), ((), ())), preferred_element_type=jnp.float32
    )
    hidden = jnp.square(jnp.maximum(inner, 0.0)).astype(jnp.bfloat16)
    channel_terms = jnp.dot(hidden, value_rows, preferred_element_type=jnp.float32)
    mixed_out = lax.psum_scatter(
        channel_terms.astype(jnp.bfloat16), "hid", scatter_dimension=1, tiled=True
    ).astype(jnp.float32)
    gate_rows = jax.nn.sigmoid(
        jnp.dot(chan_mixed[1], feedforward_accept_proj, preferred_element_type=jnp.float32)
    )
    combined = mid_share.astype(jnp.float32) + gate_rows * mixed_out
    layer_out = jnp.where(present[:, None], combined, 0.0).astype(jnp.bfloat16)[None]
    last_index = length - 1
    shift_out = jnp.stack(
        [
            lax.dynamic_index_in_dim(normed_in, last_index, 0, keepdims=False),
            lax.dynamic_index_in_dim(chan_in, last_index, 0, keepdims=False),
        ]
    ).astype(jnp.bfloat16)[None]
    return (layer_out, carried_summary[None], shift_out)


def solution(mesh):
    placed = (
        P("req", None, None),
        P("req"),
        P("req"),
        P("req"),
        P(),
        P(("req", "hid"), None),
        P(("req", "hid"), None),
        P(("req", "hid"), None),
        P(),
        P(),
        P("hid"),
        P(),
        P(None, "hid"),
        P("hid"),
        P("hid"),
        P(None, "hid"),
        P("hid", None),
        P("req", "hid", None, None, None),
        P("req", None, None),
        P(("req", "hid"), None),
        P(("req", "hid"), None),
        P(None, "hid"),
    )
    return jax.shard_map(
        local,
        mesh=mesh,
        in_specs=placed,
        out_specs=(P("req", None, "hid"), P("req", "hid", None, None), P("req", None, None)),
        check_vma=False,
    )
```

profile of v0, /device:TPU:0, one launch (start us, length us, event | category | flops | bytes accessed | tf_op | source)
XLA Modules:
  0.0 1237.8 jit_solution(1955270005850321650)
XLA Ops:
  9.0 2.5 convert_bitcast_fusion.1
  16.8 6.3 all-to-all-start
  23.2 115.7 %all-gather.4.cloned.1.call-done = bf16[3,512,4096]{2,1,0:T(8,128)(2,1)} async-done(((bf16[3,128,4096]{2,1,0:T(8,128)(2,1)}), bf16[3,512,4096]{2,1,0:T(8,128)(2,1)}) %all-gather.4.cloned.1.call-update) | async-done | bytes 12582928 | tf_op jit(solution)/shard_map/all_gather | solution.py:111
  138.9 27.0 %copy.120 = bf16[3,512,4096]{1,0,2:T(4,128)(2,1)} copy(bf16[3,512,4096]{2,1,0:T(8,128)(2,1)} %all-gather.4.cloned.1.call-done) | data formatting | bytes 25165824 | tf_op jit(solution)/shard_map/all_gather | solution.py:111
  165.9 5.9 all-to-all-start.1
  172.7 3.0 convert_reduce_fusion
  175.7 3.4 fusion.18
  183.4 2.3 copy-done.6
  185.8 7.5 fusion.26
  193.3 9.0 copy.116
  202.3 9.0 copy.117
  211.3 10.3 add_convert_fusion
  221.6 6.4 slice.77
  228.1 4.3 copy-done.5
  232.4 16.6 %copy.118 = bf16[3,512,32,128]{3,1,2,0:T(8,128)(2,1)} copy(bf16[3,512,32,128]{1,3,2,0:T(8,128)(2,1)} %bitcast.201) | data formatting | bytes 25165824 | tf_op jit(solution)/shard_map/reshape | solution.py:106
  249.0 11.3 gather_fusion
  260.3 16.7 %copy.119 = bf16[3,512,32,128]{1,3,2,0:T(8,128)(2,1)} copy(bf16[3,512,32,128]{3,1,0,2:T(8,128)(2,1)} %bitcast.202) | data formatting | bytes 25165824 | tf_op jit(solution)/shard_map/jit(_take)/gather | solution.py:105
  277.6 3.8 fusion.36
  284.0 11.1 bitcast_select_fusion
  295.9 239.6 %all-to-all-done.1 = bf16[3,512,4096]{1,0,2:T(4,128)(2,1)} async-done(((bf16[3,512,4096]{1,0,2:T(4,128)(2,1)}), bf16[3,512,4096]{1,0,2:T(4,128)(2,1)}, u32[]{:S(2)}, u32[]{:S(2)}) %all-to-all-start.1) | async-done | bytes 12582944 | tf_op jit(solution)/shard_map/all_to_all | solution.py:112
  535.4 13.2 %copy.121 = bf16[3,512,4096]{1,2,0:T(8,128)(2,1)} copy(bf16[3,512,4096]{1,0,2:T(4,128)(2,1)} %all-to-all-done.1) | data formatting | bytes 25165824 | tf_op jit(solution)/shard_map/all_to_all | solution.py:112
  548.6 16.8 %copy.122 = bf16[3,8,512,512]{3,2,1,0:T(8,128)(2,1)} copy(bf16[3,8,512,512]{2,3,1,0:T(8,128)(2,1)} %bitcast.199) | data formatting | bytes 25165824 | tf_op jit(solution)/shard_map/all_to_all | solution.py:112
  565.4 10.5 copy.123
  575.9 13.5 %fusion.56 = f32[3,512,512]{2,1,0:T(8,128)S(1)} fusion(bf16[3,512,4096]{1,2,0:T(8,128)(2,1)} %bitcast_select_fusion, bf16[3,4096,512]{2,1,0:T(8,128)(2,1)} %bitcast.204), kind=kOutput, calls=%fused_computation.115 | convolution fusion | flops 6442450944 | bytes 28311552 | tf_op jit(solution)/shard_map/mtd,mdc->mtc/dot_general | solution.py:120
  592.7 2.7 reshape_squeeze.6
  598.9 148.8 %while.12 = (s32[]{:T(128)}, f32[8,64,64]{2,1,0:T(8,128)S(1)}, f32[8,64,8,64]{3,1,2,0:T(8,128)}, f32[8,64,8,64]{3,2,1,0:T(8,128)}, f32[8,64,8,64]{3,2,1,0:T(8,12...) while((s32[]{:T(128)}, f32[8,64,64]{2,1,0:T(8,128)S(1)}, ...), condition=%wide.region_6.7_spmd, body=%wide.region_2.6_spmd.sunk | while | flops 90512896 | bytes 5305449 | solution.py:151
  602.9 9.7 multiply_reduce_fusion.6
  621.5 9.7 multiply_reduce_fusion.6
  640.1 9.7 multiply_reduce_fusion.6
  658.8 9.7 multiply_reduce_fusion.6
  677.4 9.7 multiply_reduce_fusion.6
  696.0 9.7 multiply_reduce_fusion.6
  714.6 9.7 multiply_reduce_fusion.6
  733.2 9.7 multiply_reduce_fusion.6
  747.8 2.9 copy.127
  750.7 2.2 reduce_sum.74
  752.9 2.9 multiply_reduce_fusion.2
  758.4 11.7 convolution_convert_fusion.1
  771.5 93.2 %all-reduce.2.cloned.1.call-done = bf16[512,4096]{1,0:T(8,128)(2,1)} async-done(((bf16[512,4096]{1,0:T(8,128)(2,1)}), bf16[512,4096]{1,0:T(8,128)(2,1)}) %all-reduce.2.cloned.1.call-update) | async-done | bytes 4194320 | tf_op jit(solution)/shard_map/psum | solution.py:158
  864.7 5.2 convert_reduce_fusion.1
  871.2 2.1 fusion.21
  873.3 3.5 maximum_subtract_fusion.1
  877.8 5.0 add_convert_fusion.1
  882.8 123.8 %all-gather.6.cloned.1.call-done = bf16[1792,4096]{1,0:T(8,128)(2,1)} async-done(((bf16[448,4096]{1,0:T(8,128)(2,1)}), bf16[1792,4096]{1,0:T(8,128)(2,1)}) %all-gather.6.cloned.1.call-update) | async-done | bytes 14680080 | tf_op jit(solution)/shard_map/all_gather | solution.py:168
  1006.6 141.7 %all-gather.8.cloned.1.call-done = bf16[1792,4096]{1,0:T(8,128)(2,1)} async-done(((bf16[448,4096]{1,0:T(8,128)(2,1)}), bf16[1792,4096]{1,0:T(8,128)(2,1)}) %all-gather.8.cloned.1.call-update) | async-done | bytes 14680080 | tf_op jit(solution)/shard_map/all_gather | solution.py:169
  1148.3 25.6 %convolution_convert_fusion = bf16[512,4096]{1,0:T(8,128)(2,1)} fusion(bf16[1792,4096]{1,0:T(8,128)(2,1)} %all-gather.8.cloned.1.call-done, bf16[1792,4096]{1,0:T(8,128)(2,1)} %all-gather.6.cloned.1.call-done, bf16[2,512,4096]{2,1,0:T(8,128)(2,1)} %add_convert_fusion.1), kind=kOutput, calls=%fused_computation.52 | convolution fusion | flops 15037235200 | bytes 37748736 | tf_op jit(solution)/shard_map/dot_general | solution.py:174
  1176.5 47.6 %reduce-scatter.2.cloned.1.call-done = bf16[512,512]{1,0:T(8,128)(2,1)} async-done(((bf16[512,4096]{1,0:T(8,128)(2,1)}), bf16[512,512]{1,0:T(8,128)(2,1)}) %reduce-scatter.2.cloned.1.call-update) | async-done | bytes 524304 | tf_op jit(solution)/shard_map/reduce_scatter | solution.py:175
  1224.1 7.0 fusion.43
  (195 shorter events, 100.4 us)
Async XLA Ops:
  7.2 270.4 %copy-start = (bf16[4096,128]{1,0:T(8,128)(2,1)S(1)}, bf16[4096,128]{1,0:T(8,128)(2,1)}, u32[]{:S(2)}) copy-start(bf16[4096,128]{1,0:T(8,128)(2,1)} %param.35) | copy-start | bytes 3145732
  7.2 131.7 %all-gather.4.cloned.1.call-start = ((), (), s32[]{:S(2)}) async-start(), calls=%async_computation.3 | async-start | bytes 15728640 | tf_op jit(solution)/shard_map/all_gather | solution.py:111
  16.8 149.1 %all-to-all-start = ((bf16[8,2,16384]{2,1,0:T(2,128)(2,1)}), bf16[8,2,16384]{2,1,0:T(2,128)(2,1)S(1)}, u32[]{:S(2)}, u32[]{:S(2)}) async-start(bf16[8,2,16384]{2,1,0:T(2,128)(2,1)} %reshape.260), calls=%async_computation | async-start | bytes 1048576 | tf_op jit(solution)/shard_map/all_to_all | solution.py:131
  165.9 6.8 copy-start.14
  165.9 369.5 %all-to-all-start.1 = ((bf16[3,512,4096]{1,0,2:T(4,128)(2,1)}), bf16[3,512,4096]{1,0,2:T(4,128)(2,1)}, u32[]{:S(2)}, u32[]{:S(2)}) async-start(bf16[3,512,4096]{1,0,2:T(4,128)(2,1)} %copy.120), calls=%async_computation.1 | async-start | bytes 33554432 | tf_op jit(solution)/shard_map/all_to_all | solution.py:112
  171.8 7.4 copy-start.11
  171.8 692.9 %all-reduce.2.cloned.1.call-start = ((), (), s32[]{:S(2)}) async-start(), calls=%async_computation.4 | async-start | bytes 8388608 | tf_op jit(solution)/shard_map/psum | solution.py:158
  171.9 8.6 copy-start.2
  182.4 3.3 copy-start.6
  202.3 9.0 copy-start.8
  221.6 10.7 copy-start.5
  232.4 16.6 %copy-start.18 = (s32[32]{0:T(128)S(1)}, s32[32]{0:T(128)}, u32[]{:S(2)}) copy-start(s32[32]{0:T(128)} %param.28) | copy-start | bytes 388
  260.3 17.3 %copy-start.15 = (bf16[128,512]{1,0:T(8,128)(2,1)S(1)}, bf16[128,512]{1,0:T(8,128)(2,1)}, u32[]{:S(2)}) copy-start(bf16[128,512]{1,0:T(8,128)(2,1)} %param.36) | copy-start | bytes 393220
  260.3 17.3 %copy-start.16 = (f32[512]{0:T(512)S(1)}, f32[512]{0:T(512)}, u32[]{:S(2)}) copy-start(f32[512]{0:T(512)} %param.34) | copy-start | bytes 6148
  591.1 7.8 copy-start.13
  747.7 10.7 copy-start.7
  747.8 10.7 copy-start.17
  770.1 1.4 copy-start.9
  770.1 236.5 %all-gather.6.cloned.1.call-start = ((), (), s32[]{:S(2)}) async-start(), calls=%async_computation.5 | async-start | bytes 18350080 | tf_op jit(solution)/shard_map/all_gather | solution.py:168
  770.9 377.4 %all-gather.8.cloned.1.call-start = ((), (), s32[]{:S(2)}) async-start(), calls=%async_computation.6 | async-start | bytes 18350080 | tf_op jit(solution)/shard_map/all_gather | solution.py:169
  771.5 452.7 %reduce-scatter.2.cloned.1.call-start = ((), (), s32[]{:S(2)}) async-start(), calls=%async_computation.7 | async-start | bytes 4718592 | tf_op jit(solution)/shard_map/reduce_scatter | solution.py:175
  771.5 99.6 %copy-start.10 = (f32[1,4096]{1,0:T(1,128)S(1)}, f32[1,4096]{1,0:T(1,128)}, u32[]{:S(2)}) copy-start(f32[1,4096]{1,0:T(1,128)} %get-tuple-element.127) | copy-start | bytes 49156
  869.9 3.4 copy-start.4
  869.9 3.4 copy-start.12
  873.2 4.6 copy-start.3
  1175.8 55.3 %copy-start.1 = (bf16[4096,128]{1,0:T(8,128)(2,1)S(1)}, bf16[4096,128]{1,0:T(8,128)(2,1)}, u32[]{:S(2)}) copy-start(bf16[4096,128]{1,0:T(8,128)(2,1)} %param.35) | copy-start | bytes 3145732
Sparse Core Ops, SparseCore 0:
  13.7 125.2 all-gather.3
  770.3 94.4 all-reduce.1
  866.6 140.0 all-gather.5
  1008.3 139.9 all-gather.7
  1174.1 50.0 reduce-scatter.1
where the time goes:
time: 1250 us; the launch traced here: 1240 us
  waiting for transfers between devices  763 us (61%)
  other arithmetic  180 us (14%)
  local copies, waits for them, and re-layouts  179 us (14%)
  matrix products  87 us (7%)
  between operations  16.5 us (1%)
    all_to_all x1, waiting for transfers between devices, local(): lax.all_to_all(collected, 'hid', split_axis=2, concat_axis=1, tiled=True)  240 us
    all_gather x1, waiting for transfers between devices, local(): lax.all_gather(feedforward_exit_proj, 'req', axis=0, tiled=True)  142 us
    all_gather x1, waiting for transfers between devices, local(): key_rows = lax.all_gather(feedforward_entry_proj, 'req', axis=0, tiled=True)  124 us
    all_gather x1, waiting for transfers between devices, local(): collected = lax.all_gather(local_rows, 'req', axis=1, tiled=True)  116 us
    psum x1, waiting for transfers between devices, local(): lax.psum(head_terms.astype(jnp.bfloat16), 'hid').astype(jnp.float32)  93.2 us
    reduce_sum x8, other arithmetic, segment_step(): jnp.sum(acceptance_vectors[:, None] * factor * present_lookup_vectors[Non...  77.6 us
    reduce_scatter x1, waiting for transfers between devices, local(): lax.psum_scatter(channel_terms.astype(jnp.bfloat16), 'hid', scatter_dimen...  47.6 us
    all_to_all x2, local copies, waits for them, and re-layouts, local(): lax.all_to_all(collected, 'hid', split_axis=2, concat_axis=1, tiled=True)  30 us
  transfers between devices with their start and end apart: 7, of which 6 were waited for; matrix products, arithmetic and copies ran while one was open for 13% of the time, Pallas kernels for 0%

commit v1 on v0

v1 whole, which is shorter than its diff:
```python
from functools import partial

import jax
import jax.numpy as jnp
from jax import lax
from jax.experimental import pallas as pl
from jax.experimental.pallas import tpu as pltpu
from jax.sharding import PartitionSpec as P

GROUP_DIMENSION = 64
PAIR = 2 * GROUP_DIMENSION
CHUNK = 64
BF16 = jnp.bfloat16
F32 = jnp.float32


def layer_norm(values, gain):
    center = values - jnp.mean(values, axis=-1, keepdims=True)
    spread = jnp.mean(center * center, axis=-1, keepdims=True)
    return center / jnp.sqrt(spread + 1e-05) * gain


def shifted(values, first_row):
    return jnp.concatenate([first_row[None, :], values[:-1]], axis=0)


def matmul(a, b):
    return jnp.dot(a, b, preferred_element_type=F32)


def matmul_nt(a, b):
    return lax.dot_general(a, b, (((1,), (1,)), ((), ())), preferred_element_type=F32)


def matmul_tn(a, b):
    return lax.dot_general(a, b, (((0,), (0,)), ((), ())), preferred_element_type=F32)


class Exchange:
    WINDOW = 3

    def __init__(self, req):
        self.req = req
        self.sent = {1: [], 2: []}

    def send(self, value, axis):
        past = self.sent[axis]
        if len(past) >= self.WINDOW:
            value, _ = lax.optimization_barrier((value, past[-self.WINDOW]))
        got = lax.ppermute(value, "req", [(i, i ^ axis) for i in range(4)])
        past.append(got)
        return got

    def near(self, value):
        return {0: value, 1: self.send(value, 1), 2: self.send(value, 2)}

    def far(self, pieces, axis):
        pieces[3] = self.send(pieces[3 - axis], axis)

    def whole(self, value):
        blocks = lax.all_gather(value, "req", axis=0, tiled=False)
        me = lax.axis_index("req")
        return {
            d: lax.dynamic_index_in_dim(blocks, me ^ d, 0, keepdims=False)
            for d in range(self.req)
        }


def by_head(values, first_lanes):
    zeros = jnp.zeros_like(values)
    return jnp.concatenate(
        [jnp.where(first_lanes, values, zeros), jnp.where(first_lanes, zeros, values)], axis=0
    )


def split_matmul(values, weights):
    high = values.astype(BF16)
    low = (values - high.astype(F32)).astype(BF16)
    return matmul(high, weights) + matmul(low, weights)


def recurrence_kernel(
    length_ref,
    rec_ref,
    key_ref,
    val_ref,
    decay_ref,
    gate_ref,
    bias_ref,
    bonus_ref,
    gain_ref,
    start_ref,
    gated_ref,
    state_ref,
    held,
):
    length = length_ref[0]
    tokens = rec_ref.shape[0]
    size = min(CHUNK, tokens)
    lanes = lax.broadcasted_iota(jnp.int32, (size, PAIR), 1)
    first_lanes = lanes < GROUP_DIMENSION
    row_of = lax.broadcasted_iota(jnp.int32, (size, PAIR), 0)
    t_of = lax.broadcasted_iota(jnp.int32, (size, 2 * size), 0)
    s_of = lax.broadcasted_iota(jnp.int32, (size, 2 * size), 1) & (size - 1)
    side_a = lax.broadcasted_iota(jnp.int32, (PAIR, PAIR), 0) < GROUP_DIMENSION
    side_b = lax.broadcasted_iota(jnp.int32, (PAIR, PAIR), 1) < GROUP_DIMENSION
    own_head = side_a == side_b
    average = jnp.where(own_head, 1.0 / GROUP_DIMENSION, 0.0).astype(BF16)
    start = start_ref[...].reshape(PAIR, GROUP_DIMENSION)
    held[...] = jnp.where(own_head, jnp.concatenate([start, start], axis=1), 0.0).T
    bias = bias_ref[...]
    bonus = bonus_ref[...]
    gain = gain_ref[...]
    for index in range(tokens // size):
        rows = pl.ds(index * size, size)
        present = row_of + index * size < length
        rec = rec_ref[rows, :]
        key = jnp.where(present, key_ref[rows, :], 0.0)
        val = val_ref[rows, :].astype(BF16)
        total = jnp.where(present, -jnp.exp(bias + decay_ref[rows, :]), 0.0)
        scores = jnp.where(
            t_of == s_of,
            matmul_nt((rec * bonus).astype(BF16), by_head(key.astype(BF16), first_lanes)),
            0.0,
        )
        before = jnp.zeros_like(total)
        after = jnp.zeros_like(total)
        span = 1
        while span < size:
            later = (row_of & span) != 0
            scaled = (jnp.where(later, rec, key) * jnp.exp(jnp.where(later, before, after))).astype(
                BF16
            )
            pairs = matmul_nt(scaled, by_head(scaled, first_lanes))
            chosen = (
                ((t_of & span) != 0)
                & ((s_of & span) == 0)
                & ((t_of & (-2 * span)) == (s_of & (-2 * span)))
            )
            scores = jnp.where(chosen, pairs, scores)
            partner = jnp.where(
                later, pltpu.roll(total, span, 0), pltpu.roll(total, size - span, 0)
            )
            before = before + jnp.where(later, partner, 0.0)
            after = after + jnp.where(later, 0.0, partner)
            total = total + partner
            span *= 2
        state = held[...]
        out = matmul(scores.astype(BF16), by_head(val, first_lanes))
        out = out + matmul_nt((rec * jnp.exp(before)).astype(BF16), state.astype(BF16))
        update = matmul_tn(val, (key * jnp.exp(after)).astype(BF16))
        held[...] = state * jnp.exp(total[:1, :]) + jnp.where(own_head, update, 0.0)
        center = out - split_matmul(out, average)
        spread = split_matmul(center * center, average)
        grouped = center * lax.rsqrt(spread + 0.00064) * gain
        gate = gate_ref[rows, :]
        gated_ref[rows, :] = (grouped * (gate / (1.0 + jnp.exp(-gate)))).astype(BF16)
    final = held[...].T
    state_ref[...] = (final[:, :GROUP_DIMENSION] + final[:, GROUP_DIMENSION:]).reshape(
        state_ref.shape
    )


def recurrence(length, rec, key, val, decay, gate, bias, bonus, gain, start):
    tokens, width = rec.shape
    wide = pl.BlockSpec((tokens, PAIR), lambda p: (0, p))
    row = pl.BlockSpec((1, PAIR), lambda p: (0, p))
    states = pl.BlockSpec((2, GROUP_DIMENSION, GROUP_DIMENSION), lambda p: (p, 0, 0))
    return pl.pallas_call(
        recurrence_kernel,
        grid=(width // PAIR,),
        in_specs=[pl.BlockSpec(memory_space=pltpu.SMEM)] + [wide] * 5 + [row] * 3 + [states],
        out_specs=[wide, states],
        out_shape=[
            jax.ShapeDtypeStruct((tokens, width), BF16),
            jax.ShapeDtypeStruct(start.shape, F32),
        ],
        scratch_shapes=[pltpu.VMEM((PAIR, PAIR), F32)],
        compiler_params=pltpu.CompilerParams(vmem_limit_bytes=24 << 20),
        cost_estimate=pl.CostEstimate(
            flops=tokens * width * 4096, bytes_accessed=tokens * width * 22, transcendentals=0
        ),
        name="recurrence",
    )(length, rec, key, val, decay, gate, bias, bonus, gain, start)


def prepare_kernel(
    order_ref,
    length_ref,
    tokens_ref,
    gain_ref,
    first_ref,
    mix_ref,
    out0_ref,
    out1_ref,
    out2_ref,
    out3_ref,
    out4_ref,
    last_ref,
    mean_ref,
    root_ref,
):
    step = pl.program_id(0)
    block = out0_ref.shape[1]
    seq_len, width = tokens_ref.shape

    @pl.when(step == 0)
    def _():
        count = min(64, seq_len)
        for index in range(seq_len // count):
            rows = pl.ds(index * count, count)
            values = tokens_ref[rows, :].astype(F32)
            mean = jnp.mean(values, axis=1, keepdims=True)
            center = values - mean
            spread = jnp.mean(center * center, axis=1, keepdims=True)
            mean_ref[rows, :] = jnp.broadcast_to(mean, (count, 128))
            root_ref[rows, :] = jnp.broadcast_to(lax.rsqrt(spread + 1e-05), (count, 128))

    columns = pl.ds(pl.multiple_of(order_ref[step] * block, block), block)
    values = tokens_ref[:, columns].astype(F32)
    normed = (values - mean_ref[:, :1]) * root_ref[:, :1] * gain_ref[:1, columns]
    places = lax.broadcasted_iota(jnp.int32, normed.shape, 0)
    before = jnp.where(places == 0, first_ref[:1, columns], pltpu.roll(normed, 1, 0))
    change = before - normed
    for m, out_ref in enumerate((out0_ref, out1_ref, out2_ref, out3_ref, out4_ref)):
        out_ref[...] = (normed + change * mix_ref[m : m + 1, columns]).astype(BF16)
    last = places == length_ref[0] - 1
    last_ref[...] = jnp.sum(jnp.where(last, normed, 0.0), axis=0, keepdims=True)


def prepare(order, length, tokens, gain, first, mixes):
    seq_len, width = tokens.shape
    blocks = order.shape[0]
    block = width // blocks

    def rows(count):
        return pl.BlockSpec((count, width), lambda j, *_: (0, 0))

    moved = pl.BlockSpec((seq_len, block), lambda j, *_: (0, j))
    natural = pl.BlockSpec((seq_len, block), lambda j, order, *_: (0, order[j]))
    return pl.pallas_call(
        prepare_kernel,
        grid_spec=pltpu.PrefetchScalarGridSpec(
            num_scalar_prefetch=2,
            grid=(blocks,),
            in_specs=[rows(seq_len), rows(1), rows(1), rows(mixes.shape[0])],
            out_specs=[moved] * 3
            + [natural] * 2
            + [pl.BlockSpec((1, block), lambda j, order, *_: (0, order[j]))],
            scratch_shapes=[pltpu.VMEM((seq_len, 128), F32)] * 2,
        ),
        out_shape=[jax.ShapeDtypeStruct((seq_len, width), BF16)] * 5
        + [jax.ShapeDtypeStruct((1, width), F32)],
        compiler_params=pltpu.CompilerParams(vmem_limit_bytes=32 << 20),
        cost_estimate=pl.CostEstimate(
            flops=seq_len * width * 20, bytes_accessed=seq_len * width * 12, transcendentals=0
        ),
        name="prepare",
    )(order, length, tokens, gain, first, mixes)


def exit_kernel(count, *refs):
    hidden, values, out_ref = refs[:count], refs[count : 2 * count], refs[-1]
    total = matmul(hidden[0][...], values[0][...])
    for h, v in zip(hidden[1:], values[1:]):
        total = total + matmul(h[...], v[...])
    out_ref[...] = total.astype(BF16)


def exit_product(hidden, values):
    tokens = hidden[0].shape[0]
    width = values[0].shape[1]
    tile = min(512, width)
    return pl.pallas_call(
        partial(exit_kernel, len(hidden)),
        grid=(width // tile,),
        in_specs=[pl.BlockSpec(h.shape, lambda n: (0, 0)) for h in hidden]
        + [pl.BlockSpec((v.shape[0], tile), lambda n: (0, n)) for v in values],
        out_specs=pl.BlockSpec((tokens, tile), lambda n: (0, n)),
        out_shape=jax.ShapeDtypeStruct((tokens, width), BF16),
        compiler_params=pltpu.CompilerParams(vmem_limit_bytes=32 << 20),
        cost_estimate=pl.CostEstimate(
            flops=2 * tokens * width * sum(h.shape[1] for h in hidden),
            bytes_accessed=2 * width * (tokens + sum(v.shape[0] for v in values)),
            transcendentals=0,
        ),
        name="exit_product",
    )(*hidden, *values)


def local(
    input_activations,
    prompt_extents,
    continuing_flags,
    owning_index,
    partition_arrangement,
    training_accept_pieces,
    training_lookup_pieces,
    training_content_pieces,
    normalizer_scales,
    prior_step_blends,
    forgetting_bias_vector,
    forgetting_left_lowrank,
    forgetting_right_lowrank,
    instant_emphasis,
    group_normalizer_scale,
    gating_projection,
    mixing_exit_projection,
    kept_summary_places,
    previous_normed_entries,
    feedforward_entry_proj,
    feedforward_exit_proj,
    feedforward_accept_proj,
):
    hid = lax.axis_size("hid")
    req = lax.axis_size("req")
    here = lax.axis_index("req")
    slot = lax.axis_index("hid")
    token_rows = input_activations[0]
    seq_len, width = token_rows.shape
    local_width = mixing_exit_projection.shape[0]
    heads = local_width // GROUP_DIMENSION
    shards = partition_arrangement.shape[0]
    shard_rows = width // shards
    length = prompt_extents[0]
    resuming = continuing_flags[0]
    present = jnp.arange(seq_len) < length

    owned = (resuming == 1) & (owning_index[0] == slot)
    saved = jnp.where(owned, kept_summary_places[0, 0].astype(BF16), 0)
    start = lax.psum_scatter(
        saved.reshape(saved.shape[0], -1), "hid", scatter_dimension=0, tiled=True
    )
    start = start.astype(F32).reshape(heads, GROUP_DIMENSION, GROUP_DIMENSION)

    order = jnp.concatenate(
        [
            lax.dynamic_slice_in_dim(partition_arrangement, (here ^ d) * hid, hid, 0)
            for d in range(req)
        ]
    )
    gain_rows = normalizer_scales.astype(F32)
    mix_rows = prior_step_blends.astype(F32)
    carried = jnp.where(resuming == 1, previous_normed_entries[0].astype(F32), 0.0)
    if shard_rows % 128 == 0:
        *blended, last_in = prepare(
            order, prompt_extents, token_rows, gain_rows[:1], carried[:1], mix_rows[:5]
        )
    else:
        normed_in = layer_norm(token_rows.astype(F32), gain_rows[0])
        before = shifted(normed_in, carried[0])
        blended = [
            (normed_in + (before - normed_in) * mix_rows[m][None, :]).astype(BF16)
            for m in range(5)
        ]
        for m in range(3):
            blocks = blended[m].reshape(seq_len, shards, shard_rows)
            blended[m] = jnp.take(blocks, order, axis=1).reshape(seq_len, width)
        last_in = lax.dynamic_slice_in_dim(normed_in, length - 1, 1, 0)
    low_rank = jnp.tanh(matmul(blended[3], forgetting_left_lowrank)).astype(BF16)
    decay = matmul(low_rank, forgetting_right_lowrank)
    gate = matmul(blended[4], gating_projection)

    exchange = Exchange(req)
    rows_here = feedforward_entry_proj.shape[0]
    half = rows_here // 2
    key_halves = [feedforward_entry_proj[:half], feedforward_entry_proj[half:]]
    parts = 2
    wide = local_width // parts
    split_values = feedforward_exit_proj.reshape(rows_here, hid, parts, wide)
    value_halves = [
        [
            split_values[first : first + half, :, part].reshape(half, hid * wide)
            for first in (0, half)
        ]
        for part in range(parts)
    ]
    mine = []
    for pieces in (training_lookup_pieces, training_content_pieces, training_accept_pieces):
        blocks = pieces.astype(BF16).reshape(shard_rows, hid, local_width).transpose(1, 0, 2)
        if mine:
            blocks, _ = lax.optimization_barrier((blocks, mine[-1]))
        mine.append(lax.all_to_all(blocks, "hid", split_axis=0, concat_axis=0, tiled=True))
    trainer_halves = [
        jnp.split(blocks.reshape(hid * shard_rows, local_width), 2, axis=0) for blocks in mine
    ]
    if req == 4:
        near, far = exchange.near, exchange.far
        key_rows = [near(key_halves[0])]
        trained = [[near(block) for block in trainer_halves[0]]]
        trained.append([near(block) for block in trainer_halves[1]])
        far(trained[0][0], 2)
        far(trained[0][1], 1)
        trained.append([near(block) for block in trainer_halves[2]])
        for m in (1, 2):
            far(trained[m][0], 2)
            far(trained[m][1], 1)
        key_rows.append(near(key_halves[1]))
        far(key_rows[0], 2)
        far(key_rows[1], 1)
        value_rows = []
        for part in range(parts):
            value_rows.append([near(block) for block in value_halves[part]])
            far(value_rows[part][0], 2)
            far(value_rows[part][1], 1)
    else:
        key_rows = [exchange.whole(block) for block in key_halves]
        trained = [[exchange.whole(block) for block in blocks] for blocks in trainer_halves]
        value_rows = [[exchange.whole(block) for block in blocks] for blocks in value_halves]

    half_span = hid * shard_rows // 2

    def project(values, halves):
        total = 0.0
        for d in range(req):
            for side in range(2):
                first = (2 * d + side) * half_span
                total = total + matmul(values[:, first : first + half_span], halves[side][d])
        return total

    key, val, rec = (project(blended[m], trained[at]) for at, m in enumerate((1, 2, 0)))
    gated, new_state = recurrence(
        prompt_extents,
        rec,
        key,
        val,
        decay,
        gate,
        forgetting_bias_vector[None],
        instant_emphasis[None],
        group_normalizer_scale[None],
        start,
    )
    head_terms = matmul(gated, mixing_exit_projection).astype(BF16)
    attended = lax.psum(head_terms, "hid").astype(F32)
    middle = (token_rows.astype(F32) + attended).astype(BF16)
    mid_share = lax.dynamic_slice_in_dim(middle, slot * local_width, local_width, 1)
    chan_in = layer_norm(middle.astype(F32), gain_rows[1])
    chan_before = shifted(chan_in, carried[1])
    chan_mixed = [
        (chan_in + (chan_before - chan_in) * mix_rows[5 + m][None, :]).astype(BF16)
        for m in range(2)
    ]
    gate_rows = jax.nn.sigmoid(matmul(chan_mixed[1], feedforward_accept_proj))
    hidden = [
        jnp.square(jnp.maximum(matmul_nt(chan_mixed[0], key_rows[side][d]), 0.0)).astype(BF16)
        for d in range(req)
        for side in range(2)
    ]
    summed = []
    for part in range(parts):
        terms = exit_product(
            hidden, [value_rows[part][side][d] for d in range(req) for side in range(2)]
        )
        summed.append(lax.psum_scatter(terms, "hid", scatter_dimension=1, tiled=True))
    mixed_out = jnp.concatenate(summed, axis=1).astype(F32)
    combined = mid_share.astype(F32) + gate_rows * mixed_out
    layer_out = jnp.where(present[:, None], combined, 0.0).astype(BF16)[None]
    last_chan = lax.dynamic_slice_in_dim(chan_in, length - 1, 1, 0)
    shift_out = jnp.concatenate([last_in, last_chan]).astype(BF16)[None]
    return (layer_out, new_state[None], shift_out)


def solution(mesh):
    placed = (
        P("req", None, None),
        P("req"),
        P("req"),
        P("req"),
        P(),
        P(("req", "hid"), None),
        P(("req", "hid"), None),
        P(("req", "hid"), None),
        P(),
        P(),
        P("hid"),
        P(),
        P(None, "hid"),
        P("hid"),
        P("hid"),
        P(None, "hid"),
        P("hid", None),
        P("req", "hid", None, None, None),
        P("req", None, None),
        P(("req", "hid"), None),
        P(("req", "hid"), None),
        P(None, "hid"),
    )
    return jax.shard_map(
        local,
        mesh=mesh,
        in_specs=placed,
        out_specs=(P("req", None, "hid"), P("req", "hid", None, None), P("req", None, None)),
        check_vma=False,
    )
```

time: 1250 us -> 534 us (0.43)
  waiting for transfers between devices: 763 us -> 259 us
  other arithmetic: 180 us -> 15.2 us
  local copies, waits for them, and re-layouts: 179 us -> 62.9 us
  Pallas kernels: 0 us -> 54.5 us
  starting transfers between devices: 12.4 us -> 52.2 us
  matrix products: 87 us -> 63.7 us
    all_gather x3 -> x0, waiting for transfers between devices: 381 us -> none  [the longest x1 142 us: local(): lax.all_gather(feedforward_exit_proj, 'req', axis=0, tiled=True)]
    all_to_all x2 -> x3, waiting for transfers between devices: 240 us -> 0.01 us  [local(): lax.all_to_all(blocks, 'hid', split_axis=0, concat_axis=0, tiled=True)]
    ppermute x0 -> x36, waiting for transfers between devices: none -> 222 us  [send(): got = lax.ppermute(value, 'req', [(i, i ^ axis) for i in range(4)])]
    reduce_sum x18 -> x0, other arithmetic: 92.2 us -> none  [the longest x8 77.6 us: segment_step(): jnp.sum(acceptance_vectors[:, None] * factor * present_lookup_vectors[Non...]
    psum x1, waiting for transfers between devices: 93.2 us -> 2.85 us  [local(): attended = lax.psum(head_terms, 'hid').astype(F32)]
    pallas_call x0 -> x4, Pallas kernels: none -> 54.5 us  [the longest x1 22.1 us: prepare(): pl.pallas_call(prepare_kernel, grid_spec=pltpu.PrefetchScalarGridSpec(num...]
    ppermute x0 -> x36, starting transfers between devices: none -> 37.1 us  [send(): got = lax.ppermute(value, 'req', [(i, i ^ axis) for i in range(4)])]
    all_to_all x2 -> x0, local copies, waits for them, and re-layouts: 30 us -> none  [local(): lax.all_to_all(collected, 'hid', split_axis=2, concat_axis=1, tiled=True)]
  transfers between devices with their start and end apart: 7 -> 43, of which waited for: 6 -> 26; matrix products, arithmetic and copies ran while one was open for 13% -> 21% of each run, Pallas kernels for 0% -> 5%
where the time goes in v1:
time: 534 us; the launch traced here: 524 us
  waiting for transfers between devices  259 us (49%)
  matrix products  63.7 us (12%)
  local copies, waits for them, and re-layouts  62.9 us (12%)
  Pallas kernels  54.5 us (10%)
  starting transfers between devices  52.2 us (10%)
  between operations  17 us (3%)
  other arithmetic  15.2 us (3%)
    ppermute x36, waiting for transfers between devices, send(): got = lax.ppermute(value, 'req', [(i, i ^ axis) for i in range(4)])  222 us
    dot_general x28, matrix products, matmul(): return jnp.dot(a, b, preferred_element_type=F32)  47.1 us
    ppermute x36, starting transfers between devices, send(): got = lax.ppermute(value, 'req', [(i, i ^ axis) for i in range(4)])  37.1 us
    reduce_scatter x2, waiting for transfers between devices, local(): lax.psum_scatter(terms, 'hid', scatter_dimension=1, tiled=True)  33.6 us
    pallas_call x1, Pallas kernels, prepare(): pl.pallas_call(prepare_kernel, grid_spec=pltpu.PrefetchScalarGridSpec(num...  22.1 us
    unnamed x89, local copies, waits for them, and re-layouts  21.5 us
    slice x1, local copies, waits for them, and re-layouts, local(): split_values[first:first + half, :, part].reshape(half, hid * wide)  18.9 us
    pallas_call x1, Pallas kernels, recurrence(): pl.pallas_call(recurrence_kernel, grid=(width // PAIR,), in_specs=[pl.Blo...  18.2 us
  transfers between devices with their start and end apart: 43, of which 26 were waited for; matrix products, arithmetic and copies ran while one was open for 21% of the time, Pallas kernels for 5%

profile of v1, /device:TPU:0, one launch (start us, length us, event | category | flops | bytes accessed | tf_op | source)
XLA Modules:
  0.0 524.3 jit_solution(7038705607522989835)
XLA Ops:
  7.2 4.4 fusion.90
  11.6 2.9 collective-permute-start
  17.5 4.9 all-to-all-start
  27.8 2.6 copy.70
  30.3 2.6 copy.71
  33.2 22.1 %prepare.1 = (bf16[512,4096]{1,0:T(8,128)(2,1)S(1)}, bf16[512,4096]{1,0:T(8,128)(2,1)S(1)}, bf16[512,4096]{1,0:T(8,128)(2,1)S(1)}, bf16[512,4096]{1,0:T(8,128)(2...) custom-call(s32[32]{0:T(128)S(1)} %pad_add_fusion.order_ref, s32[1]{0:T(128)} %copy.118.length_ref, ...), custom_call_target="tpu_custom_call" | custom-call | flops 41943040 | bytes 25165824 | tf_op jit(solution)/shard_map/prepare/pallas_call | solution.py:241
  55.3 1.9 copy-done.2
  57.2 2.0 copy-done.3
  59.2 2.0 copy-done.5
  61.3 2.1 copy-done.7
  63.4 2.0 copy-done.14
  65.3 3.8 fusion.42.decay_ref
  69.2 6.8 %fusion.97.gate_ref = f32[512,512]{1,0:T(8,128)} fusion(bf16[512,4096]{1,0:T(8,128)(2,1)} %copy-done.14, bf16[4096,512]{1,0:T(8,128)(2,1)} %param.37), kind=kOutput, calls=%fused_computation.134 | convolution fusion | flops 2147483648 | bytes 9437184 | tf_op jit(solution)/shard_map/dot_general | solution.py:28
  78.4 5.0 all-to-all-start.1
  88.2 3.6 collective-permute-done.15
  93.3 10.6 %collective-permute-done.3 = bf16[512,512]{1,0:T(8,128)(2,1)S(1)} collective-permute-done((bf16[512,512]{1,0:T(8,128)(2,1)S(1)}, bf16[512,512]{1,0:T(8,128)(2,1)S(1)}, u32[]{:S(2)}, u32[]{:S(2)}) %collective-permute-start.3) | collective-permute-done | bytes 524320 | tf_op jit(solution)/shard_map/ppermute | solution.py:50
  108.8 5.5 %collective-permute-done.17 = bf16[512,512]{1,0:T(8,128)(2,1)S(1)} collective-permute-done((bf16[512,512]{1,0:T(8,128)(2,1)}, bf16[512,512]{1,0:T(8,128)(2,1)S(1)}, u32[]{:S(2)}, u32[]{:S(2)}) %collective-permute-start.17) | collective-permute-done | bytes 524320 | tf_op jit(solution)/shard_map/ppermute | solution.py:50
  117.6 4.4 all-to-all-start.2
  133.2 6.7 %collective-permute-done.10 = bf16[512,512]{1,0:T(8,128)(2,1)} collective-permute-done((bf16[512,512]{1,0:T(8,128)(2,1)}, bf16[512,512]{1,0:T(8,128)(2,1)}, u32[]{:S(2)}, u32[]{:S(2)}) %collective-permute-start.10) | collective-permute-done | bytes 524320 | tf_op jit(solution)/shard_map/ppermute | solution.py:50
  144.3 6.7 %collective-permute-done.7 = bf16[512,512]{1,0:T(8,128)(2,1)S(1)} collective-permute-done((bf16[512,512]{1,0:T(8,128)(2,1)}, bf16[512,512]{1,0:T(8,128)(2,1)S(1)}, u32[]{:S(2)}, u32[]{:S(2)}) %collective-permute-start.7) | collective-permute-done | bytes 524320 | tf_op jit(solution)/shard_map/ppermute | solution.py:50
  153.8 10.0 %collective-permute-done.19 = bf16[512,512]{1,0:T(8,128)(2,1)S(1)} collective-permute-done((bf16[512,512]{1,0:T(8,128)(2,1)}, bf16[512,512]{1,0:T(8,128)(2,1)S(1)}, u32[]{:S(2)}, u32[]{:S(2)}) %collective-permute-start.19) | collective-permute-done | bytes 524320 | tf_op jit(solution)/shard_map/ppermute | solution.py:50
  177.0 6.8 %collective-permute-done.11 = bf16[512,512]{1,0:T(8,128)(2,1)} collective-permute-done((bf16[512,512]{1,0:T(8,128)(2,1)}, bf16[512,512]{1,0:T(8,128)(2,1)}, u32[]{:S(2)}, u32[]{:S(2)}) %collective-permute-start.11) | collective-permute-done | bytes 524320 | tf_op jit(solution)/shard_map/ppermute | solution.py:50
  186.0 7.3 %collective-permute-done.8 = bf16[512,512]{1,0:T(8,128)(2,1)S(1)} collective-permute-done((bf16[512,512]{1,0:T(8,128)(2,1)}, bf16[512,512]{1,0:T(8,128)(2,1)S(1)}, u32[]{:S(2)}, u32[]{:S(2)}) %collective-permute-start.8) | collective-permute-done | bytes 524320 | tf_op jit(solution)/shard_map/ppermute | solution.py:50
  197.2 8.8 %collective-permute-done.13 = bf16[512,512]{1,0:T(8,128)(2,1)S(1)} collective-permute-done((bf16[512,512]{1,0:T(8,128)(2,1)}, bf16[512,512]{1,0:T(8,128)(2,1)S(1)}, u32[]{:S(2)}, u32[]{:S(2)}) %collective-permute-start.13) | collective-permute-done | bytes 524320 | tf_op jit(solution)/shard_map/ppermute | solution.py:50
  208.4 18.2 %recurrence.1 = (bf16[512,512]{1,0:T(8,128)(2,1)S(1)}, f32[8,64,64]{2,1,0:T(8,128)}) custom-call(s32[1]{0:T(128)} %copy.118.length_ref, f32[512,512]{1,0:T(8,128)S(1)} %fusion.22.rec_ref, f32[512,512]{1,0:T(8,128)S(1)} %fusion.17.key_ref, f32[512,512]{1,0:T(8,128)S(1)} %copy-done.9, f32[512,512]{1,0:T(8,128)S(1)} %fusion.42.decay_ref, ...), custom_call_target="tpu_custom_call" | custom-call | flops 1073741824 | bytes 5767168 | tf_op jit(solution)/shard_map/recurrence/pallas_call | solution.py:169
  226.6 4.4 convolution_convert_fusion
  231.3 7.2 %reshape.98 = bf16[448,8,2,256]{3,2,1,0:T(2,128)(2,1)} reshape(bf16[448,4096]{1,0:T(8,128)(2,1)} %param.42) | data formatting | bytes 7340032 | tf_op jit(solution)/shard_map/reshape | solution.py:370
  241.0 18.9 %slice_reduce_fusion.2 = (bf16[224,8,256]{2,1,0:T(8,128)(2,1)S(1)}, bf16[224,8,256]{2,1,0:T(8,128)(2,1)}, bf16[224,8,256]{2,1,0:T(8,128)(2,1)S(1)}, bf16[224,8,256]{2,1,0:T(8,128)(2,1)}) fusion(bf16[448,8,2,256]{3,2,1,0:T(2,128)(2,1)} %reshape.98), kind=kLoop, calls=%fused_computation.15 | loop fusion | bytes 7340032 | tf_op jit(solution)/shard_map/slice | solution.py:373
  263.4 18.2 %collective-permute-done.22 = bf16[224,4096]{1,0:T(8,128)(2,1)S(1)} collective-permute-done((bf16[224,4096]{1,0:T(8,128)(2,1)}, bf16[224,4096]{1,0:T(8,128)(2,1)S(1)}, u32[]{:S(2)}, u32[]{:S(2)}) %collective-permute-start.22) | collective-permute-done | bytes 1835040 | tf_op jit(solution)/shard_map/ppermute | solution.py:50
  281.6 17.8 %collective-permute-done.24.refs_10_ = bf16[224,2048]{1,0:T(8,128)(2,1)S(1)} collective-permute-done((bf16[224,2048]{1,0:T(8,128)(2,1)S(1)}, bf16[224,2048]{1,0:T(8,128)(2,1)S(1)}, u32[]{:S(2)}, u32[]{:S(2)}) %collective-permute-start.24) | collective-permute-done | bytes 917536 | tf_op jit(solution)/shard_map/ppermute | solution.py:50
  300.1 20.9 %collective-permute-done.21 = bf16[224,4096]{1,0:T(8,128)(2,1)} collective-permute-done((bf16[224,4096]{1,0:T(8,128)(2,1)}, bf16[224,4096]{1,0:T(8,128)(2,1)}, u32[]{:S(2)}, u32[]{:S(2)}) %collective-permute-start.21) | collective-permute-done | bytes 1835040 | tf_op jit(solution)/shard_map/ppermute | solution.py:50
  324.5 2.9 all-reduce.2.cloned.1.call-done
  327.4 5.2 convert_reduce_fusion
  335.7 4.4 add_convert_fusion
  340.2 2.9 fusion.35.refs_2_
  344.4 2.9 fusion.37.refs_4_
  348.6 2.9 fusion.38.refs_5_
  352.8 24.3 %collective-permute-done.27.refs_13_ = bf16[224,2048]{1,0:T(8,128)(2,1)} collective-permute-done((bf16[224,2048]{1,0:T(8,128)(2,1)S(1)}, bf16[224,2048]{1,0:T(8,128)(2,1)}, u32[]{:S(2)}, u32[]{:S(2)}) %collective-permute-start.27) | collective-permute-done | bytes 917536 | tf_op jit(solution)/shard_map/ppermute | solution.py:50
  379.0 2.9 fusion.40.refs_7_
  381.9 15.0 %collective-permute-done.29.refs_15_ = bf16[224,2048]{1,0:T(8,128)(2,1)S(1)} collective-permute-done((bf16[224,2048]{1,0:T(8,128)(2,1)}, bf16[224,2048]{1,0:T(8,128)(2,1)S(1)}, u32[]{:S(2)}, u32[]{:S(2)}) %collective-permute-start.29) | collective-permute-done | bytes 917536 | tf_op jit(solution)/shard_map/ppermute | solution.py:50
  396.9 7.8 %exit_product.2 = bf16[512,2048]{1,0:T(8,128)(2,1)} custom-call(bf16[512,224]{1,0:T(8,128)(2,1)S(1)} %fusion.33.refs_0_, bf16[512,224]{1,0:T(8,128)(2,1)S(1)} %fusion.34.refs_1_, bf16[512,224]{1,0:T(8,128)(2,1)S(1)} %fusion.35.refs_2_, bf16[512,224]{1,0:T(8,128)(2,1)S(1)} %fusion.36.refs_3_, bf16[512,224]{1,0:T(8,128)(2,1)S(1)} %fusion.37.refs_4_, ...), custom_call_target="tpu_custom_call" | custom-call | flops 3758096384 | bytes 9437184 | tf_op jit(solution)/shard_map/exit_product/pallas_call | solution.py:274
  411.0 15.5 %collective-permute-done.30.refs_10_ = bf16[224,2048]{1,0:T(8,128)(2,1)S(1)} collective-permute-done((bf16[224,2048]{1,0:T(8,128)(2,1)S(1)}, bf16[224,2048]{1,0:T(8,128)(2,1)S(1)}, u32[]{:S(2)}, u32[]{:S(2)}) %collective-permute-start.30) | collective-permute-done | bytes 917536 | tf_op jit(solution)/shard_map/ppermute | solution.py:50
  429.0 3.3 collective-permute-done.33.refs_13_
  433.8 18.2 %collective-permute-done.32.refs_12_ = bf16[224,2048]{1,0:T(8,128)(2,1)S(1)} collective-permute-done((bf16[224,2048]{1,0:T(8,128)(2,1)S(1)}, bf16[224,2048]{1,0:T(8,128)(2,1)S(1)}, u32[]{:S(2)}, u32[]{:S(2)}) %collective-permute-start.32) | collective-permute-done | bytes 917536 | tf_op jit(solution)/shard_map/ppermute | solution.py:50
  452.0 14.7 %collective-permute-done.34.refs_14_ = bf16[224,2048]{1,0:T(8,128)(2,1)S(1)} collective-permute-done((bf16[224,2048]{1,0:T(8,128)(2,1)S(1)}, bf16[224,2048]{1,0:T(8,128)(2,1)S(1)}, u32[]{:S(2)}, u32[]{:S(2)}) %collective-permute-start.34) | collective-permute-done | bytes 917536 | tf_op jit(solution)/shard_map/ppermute | solution.py:50
  466.7 6.5 %exit_product.3 = bf16[512,2048]{1,0:T(8,128)(2,1)} custom-call(bf16[512,224]{1,0:T(8,128)(2,1)S(1)} %copy-done.24, bf16[512,224]{1,0:T(8,128)(2,1)S(1)} %copy-done.26, bf16[512,224]{1,0:T(8,128)(2,1)S(1)} %fusion.35.refs_2_, bf16[512,224]{1,0:T(8,128)(2,1)S(1)} %fusion.36.refs_3_, bf16[512,224]{1,0:T(8,128)(2,1)S(1)} %copy-done.16, ...), custom_call_target="tpu_custom_call" | custom-call | flops 3758096384 | bytes 9437184 | tf_op jit(solution)/shard_map/exit_product/pallas_call | solution.py:274
  474.9 33.6 %reduce-scatter.8.cloned.1.call-done = bf16[512,256]{1,0:T(8,128)(2,1)} async-done(((bf16[512,2048]{1,0:T(8,128)(2,1)}), bf16[512,256]{1,0:T(8,128)(2,1)}) %reduce-scatter.8.cloned.1.call-update) | async-done | bytes 262160 | tf_op jit(solution)/shard_map/reduce_scatter | solution.py:455
  508.5 8.8 %fusion.43 = bf16[1,512,512]{2,1,0:T(8,128)(2,1)} fusion(bf16[512,256]{1,0:T(8,128)(2,1)} %reduce-scatter.8.cloned.1.call-done, bf16[512,256]{1,0:T(8,128)(2,1)} %reduce-scatter.6.cloned.1.call-done, bf16[4096,512]{1,0:T(8,128)(2,1)} %param.43, f32[4096]{0:T(1024)S(1)} %bitcast.131, f32[511,4096]{1,0:T(8,128)} %bitcast.115, ...), kind=kOutput, calls=%fused_computation.71 | convolution fusion | flops 2169503744 | bytes 18403844 | tf_op jit(solution)/shard_map/dot_general | solution.py:28
  (203 shorter events, 94.5 us)
Async XLA Ops:
  11.6 115.5 %collective-permute-start = (bf16[224,4096]{1,0:T(8,128)(2,1)}, bf16[224,4096]{1,0:T(8,128)(2,1)}, u32[]{:S(2)}, u32[]{:S(2)}) collective-permute-start(bf16[224,4096]{1,0:T(8,128)(2,1)} %get-tuple-element.90), channel_id=1, source_target_pairs={{0,8},{8,0},{16,24},{24,16},{1,9},{9,1},{17,25},{25,17},{2,10},{10... | collective-permute-start | bytes 5505032 | tf_op jit(solution)/shard_map/ppermute | solution.py:50
  14.6 113.1 %collective-permute-start.6 = (bf16[224,4096]{1,0:T(8,128)(2,1)}, bf16[224,4096]{1,0:T(8,128)(2,1)}, u32[]{:S(2)}, u32[]{:S(2)}) collective-permute-start(bf16[224,4096]{1,0:T(8,128)(2,1)} %get-tuple-element.90), channel_id=1, source_target_pairs={{0,16},{8,24},{16,0},{24,8},{1,17},{9,25},{17,1},{25,9},{2,18},{10... | collective-permute-start | bytes 5505032 | tf_op jit(solution)/shard_map/ppermute | solution.py:50
  17.5 59.5 %all-to-all-start = ((bf16[8,128,512]{1,2,0:T(8,128)(2,1)}), bf16[8,128,512]{1,2,0:T(8,128)(2,1)S(1)}, u32[]{:S(2)}, u32[]{:S(2)}) async-start(bf16[8,128,512]{1,2,0:T(8,128)(2,1)} %bitcast.9), calls=%async_computation | async-start | bytes 2097152 | tf_op jit(solution)/shard_map/all_to_all | solution.py:383
  22.4 53.6 %reduce-scatter.4.cloned.1.call-start = ((), (), s32[]{:S(2)}) async-start(), calls=%async_computation.6 | async-start | bytes 589824 | tf_op jit(solution)/shard_map/reduce_scatter | solution.py:331
  77.3 14.5 %collective-permute-start.15 = (bf16[512,512]{1,0:T(8,128)(2,1)S(1)}, bf16[512,512]{1,0:T(8,128)(2,1)}, u32[]{:S(2)}, u32[]{:S(2)}) collective-permute-start(bf16[512,512]{1,0:T(8,128)(2,1)S(1)} %bitcast.124), channel_id=1, source_target_pairs={{0,16},{8,24},{16,0},{24,8},{1,17},{9,25},{17,1},{25,9},{2,18},{10... | collective-permute-start | bytes 1572872 | tf_op jit(solution)/shard_map/ppermute | solution.py:50
  77.9 14.9 %collective-permute-start.14 = (bf16[512,512]{1,0:T(8,128)(2,1)S(1)}, bf16[512,512]{1,0:T(8,128)(2,1)}, u32[]{:S(2)}, u32[]{:S(2)}) collective-permute-start(bf16[512,512]{1,0:T(8,128)(2,1)S(1)} %bitcast.125), channel_id=1, source_target_pairs={{0,8},{8,0},{16,24},{24,16},{1,9},{9,1},{17,25},{25,17},{2,10},{10... | collective-permute-start | bytes 1572872 | tf_op jit(solution)/shard_map/ppermute | solution.py:50
  78.4 39.2 %all-to-all-start.1 = ((bf16[8,128,512]{1,2,0:T(8,128)(2,1)}), bf16[8,128,512]{1,2,0:T(8,128)(2,1)}, u32[]{:S(2)}, u32[]{:S(2)}) async-start(bf16[8,128,512]{1,2,0:T(8,128)(2,1)} %bitcast.7), calls=%async_computation.1 | async-start | bytes 2097152 | tf_op jit(solution)/shard_map/all_to_all | solution.py:383
  83.7 20.2 %collective-permute-start.3 = (bf16[512,512]{1,0:T(8,128)(2,1)S(1)}, bf16[512,512]{1,0:T(8,128)(2,1)S(1)}, u32[]{:S(2)}, u32[]{:S(2)}) collective-permute-start(bf16[512,512]{1,0:T(8,128)(2,1)S(1)} %bitcast.121), channel_id=1, source_target_pairs={{0,8},{8,0},{16,24},{24,16},{1,9},{9,1},{17,25},{25,17},{2,10},{10... | collective-permute-start | bytes 1572872 | tf_op jit(solution)/shard_map/ppermute | solution.py:50
  91.7 16.6 %collective-permute-start.9 = (bf16[512,512]{1,0:T(8,128)(2,1)S(1)}, bf16[512,512]{1,0:T(8,128)(2,1)S(1)}, u32[]{:S(2)}, u32[]{:S(2)}) collective-permute-start(bf16[512,512]{1,0:T(8,128)(2,1)S(1)} %bitcast.123), channel_id=1, source_target_pairs={{0,16},{8,24},{16,0},{24,8},{1,17},{9,25},{17,1},{25,9},{2,18},{10... | collective-permute-start | bytes 1572872 | tf_op jit(solution)/shard_map/ppermute | solution.py:50
  92.7 21.6 %collective-permute-start.17 = (bf16[512,512]{1,0:T(8,128)(2,1)}, bf16[512,512]{1,0:T(8,128)(2,1)S(1)}, u32[]{:S(2)}, u32[]{:S(2)}) collective-permute-start(bf16[512,512]{1,0:T(8,128)(2,1)} %collective-permute-done.15), channel_id=1, source_target_pairs={{0,8},{8,0},{16,24},{24,16},{1,9},{9,1},{17,25},{25,17},{2,10},{10... | collective-permute-start | bytes 1572872 | tf_op jit(solution)/shard_map/ppermute | solution.py:50
  103.9 12.6 %collective-permute-start.16 = (bf16[512,512]{1,0:T(8,128)(2,1)S(1)}, bf16[512,512]{1,0:T(8,128)(2,1)S(1)}, u32[]{:S(2)}, u32[]{:S(2)}) collective-permute-start(bf16[512,512]{1,0:T(8,128)(2,1)S(1)} %collective-permute-done.3), channel_id=1, source_target_pairs={{0,16},{8,24},{16,0},{24,8},{1,17},{9,25},{17,1},{25,9},{2,18},{10... | collective-permute-start | bytes 1572872 | tf_op jit(solution)/shard_map/ppermute | solution.py:50
  117.6 48.8 %all-to-all-start.2 = ((bf16[8,128,512]{1,2,0:T(8,128)(2,1)}), bf16[8,128,512]{1,2,0:T(8,128)(2,1)}, u32[]{:S(2)}, u32[]{:S(2)}) async-start(bf16[8,128,512]{1,2,0:T(8,128)(2,1)} %bitcast.5), calls=%async_computation.2 | async-start | bytes 2097152 | tf_op jit(solution)/shard_map/all_to_all | solution.py:383
  122.0 205.3 %all-reduce.2.cloned.1.call-start = ((), (), s32[]{:S(2)}) async-start(), calls=%async_computation.7 | async-start | bytes 8388608 | tf_op jit(solution)/shard_map/psum | solution.py:435
  124.8 15.0 %collective-permute-start.10 = (bf16[512,512]{1,0:T(8,128)(2,1)}, bf16[512,512]{1,0:T(8,128)(2,1)}, u32[]{:S(2)}, u32[]{:S(2)}) collective-permute-start(bf16[512,512]{1,0:T(8,128)(2,1)} %bitcast.13), channel_id=1, source_target_pairs={{0,16},{8,24},{16,0},{24,8},{1,17},{9,25},{17,1},{25,9},{2,18},{10... | collective-permute-start | bytes 1572872 | tf_op jit(solution)/shard_map/ppermute | solution.py:50
  127.2 15.0 %collective-permute-start.1 = (bf16[512,512]{1,0:T(8,128)(2,1)}, bf16[512,512]{1,0:T(8,128)(2,1)S(1)}, u32[]{:S(2)}, u32[]{:S(2)}) collective-permute-start(bf16[512,512]{1,0:T(8,128)(2,1)} %bitcast.12), channel_id=1, source_target_pairs={{0,8},{8,0},{16,24},{24,16},{1,9},{9,1},{17,25},{25,17},{2,10},{10... | collective-permute-start | bytes 1572872 | tf_op jit(solution)/shard_map/ppermute | solution.py:50
  127.7 23.3 %collective-permute-start.7 = (bf16[512,512]{1,0:T(8,128)(2,1)}, bf16[512,512]{1,0:T(8,128)(2,1)S(1)}, u32[]{:S(2)}, u32[]{:S(2)}) collective-permute-start(bf16[512,512]{1,0:T(8,128)(2,1)} %bitcast.12), channel_id=1, source_target_pairs={{0,16},{8,24},{16,0},{24,8},{1,17},{9,25},{17,1},{25,9},{2,18},{10... | collective-permute-start | bytes 1572872 | tf_op jit(solution)/shard_map/ppermute | solution.py:50
  128.4 25.0 %collective-permute-start.4 = (bf16[512,512]{1,0:T(8,128)(2,1)}, bf16[512,512]{1,0:T(8,128)(2,1)S(1)}, u32[]{:S(2)}, u32[]{:S(2)}) collective-permute-start(bf16[512,512]{1,0:T(8,128)(2,1)} %bitcast.13), channel_id=1, source_target_pairs={{0,8},{8,0},{16,24},{24,16},{1,9},{9,1},{17,25},{25,17},{2,10},{10... | collective-permute-start | bytes 1572872 | tf_op jit(solution)/shard_map/ppermute | solution.py:50
  139.9 24.0 %collective-permute-start.19 = (bf16[512,512]{1,0:T(8,128)(2,1)}, bf16[512,512]{1,0:T(8,128)(2,1)S(1)}, u32[]{:S(2)}, u32[]{:S(2)}) collective-permute-start(bf16[512,512]{1,0:T(8,128)(2,1)} %collective-permute-done.10), channel_id=1, source_target_pairs={{0,8},{8,0},{16,24},{24,16},{1,9},{9,1},{17,25},{25,17},{2,10},{10... | collective-permute-start | bytes 1572872 | tf_op jit(solution)/shard_map/ppermute | solution.py:50
  142.1 22.2 %collective-permute-start.18 = (bf16[512,512]{1,0:T(8,128)(2,1)S(1)}, bf16[512,512]{1,0:T(8,128)(2,1)S(1)}, u32[]{:S(2)}, u32[]{:S(2)}) collective-permute-start(bf16[512,512]{1,0:T(8,128)(2,1)S(1)} %collective-permute-done.1), channel_id=1, source_target_pairs={{0,16},{8,24},{16,0},{24,8},{1,17},{9,25},{17,1},{25,9},{2,18},{10... | collective-permute-start | bytes 1572872 | tf_op jit(solution)/shard_map/ppermute | solution.py:50
  168.7 15.2 %collective-permute-start.11 = (bf16[512,512]{1,0:T(8,128)(2,1)}, bf16[512,512]{1,0:T(8,128)(2,1)}, u32[]{:S(2)}, u32[]{:S(2)}) collective-permute-start(bf16[512,512]{1,0:T(8,128)(2,1)} %bitcast.11), channel_id=1, source_target_pairs={{0,16},{8,24},{16,0},{24,8},{1,17},{9,25},{17,1},{25,9},{2,18},{10... | collective-permute-start | bytes 1572872 | tf_op jit(solution)/shard_map/ppermute | solution.py:50
  170.4 15.1 %collective-permute-start.2 = (bf16[512,512]{1,0:T(8,128)(2,1)}, bf16[512,512]{1,0:T(8,128)(2,1)S(1)}, u32[]{:S(2)}, u32[]{:S(2)}) collective-permute-start(bf16[512,512]{1,0:T(8,128)(2,1)} %bitcast.10), channel_id=1, source_target_pairs={{0,8},{8,0},{16,24},{24,16},{1,9},{9,1},{17,25},{25,17},{2,10},{10... | collective-permute-start | bytes 1572872 | tf_op jit(solution)/shard_map/ppermute | solution.py:50
  170.9 22.4 %collective-permute-start.8 = (bf16[512,512]{1,0:T(8,128)(2,1)}, bf16[512,512]{1,0:T(8,128)(2,1)S(1)}, u32[]{:S(2)}, u32[]{:S(2)}) collective-permute-start(bf16[512,512]{1,0:T(8,128)(2,1)} %bitcast.10), channel_id=1, source_target_pairs={{0,16},{8,24},{16,0},{24,8},{1,17},{9,25},{17,1},{25,9},{2,18},{10... | collective-permute-start | bytes 1572872 | tf_op jit(solution)/shard_map/ppermute | solution.py:50
  172.2 24.5 %collective-permute-start.5 = (bf16[512,512]{1,0:T(8,128)(2,1)}, bf16[512,512]{1,0:T(8,128)(2,1)S(1)}, u32[]{:S(2)}, u32[]{:S(2)}) collective-permute-start(bf16[512,512]{1,0:T(8,128)(2,1)} %bitcast.11), channel_id=1, source_target_pairs={{0,8},{8,0},{16,24},{24,16},{1,9},{9,1},{17,25},{25,17},{2,10},{10... | collective-permute-start | bytes 1572872 | tf_op jit(solution)/shard_map/ppermute | solution.py:50
  185.5 20.5 %collective-permute-start.13 = (bf16[512,512]{1,0:T(8,128)(2,1)}, bf16[512,512]{1,0:T(8,128)(2,1)S(1)}, u32[]{:S(2)}, u32[]{:S(2)}) collective-permute-start(bf16[512,512]{1,0:T(8,128)(2,1)} %collective-permute-done.11), channel_id=1, source_target_pairs={{0,8},{8,0},{16,24},{24,16},{1,9},{9,1},{17,25},{25,17},{2,10},{10... | collective-permute-start | bytes 1572872 | tf_op jit(solution)/shard_map/ppermute | solution.py:50
  193.3 13.1 %collective-permute-start.12 = (bf16[512,512]{1,0:T(8,128)(2,1)S(1)}, bf16[512,512]{1,0:T(8,128)(2,1)S(1)}, u32[]{:S(2)}, u32[]{:S(2)}) collective-permute-start(bf16[512,512]{1,0:T(8,128)(2,1)S(1)} %collective-permute-done.2), channel_id=1, source_target_pairs={{0,16},{8,24},{16,0},{24,8},{1,17},{9,25},{17,1},{25,9},{2,18},{10... | collective-permute-start | bytes 1572872 | tf_op jit(solution)/shard_map/ppermute | solution.py:50
  231.1 243.8 %reduce-scatter.6.cloned.1.call-start = ((), (), s32[]{:S(2)}) async-start(), calls=%async_computation.8 | async-start | bytes 2359296 | tf_op jit(solution)/shard_map/reduce_scatter | solution.py:455
  238.5 43.2 %collective-permute-start.22 = (bf16[224,4096]{1,0:T(8,128)(2,1)}, bf16[224,4096]{1,0:T(8,128)(2,1)S(1)}, u32[]{:S(2)}, u32[]{:S(2)}) collective-permute-start(bf16[224,4096]{1,0:T(8,128)(2,1)} %collective-permute-done), channel_id=1, source_target_pairs={{0,16},{8,24},{16,0},{24,8},{1,17},{9,25},{17,1},{25,9},{2,18},{10... | collective-permute-start | bytes 5505032 | tf_op jit(solution)/shard_map/ppermute | solution.py:50
  239.8 81.7 %collective-permute-start.20 = (bf16[224,4096]{1,0:T(8,128)(2,1)}, bf16[224,4096]{1,0:T(8,128)(2,1)S(1)}, u32[]{:S(2)}, u32[]{:S(2)}) collective-permute-start(bf16[224,4096]{1,0:T(8,128)(2,1)} %get-tuple-element.66), channel_id=1, source_target_pairs={{0,8},{8,0},{16,24},{24,16},{1,9},{9,1},{17,25},{25,17},{2,10},{10... | collective-permute-start | bytes 5505032 | tf_op jit(solution)/shard_map/ppermute | solution.py:50
  240.3 80.8 %collective-permute-start.21 = (bf16[224,4096]{1,0:T(8,128)(2,1)}, bf16[224,4096]{1,0:T(8,128)(2,1)}, u32[]{:S(2)}, u32[]{:S(2)}) collective-permute-start(bf16[224,4096]{1,0:T(8,128)(2,1)} %get-tuple-element.66), channel_id=1, source_target_pairs={{0,16},{8,24},{16,0},{24,8},{1,17},{9,25},{17,1},{25,9},{2,18},{10... | collective-permute-start | bytes 5505032 | tf_op jit(solution)/shard_map/ppermute | solution.py:50
  260.1 39.3 %collective-permute-start.24 = (bf16[224,2048]{1,0:T(8,128)(2,1)S(1)}, bf16[224,2048]{1,0:T(8,128)(2,1)S(1)}, u32[]{:S(2)}, u32[]{:S(2)}) collective-permute-start(bf16[224,2048]{1,0:T(8,128)(2,1)S(1)} %bitcast.99), channel_id=1, source_target_pairs={{0,8},{8,0},{16,24},{24,16},{1,9},{9,1},{17,25},{25,17},{2,10},{10... | collective-permute-start | bytes 2752520 | tf_op jit(solution)/shard_map/ppermute | solution.py:50
  262.0 119.8 %collective-permute-start.26 = (bf16[224,2048]{1,0:T(8,128)(2,1)S(1)}, bf16[224,2048]{1,0:T(8,128)(2,1)}, u32[]{:S(2)}, u32[]{:S(2)}) collective-permute-start(bf16[224,2048]{1,0:T(8,128)(2,1)S(1)} %bitcast.100), channel_id=1, source_target_pairs={{0,16},{8,24},{16,0},{24,8},{1,17},{9,25},{17,1},{25,9},{2,18},{10... | collective-permute-start | bytes 2752520 | tf_op jit(solution)/shard_map/ppermute | solution.py:50
  299.4 82.4 %collective-permute-start.28 = (bf16[224,2048]{1,0:T(8,128)(2,1)S(1)}, bf16[224,2048]{1,0:T(8,128)(2,1)}, u32[]{:S(2)}, u32[]{:S(2)}) collective-permute-start(bf16[224,2048]{1,0:T(8,128)(2,1)S(1)} %collective-permute-done.24.refs_10_), channel_id=1, source_target_pairs={{0,16},{8,24},{16,0},{24,8},{1,17},{9,25},{17,1},{25,9},{2,18},{10... | collective-permute-start | bytes 2752520 | tf_op jit(solution)/shard_map/ppermute | solution.py:50
  321.1 56.1 %collective-permute-start.23 = (bf16[224,4096]{1,0:T(8,128)(2,1)}, bf16[224,4096]{1,0:T(8,128)(2,1)}, u32[]{:S(2)}, u32[]{:S(2)}) collective-permute-start(bf16[224,4096]{1,0:T(8,128)(2,1)} %collective-permute-done.21), channel_id=1, source_target_pairs={{0,8},{8,0},{16,24},{24,16},{1,9},{9,1},{17,25},{25,17},{2,10},{10... | collective-permute-start | bytes 5505032 | tf_op jit(solution)/shard_map/ppermute | solution.py:50
  321.6 60.3 %collective-permute-start.25 = (bf16[224,2048]{1,0:T(8,128)(2,1)S(1)}, bf16[224,2048]{1,0:T(8,128)(2,1)}, u32[]{:S(2)}, u32[]{:S(2)}) collective-permute-start(bf16[224,2048]{1,0:T(8,128)(2,1)S(1)} %bitcast.102), channel_id=1, source_target_pairs={{0,8},{8,0},{16,24},{24,16},{1,9},{9,1},{17,25},{25,17},{2,10},{10... | collective-permute-start | bytes 2752520 | tf_op jit(solution)/shard_map/ppermute | solution.py:50
  323.2 54.0 %collective-permute-start.27 = (bf16[224,2048]{1,0:T(8,128)(2,1)S(1)}, bf16[224,2048]{1,0:T(8,128)(2,1)}, u32[]{:S(2)}, u32[]{:S(2)}) collective-permute-start(bf16[224,2048]{1,0:T(8,128)(2,1)S(1)} %bitcast.103), channel_id=1, source_target_pairs={{0,16},{8,24},{16,0},{24,8},{1,17},{9,25},{17,1},{25,9},{2,18},{10... | collective-permute-start | bytes 2752520 | tf_op jit(solution)/shard_map/ppermute | solution.py:50
  377.1 19.7 %collective-permute-start.29 = (bf16[224,2048]{1,0:T(8,128)(2,1)}, bf16[224,2048]{1,0:T(8,128)(2,1)S(1)}, u32[]{:S(2)}, u32[]{:S(2)}) collective-permute-start(bf16[224,2048]{1,0:T(8,128)(2,1)} %collective-permute-done.27.refs_13_), channel_id=1, source_target_pairs={{0,8},{8,0},{16,24},{24,16},{1,9},{9,1},{17,25},{25,17},{2,10},{10... | collective-permute-start | bytes 2752520 | tf_op jit(solution)/shard_map/ppermute | solution.py:50
  405.3 61.3 %copy-start.18 = (bf16[512,224]{1,0:T(8,128)(2,1)S(1)}, bf16[512,224]{1,0:T(8,128)(2,1)}, u32[]{:S(2)}) copy-start(bf16[512,224]{1,0:T(8,128)(2,1)} %copy-done.17) | copy-start | bytes 688132
  405.3 61.3 %copy-start.20 = (bf16[512,224]{1,0:T(8,128)(2,1)S(1)}, bf16[512,224]{1,0:T(8,128)(2,1)}, u32[]{:S(2)}) copy-start(bf16[512,224]{1,0:T(8,128)(2,1)} %copy-done.19) | copy-start | bytes 688132
  405.3 61.3 %copy-start.24 = (bf16[512,224]{1,0:T(8,128)(2,1)S(1)}, bf16[512,224]{1,0:T(8,128)(2,1)}, u32[]{:S(2)}) copy-start(bf16[512,224]{1,0:T(8,128)(2,1)} %copy-done.23) | copy-start | bytes 688132
  405.3 61.3 %copy-start.26 = (bf16[512,224]{1,0:T(8,128)(2,1)S(1)}, bf16[512,224]{1,0:T(8,128)(2,1)}, u32[]{:S(2)}) copy-start(bf16[512,224]{1,0:T(8,128)(2,1)} %copy-done.25) | copy-start | bytes 688132
  405.3 61.3 %copy-start.22 = (bf16[512,224]{1,0:T(8,128)(2,1)S(1)}, bf16[512,224]{1,0:T(8,128)(2,1)}, u32[]{:S(2)}) copy-start(bf16[512,224]{1,0:T(8,128)(2,1)} %copy-done.21) | copy-start | bytes 688132
  405.4 103.1 %reduce-scatter.8.cloned.1.call-start = ((), (), s32[]{:S(2)}) async-start(), calls=%async_computation.9 | async-start | bytes 2359296 | tf_op jit(solution)/shard_map/reduce_scatter | solution.py:455
  406.9 19.6 %collective-permute-start.30 = (bf16[224,2048]{1,0:T(8,128)(2,1)S(1)}, bf16[224,2048]{1,0:T(8,128)(2,1)S(1)}, u32[]{:S(2)}, u32[]{:S(2)}) collective-permute-start(bf16[224,2048]{1,0:T(8,128)(2,1)S(1)} %bitcast.105), channel_id=1, source_target_pairs={{0,8},{8,0},{16,24},{24,16},{1,9},{9,1},{17,25},{25,17},{2,10},{10... | collective-permute-start | bytes 2752520 | tf_op jit(solution)/shard_map/ppermute | solution.py:50
  409.0 23.4 %collective-permute-start.33 = (bf16[224,2048]{1,0:T(8,128)(2,1)S(1)}, bf16[224,2048]{1,0:T(8,128)(2,1)S(1)}, u32[]{:S(2)}, u32[]{:S(2)}) collective-permute-start(bf16[224,2048]{1,0:T(8,128)(2,1)S(1)} %bitcast.108), channel_id=1, source_target_pairs={{0,16},{8,24},{16,0},{24,8},{1,17},{9,25},{17,1},{25,9},{2,18},{10... | collective-permute-start | bytes 2752520 | tf_op jit(solution)/shard_map/ppermute | solution.py:50
  410.3 41.6 %collective-permute-start.32 = (bf16[224,2048]{1,0:T(8,128)(2,1)S(1)}, bf16[224,2048]{1,0:T(8,128)(2,1)S(1)}, u32[]{:S(2)}, u32[]{:S(2)}) collective-permute-start(bf16[224,2048]{1,0:T(8,128)(2,1)S(1)} %bitcast.106), channel_id=1, source_target_pairs={{0,16},{8,24},{16,0},{24,8},{1,17},{9,25},{17,1},{25,9},{2,18},{10... | collective-permute-start | bytes 2752520 | tf_op jit(solution)/shard_map/ppermute | solution.py:50
  426.6 40.0 %collective-permute-start.34 = (bf16[224,2048]{1,0:T(8,128)(2,1)S(1)}, bf16[224,2048]{1,0:T(8,128)(2,1)S(1)}, u32[]{:S(2)}, u32[]{:S(2)}) collective-permute-start(bf16[224,2048]{1,0:T(8,128)(2,1)S(1)} %collective-permute-done.30.refs_10_), channel_id=1, source_target_pairs={{0,16},{8,24},{16,0},{24,8},{1,17},{9,25},{17,1},{25,9},{2,18},{10... | collective-permute-start | bytes 2752520 | tf_op jit(solution)/shard_map/ppermute | solution.py:50
  428.3 38.4 %collective-permute-start.31 = (bf16[224,2048]{1,0:T(8,128)(2,1)S(1)}, bf16[224,2048]{1,0:T(8,128)(2,1)S(1)}, u32[]{:S(2)}, u32[]{:S(2)}) collective-permute-start(bf16[224,2048]{1,0:T(8,128)(2,1)S(1)} %bitcast.109), channel_id=1, source_target_pairs={{0,8},{8,0},{16,24},{24,16},{1,9},{9,1},{17,25},{25,17},{2,10},{10... | collective-permute-start | bytes 2752520 | tf_op jit(solution)/shard_map/ppermute | solution.py:50
  432.3 34.3 %collective-permute-start.35 = (bf16[224,2048]{1,0:T(8,128)(2,1)S(1)}, bf16[224,2048]{1,0:T(8,128)(2,1)S(1)}, u32[]{:S(2)}, u32[]{:S(2)}) collective-permute-start(bf16[224,2048]{1,0:T(8,128)(2,1)S(1)} %collective-permute-done.33.refs_13_), channel_id=1, source_target_pairs={{0,8},{8,0},{16,24},{24,16},{1,9},{9,1},{17,25},{25,17},{2,10},{10... | collective-permute-start | bytes 2752520 | tf_op jit(solution)/shard_map/ppermute | solution.py:50
  (36 other events, 586.7 us)
Sparse Core Ops, SparseCore 0:
  27.2 31.8 reduce-scatter.3
  231.2 96.1 all-reduce.1
  405.5 34.4 reduce-scatter.5
  473.4 35.0 reduce-scatter.7

commit v2 on v1

v2 whole, which is shorter than its diff:
```python
from functools import partial

import jax
import jax.numpy as jnp
from jax import lax
from jax.experimental import pallas as pl
from jax.experimental.pallas import tpu as pltpu
from jax.sharding import PartitionSpec as P

GROUP_DIMENSION = 64
PAIR = 2 * GROUP_DIMENSION
CHUNK = 64
BF16 = jnp.bfloat16
F32 = jnp.float32
MICROSECOND = 3690000
VMEM_BYTES = 60 << 20


def layer_norm(values, gain):
    center = values - jnp.mean(values, axis=-1, keepdims=True)
    spread = jnp.mean(center * center, axis=-1, keepdims=True)
    return center / jnp.sqrt(spread + 1e-05) * gain


def shifted(values, first_row):
    return jnp.concatenate([first_row[None, :], values[:-1]], axis=0)


def matmul(a, b):
    return jnp.dot(a, b, preferred_element_type=F32)


def matmul_nt(a, b):
    return lax.dot_general(a, b, (((1,), (1,)), ((), ())), preferred_element_type=F32)


def matmul_tn(a, b):
    return lax.dot_general(a, b, (((0,), (0,)), ((), ())), preferred_element_type=F32)


def across(value, axis):
    return lax.ppermute(value, "req", [(i, i ^ axis) for i in range(4)])


def whole(value, req):
    blocks = lax.all_gather(value, "req", axis=0, tiled=False)
    me = lax.axis_index("req")
    return [lax.dynamic_index_in_dim(blocks, me ^ d, 0, keepdims=False) for d in range(req)]


def by_head(values, first_lanes):
    zeros = jnp.zeros_like(values)
    return jnp.concatenate(
        [jnp.where(first_lanes, values, zeros), jnp.where(first_lanes, zeros, values)], axis=0
    )


def split_matmul(values, weights):
    high = values.astype(BF16)
    low = (values - high.astype(F32)).astype(BF16)
    return matmul(high, weights) + matmul(low, weights)


def recurrence_kernel(
    length_ref,
    rec_ref,
    key_ref,
    val_ref,
    decay_ref,
    gate_ref,
    bias_ref,
    bonus_ref,
    gain_ref,
    start_ref,
    gated_ref,
    state_ref,
    held,
):
    length = length_ref[0]
    tokens = rec_ref.shape[0]
    size = min(CHUNK, tokens)
    lanes = lax.broadcasted_iota(jnp.int32, (size, PAIR), 1)
    first_lanes = lanes < GROUP_DIMENSION
    row_of = lax.broadcasted_iota(jnp.int32, (size, PAIR), 0)
    t_of = lax.broadcasted_iota(jnp.int32, (size, 2 * size), 0)
    s_of = lax.broadcasted_iota(jnp.int32, (size, 2 * size), 1) & (size - 1)
    side_a = lax.broadcasted_iota(jnp.int32, (PAIR, PAIR), 0) < GROUP_DIMENSION
    side_b = lax.broadcasted_iota(jnp.int32, (PAIR, PAIR), 1) < GROUP_DIMENSION
    own_head = side_a == side_b
    average = jnp.where(own_head, 1.0 / GROUP_DIMENSION, 0.0).astype(BF16)
    pairs_here = rec_ref.shape[1] // PAIR
    for pair in range(pairs_here):
        start = start_ref[2 * pair : 2 * pair + 2].reshape(PAIR, GROUP_DIMENSION)
        start = jnp.where(own_head, jnp.concatenate([start, start], axis=1), 0.0)
        held[pair] = start.T
    for index, pair in [(i, p) for i in range(tokens // size) for p in range(pairs_here)]:
        rows = (pl.ds(index * size, size), pl.ds(pair * PAIR, PAIR))
        bias, bonus, gain = (ref[:, rows[1]] for ref in (bias_ref, bonus_ref, gain_ref))
        present = row_of + index * size < length
        rec = rec_ref[rows]
        key = jnp.where(present, key_ref[rows], 0.0)
        val = val_ref[rows].astype(BF16)
        total = jnp.where(present, -jnp.exp(bias + decay_ref[rows]), 0.0)
        scores = jnp.where(
            t_of == s_of,
            matmul_nt((rec * bonus).astype(BF16), by_head(key.astype(BF16), first_lanes)),
            0.0,
        )
        before = jnp.zeros_like(total)
        after = jnp.zeros_like(total)
        span = 1
        while span < size:
            later = (row_of & span) != 0
            scaled = (jnp.where(later, rec, key) * jnp.exp(jnp.where(later, before, after))).astype(
                BF16
            )
            pairs = matmul_nt(scaled, by_head(scaled, first_lanes))
            chosen = (
                ((t_of & span) != 0)
                & ((s_of & span) == 0)
                & ((t_of & (-2 * span)) == (s_of & (-2 * span)))
            )
            scores = jnp.where(chosen, pairs, scores)
            partner = jnp.where(
                later, pltpu.roll(total, span, 0), pltpu.roll(total, size - span, 0)
            )
            before = before + jnp.where(later, partner, 0.0)
            after = after + jnp.where(later, 0.0, partner)
            total = total + partner
            span *= 2
        state = held[pair]
        out = matmul(scores.astype(BF16), by_head(val, first_lanes))
        out = out + matmul_nt((rec * jnp.exp(before)).astype(BF16), state.astype(BF16))
        update = matmul_tn(val, (key * jnp.exp(after)).astype(BF16))
        held[pair] = state * jnp.exp(total[:1, :]) + jnp.where(own_head, update, 0.0)
        center = out - split_matmul(out, average)
        spread = split_matmul(center * center, average)
        grouped = center * lax.rsqrt(spread + 0.00064) * gain
        gate = gate_ref[rows]
        gated_ref[rows] = (grouped * (gate / (1.0 + jnp.exp(-gate)))).astype(BF16)
    for pair in range(pairs_here):
        final = held[pair].T
        final = final[:, :GROUP_DIMENSION] + final[:, GROUP_DIMENSION:]
        state_ref[2 * pair : 2 * pair + 2] = final.reshape(2, GROUP_DIMENSION, GROUP_DIMENSION)


def recurrence(length, projected, decay, gate, bias, bonus, gain, start):
    tokens, width = decay.shape
    together = min(2, width // PAIR)
    lanes = together * PAIR
    wide = pl.BlockSpec((tokens, lanes), lambda p: (0, p))
    stacked = [
        pl.BlockSpec((None, tokens, lanes), lambda p, m=m: (m, 0, p)) for m in range(3)
    ]
    row = pl.BlockSpec((1, lanes), lambda p: (0, p))
    states = pl.BlockSpec((2 * together, GROUP_DIMENSION, GROUP_DIMENSION), lambda p: (p, 0, 0))
    return pl.pallas_call(
        recurrence_kernel,
        grid=(width // lanes,),
        in_specs=[pl.BlockSpec(memory_space=pltpu.SMEM)]
        + stacked
        + [wide] * 2
        + [row] * 3
        + [states],
        out_specs=[wide, states],
        out_shape=[
            jax.ShapeDtypeStruct((tokens, width), BF16),
            jax.ShapeDtypeStruct(start.shape, F32),
        ],
        scratch_shapes=[pltpu.VMEM((together, PAIR, PAIR), F32)],
        compiler_params=pltpu.CompilerParams(vmem_limit_bytes=VMEM_BYTES),
        cost_estimate=pl.CostEstimate(
            flops=1 << 20, bytes_accessed=18 * MICROSECOND, transcendentals=0
        ),
        name="recurrence",
    )(length, projected, projected, projected, decay, gate, bias, bonus, gain, start)


def prepare_kernel(
    order_ref,
    length_ref,
    tokens_ref,
    gain_ref,
    first_ref,
    mix_ref,
    stack_ref,
    out3_ref,
    out4_ref,
    last_ref,
    mean_ref,
    root_ref,
):
    step = pl.program_id(0)
    block = out3_ref.shape[1]
    seq_len, width = tokens_ref.shape

    @pl.when(step == 0)
    def _():
        count = min(64, seq_len)
        for index in range(seq_len // count):
            rows = pl.ds(index * count, count)
            values = tokens_ref[rows, :].astype(F32)
            mean = jnp.mean(values, axis=1, keepdims=True)
            center = values - mean
            spread = jnp.mean(center * center, axis=1, keepdims=True)
            mean_ref[rows, :] = jnp.broadcast_to(mean, (count, 128))
            root_ref[rows, :] = jnp.broadcast_to(lax.rsqrt(spread + 1e-05), (count, 128))

    columns = pl.ds(pl.multiple_of(order_ref[step] * block, block), block)
    values = tokens_ref[:, columns].astype(F32)
    normed = (values - mean_ref[:, :1]) * root_ref[:, :1] * gain_ref[:1, columns]
    places = lax.broadcasted_iota(jnp.int32, normed.shape, 0)
    before = jnp.where(places == 0, first_ref[:1, columns], pltpu.roll(normed, 1, 0))
    change = before - normed
    outs = [stack_ref.at[0], stack_ref.at[1], stack_ref.at[2], out3_ref, out4_ref]
    for m, out_ref in enumerate(outs):
        out_ref[...] = (normed + change * mix_ref[m : m + 1, columns]).astype(BF16)
    last = places == length_ref[0] - 1
    last_ref[...] = jnp.sum(jnp.where(last, normed, 0.0), axis=0, keepdims=True)


def prepare(order, length, tokens, gain, first, mixes):
    seq_len, width = tokens.shape
    blocks = order.shape[0]
    block = width // blocks

    def rows(count):
        return pl.BlockSpec((count, width), lambda j, *_: (0, 0))

    moved = pl.BlockSpec((3, seq_len, block), lambda j, *_: (0, 0, j))
    natural = pl.BlockSpec((seq_len, block), lambda j, order, *_: (0, order[j]))
    return pl.pallas_call(
        prepare_kernel,
        grid_spec=pltpu.PrefetchScalarGridSpec(
            num_scalar_prefetch=2,
            grid=(blocks,),
            in_specs=[rows(seq_len), rows(1), rows(1), rows(mixes.shape[0])],
            out_specs=[moved]
            + [natural] * 2
            + [pl.BlockSpec((1, block), lambda j, order, *_: (0, order[j]))],
            scratch_shapes=[pltpu.VMEM((seq_len, 128), F32)] * 2,
        ),
        out_shape=[jax.ShapeDtypeStruct((3, seq_len, width), BF16)]
        + [jax.ShapeDtypeStruct((seq_len, width), BF16)] * 2
        + [jax.ShapeDtypeStruct((1, width), F32)],
        compiler_params=pltpu.CompilerParams(vmem_limit_bytes=VMEM_BYTES),
        cost_estimate=pl.CostEstimate(
            flops=1 << 20, bytes_accessed=22 * MICROSECOND, transcendentals=0
        ),
        name="prepare",
    )(order, length, tokens, gain, first, mixes)


def regroup_kernel(*refs):
    out_ref = refs[-1]
    rows = refs[0].shape[0]
    for at, piece_ref in enumerate(refs[:-1]):
        out_ref[0, at * rows : (at + 1) * rows, :] = piece_ref[...].astype(BF16)


def regroup(pieces, hid):
    rows, width = pieces[0].shape
    wide = width // hid
    tall = rows * len(pieces)
    return pl.pallas_call(
        regroup_kernel,
        grid=(hid,),
        in_specs=[pl.BlockSpec((rows, wide), lambda h: (0, h))] * len(pieces),
        out_specs=pl.BlockSpec((1, tall, wide), lambda h: (h, 0, 0)),
        out_shape=jax.ShapeDtypeStruct((hid, tall, wide), BF16),
        compiler_params=pltpu.CompilerParams(vmem_limit_bytes=VMEM_BYTES),
        cost_estimate=pl.CostEstimate(flops=0, bytes_accessed=20 << 20, transcendentals=0),
        name="regroup",
    )(*pieces)


def project_kernel(*refs):
    values_ref, rows, out_ref = refs[0], refs[1:-1], refs[-1]
    if len(rows[0].shape) == 3:
        total, rows = rows[0][0], rows[1:]
    else:
        total = 0.0
    first = 0
    for rows_ref in rows:
        block = rows_ref[...]
        span = block.shape[0] * block.shape[2]
        values = values_ref[0, :, first : first + span]
        total = total + matmul(values, block.reshape(span, block.shape[3]))
        first += span
    out_ref[0] = total


def project(values, rows, at, of, base=None):
    _, tokens, width = values.shape
    count, wide = rows[0].shape[1], rows[0].shape[3]
    tile = min(256, wide)
    out = pl.BlockSpec((1, tokens, tile), lambda m, n: (m, 0, n))
    return pl.pallas_call(
        project_kernel,
        grid=(count, wide // tile),
        in_specs=[pl.BlockSpec((1, tokens, width // of), lambda m, n: (m, 0, at))]
        + [out] * (base is not None)
        + [
            pl.BlockSpec((r.shape[0], 1, r.shape[2], tile), lambda m, n: (0, m, 0, n))
            for r in rows
        ],
        out_specs=out,
        out_shape=jax.ShapeDtypeStruct((count, tokens, wide), F32),
        compiler_params=pltpu.CompilerParams(vmem_limit_bytes=VMEM_BYTES),
        cost_estimate=pl.CostEstimate(
            flops=2 * count * tokens * width // of * wide,
            bytes_accessed=30 << 20,
            transcendentals=0,
        ),
        name="project",
    )(values, *([] if base is None else [base]), *rows)


def channel_kernel(
    length_ref,
    tokens_ref,
    attended_ref,
    gain_ref,
    first_ref,
    mix_ref,
    middle_ref,
    key_ref,
    accept_ref,
    last_ref,
    held,
):
    step = pl.program_id(0)
    middle = (tokens_ref[...].astype(F32) + attended_ref[...].astype(F32)).astype(BF16)
    middle_ref[...] = middle
    values = middle.astype(F32)
    center = values - jnp.mean(values, axis=1, keepdims=True)
    spread = jnp.mean(center * center, axis=1, keepdims=True)
    normed = center * lax.rsqrt(spread + 1e-05) * gain_ref[...]
    count = normed.shape[0]

    @pl.when(step == 0)
    def _():
        held[...] = first_ref[...]
        last_ref[...] = jnp.zeros_like(last_ref)

    places = lax.broadcasted_iota(jnp.int32, normed.shape, 0)
    before = jnp.where(places == 0, held[...], pltpu.roll(normed, 1, 0))
    held[...] = normed[count - 1 :, :]
    change = before - normed
    key_ref[...] = (normed + change * mix_ref[:1, :]).astype(BF16)
    accept_ref[...] = (normed + change * mix_ref[1:2, :]).astype(BF16)
    last = places + step * count == length_ref[0] - 1
    last_ref[...] += jnp.sum(jnp.where(last, normed, 0.0), axis=0, keepdims=True)


def channel_inputs(length, tokens, attended, gain, first, mixes):
    seq_len, width = tokens.shape
    count = min(64, seq_len)
    tall = pl.BlockSpec((count, width), lambda i: (i, 0))

    def rows(number):
        return pl.BlockSpec((number, width), lambda i: (0, 0))

    return pl.pallas_call(
        channel_kernel,
        grid=(seq_len // count,),
        in_specs=[pl.BlockSpec(memory_space=pltpu.SMEM), tall, tall, rows(1), rows(1), rows(2)],
        out_specs=[tall, tall, tall, rows(1)],
        out_shape=[jax.ShapeDtypeStruct((seq_len, width), BF16)] * 3
        + [jax.ShapeDtypeStruct((1, width), F32)],
        scratch_shapes=[pltpu.VMEM((1, width), F32)],
        compiler_params=pltpu.CompilerParams(vmem_limit_bytes=VMEM_BYTES),
        cost_estimate=pl.CostEstimate(
            flops=1 << 20, bytes_accessed=8 * MICROSECOND, transcendentals=0
        ),
        name="channel_inputs",
    )(length, tokens, attended, gain, first, mixes)


def entry_kernel(places, *refs):
    mixed_ref, rows = refs[0], refs[1 : 1 + len(places)]
    out_ref, held, arrived = refs[1 + len(places) :]
    count, tokens, units = out_ref.shape
    copies = [
        pltpu.make_async_copy(ref, held.at[pl.ds(first, ref.shape[0]), :], arrived.at[at])
        for at, (ref, first) in enumerate(zip(rows, places))
    ]
    for copy in copies:
        copy.start()
    ready = 0
    for at in range(count):
        while ready < len(places) and places[ready] < (at + 1) * units:
            copies[ready].wait()
            ready += 1
        block = held[at * units : (at + 1) * units, :]
        inner = jnp.maximum(matmul_nt(mixed_ref[...], block), 0.0)
        out_ref[at] = (inner * inner).astype(BF16)


def entry_product(mixed, rows, units):
    tokens, width = mixed.shape
    places = [0]
    for block in rows:
        places.append(places[-1] + block.shape[0])
    count = places[-1] // units
    return pl.pallas_call(
        partial(entry_kernel, places[:-1]),
        in_specs=[pl.BlockSpec(memory_space=pltpu.VMEM)]
        + [pl.BlockSpec(memory_space=pl.ANY)] * len(rows),
        out_specs=pl.BlockSpec(memory_space=pltpu.VMEM),
        out_shape=jax.ShapeDtypeStruct((count, tokens, units), BF16),
        scratch_shapes=[
            pltpu.VMEM((places[-1], width), BF16),
            pltpu.SemaphoreType.DMA((len(rows),)),
        ],
        compiler_params=pltpu.CompilerParams(vmem_limit_bytes=VMEM_BYTES),
        cost_estimate=pl.CostEstimate(
            flops=1 << 20, bytes_accessed=15 * MICROSECOND, transcendentals=0
        ),
        name="entry_product",
    )(mixed, *rows)


def exit_kernel(hidden_ref, *refs):
    values, out_ref = refs[:-1], refs[-1]
    units = hidden_ref.shape[2]
    total, at, blocks = 0.0, 0, []
    for values_ref in values:
        blocks.append(values_ref[...])
        if sum(block.shape[0] for block in blocks) == units:
            total = total + matmul(hidden_ref[at], jnp.concatenate(blocks, axis=0))
            at, blocks = at + 1, []
    out_ref[...] = total.astype(BF16)


def exit_product(hidden, values):
    tokens = hidden.shape[1]
    width = values[0].shape[1]
    tile = min(512, width)
    return pl.pallas_call(
        exit_kernel,
        grid=(width // tile,),
        in_specs=[pl.BlockSpec(hidden.shape, lambda n: (0, 0, 0))]
        + [pl.BlockSpec((v.shape[0], tile), lambda n: (0, n)) for v in values],
        out_specs=pl.BlockSpec((tokens, tile), lambda n: (0, n)),
        out_shape=jax.ShapeDtypeStruct((tokens, width), BF16),
        compiler_params=pltpu.CompilerParams(vmem_limit_bytes=VMEM_BYTES),
        cost_estimate=pl.CostEstimate(
            flops=1 << 20, bytes_accessed=7 * MICROSECOND, transcendentals=0
        ),
        name="exit_product",
    )(hidden, *values)


def combine_kernel(slot_ref, length_ref, middle_ref, gate_ref, *refs):
    out_ref = refs[-1]
    present = lax.broadcasted_iota(jnp.int32, gate_ref.shape, 0) < length_ref[0]
    summed = jnp.concatenate([ref[...] for ref in refs[:-1]], axis=1).astype(F32)
    accept = 1.0 / (1.0 + jnp.exp(-gate_ref[...]))
    combined = middle_ref[...].astype(F32) + accept * summed
    out_ref[...] = jnp.where(present, combined, 0.0).astype(BF16)


def combine(slot, length, middle, gate, summed):
    seq_len, wide = gate.shape
    whole = pl.BlockSpec((seq_len, wide), lambda i, *_: (0, 0))
    parts = [pl.BlockSpec(part.shape, lambda i, *_: (0, 0)) for part in summed]
    return pl.pallas_call(
        combine_kernel,
        grid_spec=pltpu.PrefetchScalarGridSpec(
            num_scalar_prefetch=2,
            grid=(1,),
            in_specs=[pl.BlockSpec((seq_len, wide), lambda i, slot, *_: (0, slot[0])), whole]
            + parts,
            out_specs=whole,
        ),
        out_shape=jax.ShapeDtypeStruct((seq_len, wide), BF16),
        compiler_params=pltpu.CompilerParams(vmem_limit_bytes=VMEM_BYTES),
        cost_estimate=pl.CostEstimate(
            flops=1 << 20, bytes_accessed=3 * MICROSECOND, transcendentals=0
        ),
        name="combine",
    )(slot, length, middle, gate, *summed)


def local(
    input_activations,
    prompt_extents,
    continuing_flags,
    owning_index,
    partition_arrangement,
    training_accept_pieces,
    training_lookup_pieces,
    training_content_pieces,
    normalizer_scales,
    prior_step_blends,
    forgetting_bias_vector,
    forgetting_left_lowrank,
    forgetting_right_lowrank,
    instant_emphasis,
    group_normalizer_scale,
    gating_projection,
    mixing_exit_projection,
    kept_summary_places,
    previous_normed_entries,
    feedforward_entry_proj,
    feedforward_exit_proj,
    feedforward_accept_proj,
):
    hid = lax.axis_size("hid")
    req = lax.axis_size("req")
    here = lax.axis_index("req")
    slot = lax.axis_index("hid")
    token_rows = input_activations[0]
    seq_len, width = token_rows.shape
    local_width = mixing_exit_projection.shape[0]
    heads = local_width // GROUP_DIMENSION
    shards = partition_arrangement.shape[0]
    shard_rows = width // shards
    length = prompt_extents[0]
    resuming = continuing_flags[0]

    owned = (resuming == 1) & (owning_index[0] == slot)
    saved = jnp.where(owned, kept_summary_places[0, 0].astype(BF16), 0)
    start = lax.psum_scatter(
        saved.reshape(saved.shape[0], -1), "hid", scatter_dimension=0, tiled=True
    )
    start = start.astype(F32).reshape(heads, GROUP_DIMENSION, GROUP_DIMENSION)

    order = jnp.concatenate(
        [
            lax.dynamic_slice_in_dim(partition_arrangement, (here ^ d) * hid, hid, 0)
            for d in range(req)
        ]
    )
    gain_rows = normalizer_scales.astype(F32)
    mix_rows = prior_step_blends.astype(F32)
    carried = jnp.where(resuming == 1, previous_normed_entries[0].astype(F32), 0.0)
    if shard_rows % 128 == 0:
        blended, decay_in, gate_in, last_in = prepare(
            order, prompt_extents, token_rows, gain_rows[:1], carried[:1], mix_rows[:5]
        )
    else:
        normed_in = layer_norm(token_rows.astype(F32), gain_rows[0])
        before = shifted(normed_in, carried[0])
        rec_in, key_in, val_in, decay_in, gate_in = [
            (normed_in + (before - normed_in) * mix_rows[m][None, :]).astype(BF16)
            for m in range(5)
        ]
        blended = jnp.stack([rec_in, key_in, val_in]).reshape(3, seq_len, shards, shard_rows)
        blended = jnp.take(blended, order, axis=2).reshape(3, seq_len, width)
        last_in = lax.dynamic_slice_in_dim(normed_in, length - 1, 1, 0)

    def side_products(decay_in, gate_in):
        low_rank = jnp.tanh(matmul(decay_in, forgetting_left_lowrank)).astype(BF16)
        return matmul(low_rank, forgetting_right_lowrank), matmul(gate_in, gating_projection)

    def to_heads(columns):
        mine = lax.all_to_all(columns, "hid", split_axis=0, concat_axis=0, tiled=True)
        mine = mine.reshape(hid, -1, shard_rows, local_width)
        return [mine[: hid // 2], mine[hid // 2 :]]

    columns = regroup(
        [training_accept_pieces, training_lookup_pieces, training_content_pieces], hid
    )
    units = feedforward_entry_proj.shape[0]
    hold = lax.optimization_barrier
    if req == 4:
        half = units // 2
        cut = half * 5 // 7 // 16 * 16
        key_mine, value_mine = feedforward_entry_proj, feedforward_exit_proj
        key_x, key_y = across(key_mine, 1), across(key_mine, 2)
        mine = to_heads(columns)
        decay, gate = side_products(decay_in, gate_in)
        mine, key_x, key_y, blended, decay, gate, start = hold(
            (mine, key_x, key_y, blended, decay, gate, start)
        )
        trained = [mine, [across(rows, 1) for rows in mine], [across(rows, 2) for rows in mine]]
        first = [key_x[:cut], key_y[half : half + cut]]
        second = [key_x[cut:half], key_y[half + cut :]]
        trained, first, second = hold((trained, first, second))
        opposite = [across(trained[1][0], 2), across(trained[2][1], 1)]
        projected = project(blended, sum(trained, []), 0, 1)
        projected, opposite, first = hold((projected, opposite, first))
        key_far = [across(first[0], 2), across(first[1], 1)]
        projected = project(blended, opposite, 3, 4, projected)
    else:
        decay, gate = side_products(decay_in, gate_in)
        low, high = [whole(side, req) for side in to_heads(columns)]
        projected = project(blended, [side[d] for d in range(req) for side in (low, high)], 0, 1)
    gated, new_state = recurrence(
        prompt_extents,
        projected,
        decay,
        gate,
        forgetting_bias_vector[None],
        instant_emphasis[None],
        group_normalizer_scale[None],
        start,
    )
    if req == 4:
        gated, value_mine, second, key_far = hold((gated, value_mine, second, key_far))
    head_terms = matmul(gated, mixing_exit_projection).astype(BF16)
    attended = lax.psum(head_terms, "hid")
    if req == 4:
        value_x, value_y = across(value_mine, 1), across(value_mine, 2)
        key_far.insert(1, across(second[0], 2))
        key_far.append(across(second[1], 1))
        value_far = [value_x[:half], value_y[half:]]
        attended, key_far, value_far = hold((attended, key_far, value_far))
        value_far = [across(value_far[0], 2), across(value_far[1], 1)]
        key_rows = [key_mine, key_x, key_y, *key_far]
        value_rows = [value_mine, value_x, value_y, *value_far]
    else:
        key_rows = whole(feedforward_entry_proj, req)
        value_rows = whole(feedforward_exit_proj, req)
    middle, mixed_key, mixed_accept, last_chan = channel_inputs(
        prompt_extents, token_rows, attended, gain_rows[1:], carried[1:], mix_rows[5:]
    )
    accept = matmul(mixed_accept, feedforward_accept_proj)
    hidden = entry_product(mixed_key, key_rows, units)
    terms = exit_product(hidden, value_rows)
    summed = lax.psum_scatter(terms, "hid", scatter_dimension=1, tiled=True)
    layer_out = combine(slot[None], prompt_extents, middle, accept, [summed])[None]
    shift_out = jnp.concatenate([last_in, last_chan]).astype(BF16)[None]
    return (layer_out, new_state[None], shift_out)


def solution(mesh):
    placed = (
        P("req", None, None),
        P("req"),
        P("req"),
        P("req"),
        P(),
        P(("req", "hid"), None),
        P(("req", "hid"), None),
        P(("req", "hid"), None),
        P(),
        P(),
        P("hid"),
        P(),
        P(None, "hid"),
        P("hid"),
        P("hid"),
        P(None, "hid"),
        P("hid", None),
        P("req", "hid", None, None, None),
        P("req", None, None),
        P(("req", "hid"), None),
        P(("req", "hid"), None),
        P(None, "hid"),
    )
    return jax.shard_map(
        local,
        mesh=mesh,
        in_specs=placed,
        out_specs=(P("req", None, "hid"), P("req", "hid", None, None), P("req", None, None)),
        check_vma=False,
    )
```

time: 534 us -> 464 us (0.87); the launches traced: 524 us -> 462 us
  Pallas kernels: 54.5 us -> 118 us
  local copies, waits for them, and re-layouts: 62.9 us -> 23.6 us
  matrix products: 63.7 us -> 25.2 us
  starting transfers between devices: 52.2 us -> 24 us
  other arithmetic: 15.2 us -> 3.03 us
  waiting for transfers between devices: 259 us -> 253 us
    pallas_call x3 -> x8, Pallas kernels: 32.5 us -> 92.1 us  [the longest x2 21.5 us: project(): pl.pallas_call(project_kernel, grid=(count, wide // tile), in_specs=[pl.B...]
    ppermute x36 -> x16, waiting for transfers between devices: 222 us -> 169 us  [across(): return lax.ppermute(value, 'req', [(i, i ^ axis) for i in range(4)])]
    all_to_all x3 -> x1, waiting for transfers between devices: 0.01 us -> 26.5 us  [to_heads(): lax.all_to_all(columns, 'hid', split_axis=0, concat_axis=0, tiled=True)]
    dot_general x28 -> x4, matrix products: 47.1 us -> 25.2 us  [matmul(): return jnp.dot(a, b, preferred_element_type=F32)]
    unnamed x89 -> x34, local copies, waits for them, and re-layouts: 21.5 us -> 1.94 us
    ppermute x36 -> x16, starting transfers between devices: 37.1 us -> 17.5 us  [across(): return lax.ppermute(value, 'req', [(i, i ^ axis) for i in range(4)])]
    dot_general x8 -> x0, matrix products: 16.7 us -> none  [matmul_nt(): lax.dot_general(a, b, (((1,), (1,)), ((), ())), preferred_element_type=F32)]
    psum x1, waiting for transfers between devices: 2.85 us -> 15.3 us  [local(): attended = lax.psum(head_terms, 'hid')]
  transfers between devices with their start and end apart: 43 -> 20, of which waited for: 26 -> 16; matrix products, arithmetic and copies ran while one was open for 21% -> 11% of each run, Pallas kernels for 5% -> 20%
where the time goes in v2:
time: 464 us; the launch traced here: 462 us
  waiting for transfers between devices  253 us (55%)
  Pallas kernels  118 us (25%)
  matrix products  25.2 us (5%)
  starting transfers between devices  24 us (5%)
  local copies, waits for them, and re-layouts  23.6 us (5%)
  between operations  15.9 us (3%)
    ppermute x16, waiting for transfers between devices, across(): return lax.ppermute(value, 'req', [(i, i ^ axis) for i in range(4)])  169 us
    reduce_scatter x1, waiting for transfers between devices, local(): summed = lax.psum_scatter(terms, 'hid', scatter_dimension=1, tiled=True)  42.1 us
    all_to_all x1, waiting for transfers between devices, to_heads(): lax.all_to_all(columns, 'hid', split_axis=0, concat_axis=0, tiled=True)  26.5 us
    pallas_call x1, Pallas kernels, prepare(): pl.pallas_call(prepare_kernel, grid_spec=pltpu.PrefetchScalarGridSpec(num...  25.4 us
    dot_general x4, matrix products, matmul(): return jnp.dot(a, b, preferred_element_type=F32)  25.2 us
    pallas_call x2, Pallas kernels, project(): pl.pallas_call(project_kernel, grid=(count, wide // tile), in_specs=[pl.B...  21.5 us
    pallas_call x1, Pallas kernels, recurrence(): pl.pallas_call(recurrence_kernel, grid=(width // lanes,), in_specs=[pl.Bl...  19 us
    ppermute x16, starting transfers between devices, across(): return lax.ppermute(value, 'req', [(i, i ^ axis) for i in range(4)])  17.5 us
  transfers between devices with their start and end apart: 20, of which 16 were waited for; matrix products, arithmetic and copies ran while one was open for 11% of the time, Pallas kernels for 20%

profile of v2, /device:TPU:0, one launch (start us, length us, event | category | flops | bytes accessed | tf_op | source)
XLA Modules:
  0.0 462.5 jit_solution(2484954702592747494)
XLA Ops:
  7.2 6.8 %regroup.1 = bf16[8,384,512]{2,1,0:T(8,128)(2,1)} custom-call(f32[128,4096]{1,0:T(8,128)} %refs_0_.1, f32[128,4096]{1,0:T(8,128)} %refs_1_.2, f32[128,4096]{1,0:T(8,128)} %refs_2_.1), custom_call_target="tpu_custom_call" | custom-call | bytes 20971520 | tf_op jit(solution)/shard_map/regroup/pallas_call | solution.py:265
  14.0 6.3 %all-to-all-start = ((bf16[8,384,512]{2,1,0:T(8,128)(2,1)}), bf16[8,384,512]{2,1,0:T(8,128)(2,1)}, u32[]{:S(2)}, u32[]{:S(2)}) async-start(bf16[8,384,512]{2,1,0:T(8,128)(2,1)} %regroup.1), calls=%async_computation | async-start | bytes 6291456 | tf_op jit(solution)/shard_map/all_to_all | solution.py:559
  20.4 1.6 collective-permute-start
  22.0 1.5 collective-permute-start.1
  24.8 1.7 convert_select_fusion
  26.5 1.6 select_n.41
  31.6 25.4 %prepare.1 = (bf16[3,512,4096]{2,1,0:T(8,128)(2,1)}, bf16[512,4096]{1,0:T(8,128)(2,1)}, bf16[512,4096]{1,0:T(8,128)(2,1)}, f32[1,4096]{1,0:T(1,128)}) custom-call(s32[32]{0:T(128)} %pad_add_fusion.order_ref, s32[1]{0:T(128)S(6)} %copy.26.length_ref, bf16[512,4096]{1,0:T(8,128)(2,1)} %bitcast.31, f32[1,4096]{1,0:T(1,128)} %get-tuple-element.100.gain_ref, ...), custom_call_target="tpu_custom_call" | custom-call | flops 1048576 | bytes 81180000 | tf_op jit(solution)/shard_map/prepare/pallas_call | solution.py:232
  57.0 4.8 %fusion.1.decay_ref = f32[512,512]{1,0:T(8,128)} fusion(bf16[128,512]{1,0:T(8,128)(2,1)S(1)} %copy-done.11, bf16[512,4096]{1,0:T(8,128)(2,1)} %get-tuple-element.50, bf16[4096,128]{1,0:T(8,128)(2,1)S(1)} %copy-done), kind=kOutput, calls=%fused_computation.3 | convolution fusion | flops 604045312 | bytes 6422528 | tf_op jit(solution)/shard_map/dot_general | solution.py:30
  61.8 6.8 %fusion.5.gate_ref = f32[512,512]{1,0:T(8,128)} fusion(bf16[512,4096]{1,0:T(8,128)(2,1)} %get-tuple-element.51, bf16[4096,512]{1,0:T(8,128)(2,1)} %param.37), kind=kOutput, calls=%fused_computation.15 | convolution fusion | flops 2147483648 | bytes 9437184 | tf_op jit(solution)/shard_map/dot_general | solution.py:30
  68.7 1.8 reshape.63.start_ref
  70.4 26.5 %all-to-all-done = bf16[8,384,512]{2,1,0:T(8,128)(2,1)} async-done(((bf16[8,384,512]{2,1,0:T(8,128)(2,1)}), bf16[8,384,512]{2,1,0:T(8,128)(2,1)}, u32[]{:S(2)}, u32[]{:S(2)}) %all-to-all-start) | async-done | bytes 3145760 | tf_op jit(solution)/shard_map/all_to_all | solution.py:559
  96.9 2.1 fusion.2
  99.0 3.5 collective-permute-done.refs_2_
  102.5 1.2 collective-permute-done.1.refs_3_
  103.8 1.5 collective-permute-start.4
  106.3 1.5 collective-permute-start.3
  107.8 1.9 slice.64
  109.7 2.5 slice.62
  112.2 1.9 slice.65
  114.0 1.4 slice.63
  115.5 25.6 %collective-permute-done.4.refs_5_ = bf16[4,3,128,512]{3,2,1,0:T(8,128)(2,1)S(1)} collective-permute-done((bf16[4,3,128,512]{3,2,1,0:T(8,128)(2,1)S(1)}, bf16[4,3,128,512]{3,2,1,0:T(8,128)(2,1)S(1)}, u32[]{:S(2)}, u32[]{:S(2)}) %collective-permute-start.4) | collective-permute-done | bytes 1572896 | tf_op jit(solution)/shard_map/ppermute | solution.py:42
  141.1 1.6 collective-permute-done.2.refs_3_
  142.7 30.5 %collective-permute-done.5.refs_6_ = bf16[4,3,128,512]{3,2,1,0:T(8,128)(2,1)} collective-permute-done((bf16[4,3,128,512]{3,2,1,0:T(8,128)(2,1)S(1)}, bf16[4,3,128,512]{3,2,1,0:T(8,128)(2,1)}, u32[]{:S(2)}, u32[]{:S(2)}) %collective-permute-start.5) | collective-permute-done | bytes 1572896 | tf_op jit(solution)/shard_map/ppermute | solution.py:42
  173.2 1.1 collective-permute-done.3.refs_4_
  174.4 1.2 copy-done.6
  176.7 13.5 %project.2.refs_1_ = f32[3,512,512]{2,1,0:T(8,128)} custom-call(bf16[3,512,4096]{2,1,0:T(8,128)(2,1)} %get-tuple-element.52.refs_0_, bf16[4,3,128,512]{3,2,1,0:T(8,128)(2,1)} %bitcast.38, bf16[4,3,128,512]{3,2,1,0:T(8,128)(2,1)} %bitcast.35, bf16[4,3,128,512]{3,2,1,0:T(8,128)(2,1)} %collective-permute-done.2.refs_3_, bf16[4,3,128,512]{3,2,1,0:T(8,128)(2,1)} %copy-done.6, ...), custom_call_target="tpu_custom_call" | custom-call | flops 6442450944 | bytes 31457280 | tf_op jit(solution)/shard_map/project/pallas_call | solution.py:298
  190.2 20.3 %collective-permute-done.6.refs_2_ = bf16[4,3,128,512]{3,2,1,0:T(8,128)(2,1)} collective-permute-done((bf16[4,3,128,512]{3,2,1,0:T(8,128)(2,1)}, bf16[4,3,128,512]{3,2,1,0:T(8,128)(2,1)}, u32[]{:S(2)}, u32[]{:S(2)}) %collective-permute-start.6) | collective-permute-done | bytes 1572896 | tf_op jit(solution)/shard_map/ppermute | solution.py:42
  210.7 1.5 collective-permute-start.8
  212.9 8.0 %project.3.rec_ref.key_ref.val_ref = f32[3,512,512]{2,1,0:T(8,128)} custom-call(bf16[3,512,4096]{2,1,0:T(8,128)(2,1)} %get-tuple-element.52.refs_0_, f32[3,512,512]{2,1,0:T(8,128)} %project.2.refs_1_, bf16[4,3,128,512]{3,2,1,0:T(8,128)(2,1)} %collective-permute-done.6.refs_2_, bf16[4,3,128,512]{3,2,1,0:T(8,128)(2,1)} %collective-permute-done.7.refs_3_), custom_call_target="tpu_custom_call" | custom-call | flops 1610612736 | bytes 31457280 | tf_op jit(solution)/shard_map/project/pallas_call | solution.py:298
  220.9 19.0 %recurrence.1 = (bf16[512,512]{1,0:T(8,128)(2,1)}, f32[8,64,64]{2,1,0:T(8,128)}) custom-call(s32[1]{0:T(128)S(6)} %copy.26.length_ref, f32[3,512,512]{2,1,0:T(8,128)} %project.3.rec_ref.key_ref.val_ref, f32[3,512,512]{2,1,0:T(8,128)} %project.3.rec_ref.key_ref.val_ref, f32[3,512,512]{2,1,0:T(8,128)} %project.3.rec_ref.key_ref.val_ref, ...), custom_call_target="tpu_custom_call" | custom-call | flops 1048576 | bytes 66420000 | tf_op jit(solution)/shard_map/recurrence/pallas_call | solution.py:157
  240.5 1.3 collective-permute-start.12
  241.9 6.7 %convolution_convert_fusion = bf16[512,4096]{1,0:T(8,128)(2,1)} fusion(bf16[512,512]{1,0:T(8,128)(2,1)} %get-tuple-element.76, bf16[512,4096]{1,0:T(8,128)(2,1)} %param.38), kind=kOutput, calls=%fused_computation | convolution fusion | flops 2149580800 | bytes 8912896 | tf_op jit(solution)/shard_map/dot_general | solution.py:30
  248.6 1.5 collective-permute-start.10
  250.8 71.7 %collective-permute-done.13.refs_2_ = bf16[448,4096]{1,0:T(8,128)(2,1)} collective-permute-done((bf16[448,4096]{1,0:T(8,128)(2,1)}, bf16[448,4096]{1,0:T(8,128)(2,1)}, u32[]{:S(2)}, u32[]{:S(2)}) %collective-permute-start.13) | collective-permute-done | bytes 3670048 | tf_op jit(solution)/shard_map/ppermute | solution.py:42
  322.5 3.0 slice.78
  325.5 3.0 slice.77
  328.5 0.8 collective-permute-done.10.refs_5_
  329.6 15.3 %all-reduce.2.cloned.1.call-done.attended_ref = bf16[512,4096]{1,0:T(8,128)(2,1)} async-done(((bf16[512,4096]{1,0:T(8,128)(2,1)}), bf16[512,4096]{1,0:T(8,128)(2,1)}) %all-reduce.2.cloned.1.call-update) | async-done | bytes 4194320 | tf_op jit(solution)/shard_map/psum | solution.py:604
  344.8 1.5 collective-permute-start.14
  346.3 1.5 collective-permute-start.15
  348.4 12.2 %channel_inputs.1 = (bf16[512,4096]{1,0:T(8,128)(2,1)}, bf16[512,4096]{1,0:T(8,128)(2,1)}, bf16[512,4096]{1,0:T(8,128)(2,1)}, f32[1,4096]{1,0:T(1,128)}) custom-call(s32[1]{0:T(128)S(6)} %copy.26.length_ref, bf16[512,4096]{1,0:T(8,128)(2,1)} %bitcast.32, bf16[512,4096]{1,0:T(8,128)(2,1)} %all-reduce.2.cloned.1.call-done.attended_ref, ...), custom_call_target="tpu_custom_call" | custom-call | flops 1048576 | bytes 29520000 | tf_op jit(solution)/shard_map/channel_inputs/pallas_call | solution.py:364
  360.6 15.0 %entry_product.1.hidden_ref = bf16[4,512,448]{2,1,0:T(8,128)(2,1)} custom-call(bf16[512,4096]{1,0:T(8,128)(2,1)} %get-tuple-element.85.refs_0_, bf16[448,4096]{1,0:T(8,128)(2,1)} %refs_1_.3, bf16[448,4096]{1,0:T(8,128)(2,1)} %collective-permute-done.refs_2_, bf16[448,4096]{1,0:T(8,128)(2,1)} %collective-permute-done.1.refs_3_, ...), custom_call_target="tpu_custom_call" | custom-call | flops 1048576 | bytes 55350000 | tf_op jit(solution)/shard_map/entry_product/pallas_call | solution.py:406
  375.6 11.1 %collective-permute-done.14.refs_3_ = bf16[224,4096]{1,0:T(8,128)(2,1)S(1)} collective-permute-done((bf16[224,4096]{1,0:T(8,128)(2,1)}, bf16[224,4096]{1,0:T(8,128)(2,1)S(1)}, u32[]{:S(2)}, u32[]{:S(2)}) %collective-permute-start.14) | collective-permute-done | bytes 1835040 | tf_op jit(solution)/shard_map/ppermute | solution.py:42
  386.7 1.3 collective-permute-done.15.refs_4_
  388.0 14.9 %exit_product.1 = bf16[512,4096]{1,0:T(8,128)(2,1)} custom-call(bf16[4,512,448]{2,1,0:T(8,128)(2,1)} %entry_product.1.hidden_ref, bf16[448,4096]{1,0:T(8,128)(2,1)} %refs_0_.2, bf16[448,4096]{1,0:T(8,128)(2,1)} %collective-permute-done.12.refs_1_, bf16[448,4096]{1,0:T(8,128)(2,1)} %collective-permute-done.13.refs_2_, bf16[224,4096]{1,0:T(8,128)(2,1)} %copy-done.4, ...), custom_call_target="tpu_custom_call" | custom-call | flops 1048576 | bytes 25830000 | tf_op jit(solution)/shard_map/exit_product/pallas_call | solution.py:440
  404.3 6.9 %fusion.6.gate_ref = f32[512,512]{1,0:T(8,128)} fusion(bf16[512,4096]{1,0:T(8,128)(2,1)} %get-tuple-element.84, bf16[4096,512]{1,0:T(8,128)(2,1)} %param.43), kind=kOutput, calls=%fused_computation.16 | convolution fusion | flops 2147483648 | bytes 9437184 | tf_op jit(solution)/shard_map/dot_general | solution.py:30
  411.2 42.1 %reduce-scatter.5.cloned.1.call-done.refs_0_ = bf16[512,512]{1,0:T(8,128)(2,1)} async-done(((bf16[512,4096]{1,0:T(8,128)(2,1)}), bf16[512,512]{1,0:T(8,128)(2,1)}) %reduce-scatter.5.cloned.1.call-update) | async-done | bytes 524304 | tf_op jit(solution)/shard_map/reduce_scatter | solution.py:623
  453.2 2.7 combine.1
  (61 shorter events, 9.7 us)
Async XLA Ops:
  7.2 49.8 %copy-start = (bf16[4096,128]{1,0:T(8,128)(2,1)S(1)}, bf16[4096,128]{1,0:T(8,128)(2,1)}, u32[]{:S(2)}) copy-start(bf16[4096,128]{1,0:T(8,128)(2,1)} %param.33) | copy-start | bytes 3145732
  14.0 82.9 %all-to-all-start = ((bf16[8,384,512]{2,1,0:T(8,128)(2,1)}), bf16[8,384,512]{2,1,0:T(8,128)(2,1)}, u32[]{:S(2)}, u32[]{:S(2)}) async-start(bf16[8,384,512]{2,1,0:T(8,128)(2,1)} %regroup.1), calls=%async_computation | async-start | bytes 6291456 | tf_op jit(solution)/shard_map/all_to_all | solution.py:559
  20.3 7.9 %copy-start.13 = (bf16[1,2,4096]{2,1,0:T(2,128)(2,1)S(1)}, bf16[1,2,4096]{2,1,0:T(2,128)(2,1)}, u32[]{:S(2)}) copy-start(bf16[1,2,4096]{2,1,0:T(2,128)(2,1)} %param.40) | copy-start | bytes 49156
  20.3 8.6 %copy-start.10 = (bf16[7,4096]{1,0:T(8,128)(2,1)S(1)}, bf16[7,4096]{1,0:T(8,128)(2,1)}, u32[]{:S(2)}) copy-start(bf16[7,4096]{1,0:T(8,128)(2,1)} %param.31) | copy-start | bytes 172036
  20.4 9.2 %copy-start.16 = (s32[32]{0:T(128)S(1)}, s32[32]{0:T(128)}, u32[]{:S(2)}) copy-start(s32[32]{0:T(128)} %param.26) | copy-start | bytes 388
  20.4 10.0 %copy-start.12 = (bf16[2,4096]{1,0:T(2,128)(2,1)S(1)}, bf16[2,4096]{1,0:T(2,128)(2,1)}, u32[]{:S(2)}) copy-start(bf16[2,4096]{1,0:T(2,128)(2,1)} %param.30) | copy-start | bytes 49156
  20.4 48.3 %reduce-scatter.3.cloned.1.call-start = ((), (), s32[]{:S(2)}) async-start(), calls=%async_computation.3 | async-start | bytes 589824 | tf_op jit(solution)/shard_map/reduce_scatter | solution.py:525
  20.4 82.1 %collective-permute-start = (bf16[448,4096]{1,0:T(8,128)(2,1)}, bf16[448,4096]{1,0:T(8,128)(2,1)}, u32[]{:S(2)}, u32[]{:S(2)}) collective-permute-start(bf16[448,4096]{1,0:T(8,128)(2,1)} %refs_1_.3), channel_id=1, source_target_pairs={{0,8},{8,0},{16,24},{24,16},{1,9},{9,1},{17,25},{25,17},{2,10},{10... | collective-permute-start | bytes 11010056 | tf_op jit(solution)/shard_map/ppermute | solution.py:42
  22.0 81.8 %collective-permute-start.1 = (bf16[448,4096]{1,0:T(8,128)(2,1)}, bf16[448,4096]{1,0:T(8,128)(2,1)}, u32[]{:S(2)}, u32[]{:S(2)}) collective-permute-start(bf16[448,4096]{1,0:T(8,128)(2,1)} %refs_1_.3), channel_id=1, source_target_pairs={{0,16},{8,24},{16,0},{24,8},{1,17},{9,25},{17,1},{25,9},{2,18},{10... | collective-permute-start | bytes 11010056 | tf_op jit(solution)/shard_map/ppermute | solution.py:42
  26.5 30.5 %copy-start.11 = (bf16[128,512]{1,0:T(8,128)(2,1)S(1)}, bf16[128,512]{1,0:T(8,128)(2,1)}, u32[]{:S(2)}) copy-start(bf16[128,512]{1,0:T(8,128)(2,1)} %param.34) | copy-start | bytes 393220
  28.2 316.7 %all-reduce.2.cloned.1.call-start = ((), (), s32[]{:S(2)}) async-start(), calls=%async_computation.4 | async-start | bytes 8388608 | tf_op jit(solution)/shard_map/psum | solution.py:604
  99.0 16.5 %copy-start.2 = (bf16[4,384,512]{2,1,0:T(8,128)(2,1)}, bf16[4,384,512]{2,1,0:T(8,128)(2,1)S(1)}, u32[]{:S(2)}) copy-start(bf16[4,384,512]{2,1,0:T(8,128)(2,1)S(1)} %get-tuple-element.95) | copy-start | bytes 4718596
  99.0 16.5 %copy-start.3 = (bf16[4,384,512]{2,1,0:T(8,128)(2,1)}, bf16[4,384,512]{2,1,0:T(8,128)(2,1)S(1)}, u32[]{:S(2)}) copy-start(bf16[4,384,512]{2,1,0:T(8,128)(2,1)S(1)} %get-tuple-element.96) | copy-start | bytes 4718596
  103.8 37.3 %collective-permute-start.4 = (bf16[4,3,128,512]{3,2,1,0:T(8,128)(2,1)S(1)}, bf16[4,3,128,512]{3,2,1,0:T(8,128)(2,1)S(1)}, u32[]{:S(2)}, u32[]{:S(2)}) collective-permute-start(bf16[4,3,128,512]{3,2,1,0:T(8,128)(2,1)S(1)} %bitcast.36), channel_id=1, source_target_pairs={{0,16},{8,24},{16,0},{24,8},{1,17},{9,25},{17,1},{25,9},{2,18},{10... | collective-permute-start | bytes 4718600 | tf_op jit(solution)/shard_map/ppermute | solution.py:42
  105.3 37.4 %collective-permute-start.2 = (bf16[4,3,128,512]{3,2,1,0:T(8,128)(2,1)S(1)}, bf16[4,3,128,512]{3,2,1,0:T(8,128)(2,1)}, u32[]{:S(2)}, u32[]{:S(2)}) collective-permute-start(bf16[4,3,128,512]{3,2,1,0:T(8,128)(2,1)S(1)} %bitcast.37), channel_id=1, source_target_pairs={{0,8},{8,0},{16,24},{24,16},{1,9},{9,1},{17,25},{25,17},{2,10},{10... | collective-permute-start | bytes 4718600 | tf_op jit(solution)/shard_map/ppermute | solution.py:42
  105.8 67.4 %collective-permute-start.5 = (bf16[4,3,128,512]{3,2,1,0:T(8,128)(2,1)S(1)}, bf16[4,3,128,512]{3,2,1,0:T(8,128)(2,1)}, u32[]{:S(2)}, u32[]{:S(2)}) collective-permute-start(bf16[4,3,128,512]{3,2,1,0:T(8,128)(2,1)S(1)} %bitcast.33), channel_id=1, source_target_pairs={{0,16},{8,24},{16,0},{24,8},{1,17},{9,25},{17,1},{25,9},{2,18},{10... | collective-permute-start | bytes 4718600 | tf_op jit(solution)/shard_map/ppermute | solution.py:42
  106.3 68.1 %collective-permute-start.3 = (bf16[4,3,128,512]{3,2,1,0:T(8,128)(2,1)S(1)}, bf16[4,3,128,512]{3,2,1,0:T(8,128)(2,1)S(1)}, u32[]{:S(2)}, u32[]{:S(2)}) collective-permute-start(bf16[4,3,128,512]{3,2,1,0:T(8,128)(2,1)S(1)} %bitcast.34), channel_id=1, source_target_pairs={{0,8},{8,0},{16,24},{24,16},{1,9},{9,1},{17,25},{25,17},{2,10},{10... | collective-permute-start | bytes 4718600 | tf_op jit(solution)/shard_map/ppermute | solution.py:42
  141.1 35.6 %copy-start.5 = (bf16[4,3,128,512]{3,2,1,0:T(8,128)(2,1)}, bf16[4,3,128,512]{3,2,1,0:T(8,128)(2,1)S(1)}, u32[]{:S(2)}) copy-start(bf16[4,3,128,512]{3,2,1,0:T(8,128)(2,1)S(1)} %collective-permute-done.4.refs_5_) | copy-start | bytes 4718596
  174.4 1.2 copy-start.6
  175.5 34.9 %collective-permute-start.6 = (bf16[4,3,128,512]{3,2,1,0:T(8,128)(2,1)}, bf16[4,3,128,512]{3,2,1,0:T(8,128)(2,1)}, u32[]{:S(2)}, u32[]{:S(2)}) collective-permute-start(bf16[4,3,128,512]{3,2,1,0:T(8,128)(2,1)} %collective-permute-done.2.refs_3_), channel_id=1, source_target_pairs={{0,16},{8,24},{16,0},{24,8},{1,17},{9,25},{17,1},{25,9},{2,18},{10... | collective-permute-start | bytes 4718600 | tf_op jit(solution)/shard_map/ppermute | solution.py:42
  176.1 34.7 %collective-permute-start.7 = (bf16[4,3,128,512]{3,2,1,0:T(8,128)(2,1)}, bf16[4,3,128,512]{3,2,1,0:T(8,128)(2,1)}, u32[]{:S(2)}, u32[]{:S(2)}) collective-permute-start(bf16[4,3,128,512]{3,2,1,0:T(8,128)(2,1)} %collective-permute-done.5.refs_6_), channel_id=1, source_target_pairs={{0,8},{8,0},{16,24},{24,16},{1,9},{9,1},{17,25},{25,17},{2,10},{10... | collective-permute-start | bytes 4718600 | tf_op jit(solution)/shard_map/ppermute | solution.py:42
  210.7 29.1 %collective-permute-start.8 = (bf16[160,4096]{1,0:T(8,128)(2,1)}, bf16[160,4096]{1,0:T(8,128)(2,1)}, u32[]{:S(2)}, u32[]{:S(2)}) collective-permute-start(bf16[160,4096]{1,0:T(8,128)(2,1)} %slice.62), channel_id=1, source_target_pairs={{0,16},{8,24},{16,0},{24,8},{1,17},{9,25},{17,1},{25,9},{2,18},{10... | collective-permute-start | bytes 3932168 | tf_op jit(solution)/shard_map/ppermute | solution.py:42
  212.2 27.7 %collective-permute-start.9 = (bf16[160,4096]{1,0:T(8,128)(2,1)S(1)}, bf16[160,4096]{1,0:T(8,128)(2,1)}, u32[]{:S(2)}, u32[]{:S(2)}) collective-permute-start(bf16[160,4096]{1,0:T(8,128)(2,1)S(1)} %slice.63), channel_id=1, source_target_pairs={{0,8},{8,0},{16,24},{24,16},{1,9},{9,1},{17,25},{25,17},{2,10},{10... | collective-permute-start | bytes 3932168 | tf_op jit(solution)/shard_map/ppermute | solution.py:42
  239.9 82.7 %collective-permute-start.13 = (bf16[448,4096]{1,0:T(8,128)(2,1)}, bf16[448,4096]{1,0:T(8,128)(2,1)}, u32[]{:S(2)}, u32[]{:S(2)}) collective-permute-start(bf16[448,4096]{1,0:T(8,128)(2,1)} %refs_0_.2), channel_id=1, source_target_pairs={{0,16},{8,24},{16,0},{24,8},{1,17},{9,25},{17,1},{25,9},{2,18},{10... | collective-permute-start | bytes 11010056 | tf_op jit(solution)/shard_map/ppermute | solution.py:42
  240.5 85.0 %collective-permute-start.12 = (bf16[448,4096]{1,0:T(8,128)(2,1)}, bf16[448,4096]{1,0:T(8,128)(2,1)}, u32[]{:S(2)}, u32[]{:S(2)}) collective-permute-start(bf16[448,4096]{1,0:T(8,128)(2,1)} %refs_0_.2), channel_id=1, source_target_pairs={{0,8},{8,0},{16,24},{24,16},{1,9},{9,1},{17,25},{25,17},{2,10},{10... | collective-permute-start | bytes 11010056 | tf_op jit(solution)/shard_map/ppermute | solution.py:42
  248.5 1.6 copy-start.9
  248.6 204.7 %reduce-scatter.5.cloned.1.call-start = ((), (), s32[]{:S(2)}) async-start(), calls=%async_computation.5 | async-start | bytes 4718592 | tf_op jit(solution)/shard_map/reduce_scatter | solution.py:623
  248.6 80.6 %collective-permute-start.10 = (bf16[64,4096]{1,0:T(8,128)(2,1)}, bf16[64,4096]{1,0:T(8,128)(2,1)S(1)}, u32[]{:S(2)}, u32[]{:S(2)}) collective-permute-start(bf16[64,4096]{1,0:T(8,128)(2,1)} %slice.64), channel_id=1, source_target_pairs={{0,16},{8,24},{16,0},{24,8},{1,17},{9,25},{17,1},{25,9},{2,18},{10... | collective-permute-start | bytes 1572872 | tf_op jit(solution)/shard_map/ppermute | solution.py:42
  250.1 79.4 %collective-permute-start.11 = (bf16[64,4096]{1,0:T(8,128)(2,1)S(1)}, bf16[64,4096]{1,0:T(8,128)(2,1)S(1)}, u32[]{:S(2)}, u32[]{:S(2)}) collective-permute-start(bf16[64,4096]{1,0:T(8,128)(2,1)S(1)} %copy-done.9), channel_id=1, source_target_pairs={{0,8},{8,0},{16,24},{24,16},{1,9},{9,1},{17,25},{25,17},{2,10},{10... | collective-permute-start | bytes 1572872 | tf_op jit(solution)/shard_map/ppermute | solution.py:42
  329.2 31.4 %copy-start.7 = (bf16[64,4096]{1,0:T(8,128)(2,1)}, bf16[64,4096]{1,0:T(8,128)(2,1)S(1)}, u32[]{:S(2)}) copy-start(bf16[64,4096]{1,0:T(8,128)(2,1)S(1)} %collective-permute-done.10.refs_5_) | copy-start | bytes 1572868
  329.6 31.0 %copy-start.8 = (bf16[64,4096]{1,0:T(8,128)(2,1)}, bf16[64,4096]{1,0:T(8,128)(2,1)S(1)}, u32[]{:S(2)}) copy-start(bf16[64,4096]{1,0:T(8,128)(2,1)S(1)} %collective-permute-done.11.refs_7_) | copy-start | bytes 1572868
  344.8 41.9 %collective-permute-start.14 = (bf16[224,4096]{1,0:T(8,128)(2,1)}, bf16[224,4096]{1,0:T(8,128)(2,1)S(1)}, u32[]{:S(2)}, u32[]{:S(2)}) collective-permute-start(bf16[224,4096]{1,0:T(8,128)(2,1)} %slice.77), channel_id=1, source_target_pairs={{0,16},{8,24},{16,0},{24,8},{1,17},{9,25},{17,1},{25,9},{2,18},{10... | collective-permute-start | bytes 5505032 | tf_op jit(solution)/shard_map/ppermute | solution.py:42
  346.3 41.7 %collective-permute-start.15 = (bf16[224,4096]{1,0:T(8,128)(2,1)}, bf16[224,4096]{1,0:T(8,128)(2,1)}, u32[]{:S(2)}, u32[]{:S(2)}) collective-permute-start(bf16[224,4096]{1,0:T(8,128)(2,1)} %slice.78), channel_id=1, source_target_pairs={{0,8},{8,0},{16,24},{24,16},{1,9},{9,1},{17,25},{25,17},{2,10},{10... | collective-permute-start | bytes 5505032 | tf_op jit(solution)/shard_map/ppermute | solution.py:42
  386.7 1.3 copy-start.4
  402.9 0.7 copy-start.14
  402.9 0.7 copy-start.15
  404.3 51.6 %copy-start.1 = (bf16[4096,128]{1,0:T(8,128)(2,1)S(1)}, bf16[4096,128]{1,0:T(8,128)(2,1)}, u32[]{:S(2)}) copy-start(bf16[4096,128]{1,0:T(8,128)(2,1)} %param.33) | copy-start | bytes 3145732
Sparse Core Ops, SparseCore 0:
  28.3 33.8 reduce-scatter.2
  248.7 96.1 all-reduce.1
  403.1 50.1 reduce-scatter.4

commit v3 on v2

--- a/solution.py
+++ b/solution.py
@@ -62,22 +62,21 @@
 
 
 def recurrence_kernel(
+    steps,
+    count,
     length_ref,
-    rec_ref,
-    key_ref,
-    val_ref,
-    decay_ref,
-    gate_ref,
-    bias_ref,
-    bonus_ref,
-    gain_ref,
-    start_ref,
-    gated_ref,
-    state_ref,
-    held,
+    base_ref,
+    values_ref,
+    *refs,
 ):
+    rows_far, refs = refs[:count], refs[count:]
+    decay_ref, gate_ref, bias_ref, bonus_ref, gain_ref, start_ref, exit_ref = refs[:7]
+    terms_ref, state_ref, held, projected, gated_ref, total_ref = refs[7:]
+    rec_ref, key_ref, val_ref = (projected.at[m] for m in range(3))
+    for m in range(3):
+        projected[m] = rows_product(base_ref[m], values_ref, m, rows_far)
     length = length_ref[0]
-    tokens = rec_ref.shape[0]
+    tokens = base_ref.shape[1]
     size = min(CHUNK, tokens)
     lanes = lax.broadcasted_iota(jnp.int32, (size, PAIR), 1)
     first_lanes = lanes < GROUP_DIMENSION
@@ -88,7 +87,7 @@
     side_b = lax.broadcasted_iota(jnp.int32, (PAIR, PAIR), 1) < GROUP_DIMENSION
     own_head = side_a == side_b
     average = jnp.where(own_head, 1.0 / GROUP_DIMENSION, 0.0).astype(BF16)
-    pairs_here = rec_ref.shape[1] // PAIR
+    pairs_here = base_ref.shape[2] // PAIR
     for pair in range(pairs_here):
         start = start_ref[2 * pair : 2 * pair + 2].reshape(PAIR, GROUP_DIMENSION)
         start = jnp.where(own_head, jnp.concatenate([start, start], axis=1), 0.0)
@@ -142,38 +141,69 @@
         final = held[pair].T
         final = final[:, :GROUP_DIMENSION] + final[:, GROUP_DIMENSION:]
         state_ref[2 * pair : 2 * pair + 2] = final.reshape(2, GROUP_DIMENSION, GROUP_DIMENSION)
-
-
-def recurrence(length, projected, decay, gate, bias, bonus, gain, start):
+    step = pl.program_id(0)
+    width = exit_ref.shape[1]
+    tile = min(1024, width)
+    for first in range(0, width, tile):
+        columns = slice(first, first + tile)
+        part = matmul(gated_ref[...], exit_ref[:, columns])
+        if steps == 1:
+            terms_ref[:, columns] = part.astype(BF16)
+            continue
+
+        @pl.when(step == 0)
+        def _():
+            total_ref[:, columns] = part
+
+        @pl.when((step > 0) & (step < steps - 1))
+        def _():
+            total_ref[:, columns] += part
+
+        @pl.when(step == steps - 1)
+        def _():
+            terms_ref[:, columns] = (total_ref[:, columns] + part).astype(BF16)
+
+
+def recurrence(length, base, values, far, decay, gate, bias, bonus, gain, start, exit_rows):
     tokens, width = decay.shape
+    out_width = exit_rows.shape[1]
     together = min(2, width // PAIR)
     lanes = together * PAIR
+    steps = width // lanes
+    reach = sum(r.shape[0] * r.shape[2] for r in far) or 128
+    place = values.shape[2] // reach - 1
     wide = pl.BlockSpec((tokens, lanes), lambda p: (0, p))
-    stacked = [
-        pl.BlockSpec((None, tokens, lanes), lambda p, m=m: (m, 0, p)) for m in range(3)
-    ]
     row = pl.BlockSpec((1, lanes), lambda p: (0, p))
     states = pl.BlockSpec((2 * together, GROUP_DIMENSION, GROUP_DIMENSION), lambda p: (p, 0, 0))
     return pl.pallas_call(
-        recurrence_kernel,
-        grid=(width // lanes,),
-        in_specs=[pl.BlockSpec(memory_space=pltpu.SMEM)]
-        + stacked
+        partial(recurrence_kernel, steps, len(far)),
+        grid=(steps,),
+        in_specs=[
+            pl.BlockSpec(memory_space=pltpu.SMEM),
+            pl.BlockSpec((3, tokens, lanes), lambda p: (0, 0, p)),
+            pl.BlockSpec((3, tokens, reach), lambda p: (0, 0, place)),
+        ]
+        + [pl.BlockSpec((*r.shape[:3], lanes), lambda p: (0, 0, 0, p)) for r in far]
         + [wide] * 2
         + [row] * 3
-        + [states],
-        out_specs=[wide, states],
+        + [states, pl.BlockSpec((lanes, out_width), lambda p: (p, 0))],
+        out_specs=[pl.BlockSpec((tokens, out_width), lambda p: (0, 0)), states],
         out_shape=[
-            jax.ShapeDtypeStruct((tokens, width), BF16),
+            jax.ShapeDtypeStruct((tokens, out_width), BF16),
             jax.ShapeDtypeStruct(start.shape, F32),
         ],
-        scratch_shapes=[pltpu.VMEM((together, PAIR, PAIR), F32)],
+        scratch_shapes=[
+            pltpu.VMEM((together, PAIR, PAIR), F32),
+            pltpu.VMEM((3, tokens, lanes), F32),
+            pltpu.VMEM((tokens, lanes), BF16),
+            pltpu.VMEM((tokens, out_width), F32),
+        ],
         compiler_params=pltpu.CompilerParams(vmem_limit_bytes=VMEM_BYTES),
         cost_estimate=pl.CostEstimate(
-            flops=1 << 20, bytes_accessed=18 * MICROSECOND, transcendentals=0
+            flops=1 << 20, bytes_accessed=24 * MICROSECOND, transcendentals=0
         ),
         name="recurrence",
-    )(length, projected, projected, projected, decay, gate, bias, bonus, gain, start)
+    )(length, base, values, *far, decay, gate, bias, bonus, gain, start, exit_rows)
 
 
 def prepare_kernel(
@@ -274,32 +304,30 @@
     )(*pieces)
 
 
-def project_kernel(*refs):
-    values_ref, rows, out_ref = refs[0], refs[1:-1], refs[-1]
-    if len(rows[0].shape) == 3:
-        total, rows = rows[0][0], rows[1:]
-    else:
-        total = 0.0
+def rows_product(total, values_ref, m, rows):
     first = 0
     for rows_ref in rows:
-        block = rows_ref[...]
-        span = block.shape[0] * block.shape[2]
-        values = values_ref[0, :, first : first + span]
-        total = total + matmul(values, block.reshape(span, block.shape[3]))
+        block = rows_ref[:, m]
+        span = block.shape[0] * block.shape[1]
+        values = values_ref[m, :, first : first + span]
+        total = total + matmul(values, block.reshape(span, block.shape[2]))
         first += span
-    out_ref[0] = total
-
-
-def project(values, rows, at, of, base=None):
-    _, tokens, width = values.shape
-    count, wide = rows[0].shape[1], rows[0].shape[3]
+    return total
+
+
+def project_kernel(values_ref, *refs):
+    refs[-1][0] = rows_product(0.0, values_ref, 0, refs[:-1])
+
+
+def project(values, rows):
+    count, tokens, width = values.shape
+    wide = rows[0].shape[-1]
     tile = min(256, wide)
     out = pl.BlockSpec((1, tokens, tile), lambda m, n: (m, 0, n))
     return pl.pallas_call(
         project_kernel,
         grid=(count, wide // tile),
-        in_specs=[pl.BlockSpec((1, tokens, width // of), lambda m, n: (m, 0, at))]
-        + [out] * (base is not None)
+        in_specs=[pl.BlockSpec((1, tokens, width), lambda m, n: (m, 0, 0))]
         + [
             pl.BlockSpec((r.shape[0], 1, r.shape[2], tile), lambda m, n: (0, m, 0, n))
             for r in rows
@@ -308,117 +336,109 @@
         out_shape=jax.ShapeDtypeStruct((count, tokens, wide), F32),
         compiler_params=pltpu.CompilerParams(vmem_limit_bytes=VMEM_BYTES),
         cost_estimate=pl.CostEstimate(
-            flops=2 * count * tokens * width // of * wide,
-            bytes_accessed=30 << 20,
-            transcendentals=0,
+            flops=1 << 20, bytes_accessed=13 * MICROSECOND, transcendentals=0
         ),
         name="project",
-    )(values, *([] if base is None else [base]), *rows)
-
-
-def channel_kernel(
-    length_ref,
-    tokens_ref,
-    attended_ref,
-    gain_ref,
-    first_ref,
-    mix_ref,
-    middle_ref,
-    key_ref,
-    accept_ref,
-    last_ref,
-    held,
-):
+    )(values, *rows)
+
+
+def channel_kernel(places, steps, length_ref, tokens_ref, attended_ref, gain_ref, first_ref, mix_ref, *refs):
+    count = len(places)
+    rows, refs = refs[:count], refs[count:]
+    hidden_ref, accept_ref, last_ref, held, mixed, taken, arrived = refs
     step = pl.program_id(0)
+    copies = [
+        pltpu.make_async_copy(ref, taken.at[pl.ds(first, ref.shape[0]), :], arrived.at[at])
+        for at, (ref, first) in enumerate(zip(rows, places))
+    ]
+
+    @pl.when(step == 0)
+    def _():
+        for copy in copies:
+            copy.start()
+        held[...] = first_ref[...]
+        last_ref[...] = jnp.zeros_like(last_ref)
+
     middle = (tokens_ref[...].astype(F32) + attended_ref[...].astype(F32)).astype(BF16)
-    middle_ref[...] = middle
     values = middle.astype(F32)
     center = values - jnp.mean(values, axis=1, keepdims=True)
     spread = jnp.mean(center * center, axis=1, keepdims=True)
     normed = center * lax.rsqrt(spread + 1e-05) * gain_ref[...]
-    count = normed.shape[0]
-
-    @pl.when(step == 0)
+    tall = normed.shape[0]
+    row_of = lax.broadcasted_iota(jnp.int32, normed.shape, 0)
+    before = jnp.where(row_of == 0, held[...], pltpu.roll(normed, 1, 0))
+    held[...] = normed[tall - 1 :, :]
+    change = before - normed
+    mixed[pl.ds(pl.multiple_of(step * tall, tall), tall), :] = (
+        normed + change * mix_ref[:1, :]
+    ).astype(BF16)
+    accept_ref[...] = (normed + change * mix_ref[1:2, :]).astype(BF16)
+    place = length_ref[0] - 1 - step * tall
+
+    @pl.when((place >= 0) & (place < tall))
     def _():
-        held[...] = first_ref[...]
-        last_ref[...] = jnp.zeros_like(last_ref)
-
-    places = lax.broadcasted_iota(jnp.int32, normed.shape, 0)
-    before = jnp.where(places == 0, held[...], pltpu.roll(normed, 1, 0))
-    held[...] = normed[count - 1 :, :]
-    change = before - normed
-    key_ref[...] = (normed + change * mix_ref[:1, :]).astype(BF16)
-    accept_ref[...] = (normed + change * mix_ref[1:2, :]).astype(BF16)
-    last = places + step * count == length_ref[0] - 1
-    last_ref[...] += jnp.sum(jnp.where(last, normed, 0.0), axis=0, keepdims=True)
-
-
-def channel_inputs(length, tokens, attended, gain, first, mixes):
+        last_ref[...] = jnp.sum(jnp.where(row_of == place, normed, 0.0), axis=0, keepdims=True)
+
+    @pl.when(step == steps - 1)
+    def _():
+        blocks, _, units = hidden_ref.shape
+        ready = 0
+        for at in range(blocks):
+            while ready < count and places[ready] < (at + 1) * units:
+                copies[ready].wait()
+                ready += 1
+            inner = matmul_nt(mixed[...], taken[at * units : (at + 1) * units, :])
+            inner = jnp.maximum(inner, 0.0)
+            hidden_ref[at] = (inner * inner).astype(BF16)
+
+
+def channel_inputs(length, tokens, attended, gain, first, mixes, rows, units):
     seq_len, width = tokens.shape
-    count = min(64, seq_len)
-    tall = pl.BlockSpec((count, width), lambda i: (i, 0))
-
-    def rows(number):
-        return pl.BlockSpec((number, width), lambda i: (0, 0))
-
-    return pl.pallas_call(
-        channel_kernel,
-        grid=(seq_len // count,),
-        in_specs=[pl.BlockSpec(memory_space=pltpu.SMEM), tall, tall, rows(1), rows(1), rows(2)],
-        out_specs=[tall, tall, tall, rows(1)],
-        out_shape=[jax.ShapeDtypeStruct((seq_len, width), BF16)] * 3
-        + [jax.ShapeDtypeStruct((1, width), F32)],
-        scratch_shapes=[pltpu.VMEM((1, width), F32)],
-        compiler_params=pltpu.CompilerParams(vmem_limit_bytes=VMEM_BYTES),
-        cost_estimate=pl.CostEstimate(
-            flops=1 << 20, bytes_accessed=8 * MICROSECOND, transcendentals=0
-        ),
-        name="channel_inputs",
-    )(length, tokens, attended, gain, first, mixes)
-
-
-def entry_kernel(places, *refs):
-    mixed_ref, rows = refs[0], refs[1 : 1 + len(places)]
-    out_ref, held, arrived = refs[1 + len(places) :]
-    count, tokens, units = out_ref.shape
-    copies = [
-        pltpu.make_async_copy(ref, held.at[pl.ds(first, ref.shape[0]), :], arrived.at[at])
-        for at, (ref, first) in enumerate(zip(rows, places))
-    ]
-    for copy in copies:
-        copy.start()
-    ready = 0
-    for at in range(count):
-        while ready < len(places) and places[ready] < (at + 1) * units:
-            copies[ready].wait()
-            ready += 1
-        block = held[at * units : (at + 1) * units, :]
-        inner = jnp.maximum(matmul_nt(mixed_ref[...], block), 0.0)
-        out_ref[at] = (inner * inner).astype(BF16)
-
-
-def entry_product(mixed, rows, units):
-    tokens, width = mixed.shape
+    tall = min(64, seq_len)
+    steps = seq_len // tall
+    by_rows = pl.BlockSpec((tall, width), lambda i: (i, 0))
     places = [0]
     for block in rows:
         places.append(places[-1] + block.shape[0])
-    count = places[-1] // units
+    blocks = places[-1] // units
+
+    def wide(number):
+        return pl.BlockSpec((number, width), lambda i: (0, 0))
+
     return pl.pallas_call(
-        partial(entry_kernel, places[:-1]),
-        in_specs=[pl.BlockSpec(memory_space=pltpu.VMEM)]
+        partial(channel_kernel, places[:-1], steps),
+        grid=(steps,),
+        in_specs=[
+            pl.BlockSpec(memory_space=pltpu.SMEM),
+            by_rows,
+            by_rows,
+            wide(1),
+            wide(1),
+            wide(2),
+        ]
         + [pl.BlockSpec(memory_space=pl.ANY)] * len(rows),
-        out_specs=pl.BlockSpec(memory_space=pltpu.VMEM),
-        out_shape=jax.ShapeDtypeStruct((count, tokens, units), BF16),
+        out_specs=[
+            pl.BlockSpec((blocks, seq_len, units), lambda i: (0, 0, 0)),
+            by_rows,
+            wide(1),
+        ],
+        out_shape=[
+            jax.ShapeDtypeStruct((blocks, seq_len, units), BF16),
+            jax.ShapeDtypeStruct((seq_len, width), BF16),
+            jax.ShapeDtypeStruct((1, width), F32),
+        ],
         scratch_shapes=[
+            pltpu.VMEM((1, width), F32),
+            pltpu.VMEM((seq_len, width), BF16),
             pltpu.VMEM((places[-1], width), BF16),
             pltpu.SemaphoreType.DMA((len(rows),)),
         ],
         compiler_params=pltpu.CompilerParams(vmem_limit_bytes=VMEM_BYTES),
         cost_estimate=pl.CostEstimate(
-            flops=1 << 20, bytes_accessed=15 * MICROSECOND, transcendentals=0
-        ),
-        name="entry_product",
-    )(mixed, *rows)
+            flops=1 << 20, bytes_accessed=22 * MICROSECOND, transcendentals=0
+        ),
+        name="channel_inputs",
+    )(length, tokens, attended, gain, first, mixes, *rows)
 
 
 def exit_kernel(hidden_ref, *refs):
@@ -452,16 +472,17 @@
     )(hidden, *values)
 
 
-def combine_kernel(slot_ref, length_ref, middle_ref, gate_ref, *refs):
+def combine_kernel(slot_ref, length_ref, tokens_ref, attended_ref, gate_ref, *refs):
     out_ref = refs[-1]
     present = lax.broadcasted_iota(jnp.int32, gate_ref.shape, 0) < length_ref[0]
     summed = jnp.concatenate([ref[...] for ref in refs[:-1]], axis=1).astype(F32)
     accept = 1.0 / (1.0 + jnp.exp(-gate_ref[...]))
-    combined = middle_ref[...].astype(F32) + accept * summed
+    middle = (tokens_ref[...].astype(F32) + attended_ref[...].astype(F32)).astype(BF16)
+    combined = middle.astype(F32) + accept * summed
     out_ref[...] = jnp.where(present, combined, 0.0).astype(BF16)
 
 
-def combine(slot, length, middle, gate, summed):
+def combine(slot, length, tokens, attended, gate, summed):
     seq_len, wide = gate.shape
     whole = pl.BlockSpec((seq_len, wide), lambda i, *_: (0, 0))
     parts = [pl.BlockSpec(part.shape, lambda i, *_: (0, 0)) for part in summed]
@@ -470,7 +491,8 @@
         grid_spec=pltpu.PrefetchScalarGridSpec(
             num_scalar_prefetch=2,
             grid=(1,),
-            in_specs=[pl.BlockSpec((seq_len, wide), lambda i, slot, *_: (0, slot[0])), whole]
+            in_specs=[pl.BlockSpec((seq_len, wide), lambda i, slot, *_: (0, slot[0]))] * 2
+            + [whole]
             + parts,
             out_specs=whole,
         ),
@@ -480,7 +502,7 @@
             flops=1 << 20, bytes_accessed=3 * MICROSECOND, transcendentals=0
         ),
         name="combine",
-    )(slot, length, middle, gate, *summed)
+    )(slot, length, tokens, attended, gate, *summed)
 
 
 def local(
@@ -580,48 +602,60 @@
         second = [key_x[cut:half], key_y[half + cut :]]
         trained, first, second = hold((trained, first, second))
         opposite = [across(trained[1][0], 2), across(trained[2][1], 1)]
-        projected = project(blended, sum(trained, []), 0, 1)
+        projected = project(blended, sum(trained, []))
         projected, opposite, first = hold((projected, opposite, first))
         key_far = [across(first[0], 2), across(first[1], 1)]
-        projected = project(blended, opposite, 3, 4, projected)
     else:
         decay, gate = side_products(decay_in, gate_in)
         low, high = [whole(side, req) for side in to_heads(columns)]
-        projected = project(blended, [side[d] for d in range(req) for side in (low, high)], 0, 1)
-    gated, new_state = recurrence(
+        opposite = []
+        projected = project(blended, [side[d] for d in range(req) for side in (low, high)])
+    head_terms, new_state = recurrence(
         prompt_extents,
         projected,
+        blended,
+        opposite,
         decay,
         gate,
         forgetting_bias_vector[None],
         instant_emphasis[None],
         group_normalizer_scale[None],
         start,
+        mixing_exit_projection,
     )
     if req == 4:
-        gated, value_mine, second, key_far = hold((gated, value_mine, second, key_far))
-    head_terms = matmul(gated, mixing_exit_projection).astype(BF16)
+        head_terms, value_mine, second, key_far = hold(
+            (head_terms, value_mine, second, key_far)
+        )
     attended = lax.psum(head_terms, "hid")
     if req == 4:
         value_x, value_y = across(value_mine, 1), across(value_mine, 2)
         key_far.insert(1, across(second[0], 2))
         key_far.append(across(second[1], 1))
         value_far = [value_x[:half], value_y[half:]]
-        attended, key_far, value_far = hold((attended, key_far, value_far))
+        value_far, key_far = hold((value_far, key_far))
         value_far = [across(value_far[0], 2), across(value_far[1], 1)]
         key_rows = [key_mine, key_x, key_y, *key_far]
         value_rows = [value_mine, value_x, value_y, *value_far]
     else:
         key_rows = whole(feedforward_entry_proj, req)
         value_rows = whole(feedforward_exit_proj, req)
-    middle, mixed_key, mixed_accept, last_chan = channel_inputs(
-        prompt_extents, token_rows, attended, gain_rows[1:], carried[1:], mix_rows[5:]
-    )
-    accept = matmul(mixed_accept, feedforward_accept_proj)
-    hidden = entry_product(mixed_key, key_rows, units)
+    hidden, accept_in, last_chan = channel_inputs(
+        prompt_extents,
+        token_rows,
+        attended,
+        gain_rows[1:],
+        carried[1:],
+        mix_rows[5:],
+        key_rows,
+        units,
+    )
+    accept = matmul(accept_in, feedforward_accept_proj)
     terms = exit_product(hidden, value_rows)
     summed = lax.psum_scatter(terms, "hid", scatter_dimension=1, tiled=True)
-    layer_out = combine(slot[None], prompt_extents, middle, accept, [summed])[None]
+    layer_out = combine(
+        slot[None], prompt_extents, token_rows, attended, accept, [summed]
+    )[None]
     shift_out = jnp.concatenate([last_in, last_chan]).astype(BF16)[None]
     return (layer_out, new_state[None], shift_out)
 

time: 464 us -> 448 us (0.966)
  waiting for transfers between devices: 253 us -> 242 us
  matrix products: 25.2 us -> 18.6 us
    pallas_call x3 -> x2, Pallas kernels: 46.2 us -> 56.1 us  [the longest x1 30 us: recurrence(): pl.pallas_call(partial(recurrence_kernel, steps, len(far)), grid=(steps,)...]
    psum x1, waiting for transfers between devices: 15.3 us -> 6.16 us  [local(): attended = lax.psum(head_terms, 'hid')]
    pallas_call x2 -> x1, Pallas kernels: 21.5 us -> 13.5 us  [project(): pl.pallas_call(project_kernel, grid=(count, wide // tile), in_specs=[pl.B...]
    dot_general x4 -> x3, matrix products: 25.2 us -> 18.6 us  [matmul(): return jnp.dot(a, b, preferred_element_type=F32)]
  transfers between devices with their start and end apart: 20 -> 20, of which waited for: 16 -> 13; matrix products, arithmetic and copies ran while one was open for 11% -> 10% of each run, Pallas kernels for 20% -> 21%
where the time goes in v3:
time: 448 us; the launch traced here: 447 us
  waiting for transfers between devices  242 us (54%)
  Pallas kernels  120 us (27%)
  local copies, waits for them, and re-layouts  23.6 us (5%)
  starting transfers between devices  23.3 us (5%)
  matrix products  18.6 us (4%)
  between operations  15.9 us (4%)
    ppermute x16, waiting for transfers between devices, across(): return lax.ppermute(value, 'req', [(i, i ^ axis) for i in range(4)])  169 us
    reduce_scatter x1, waiting for transfers between devices, local(): summed = lax.psum_scatter(terms, 'hid', scatter_dimension=1, tiled=True)  40.4 us
    pallas_call x1, Pallas kernels, recurrence(): pl.pallas_call(partial(recurrence_kernel, steps, len(far)), grid=(steps,)...  30 us
    all_to_all x1, waiting for transfers between devices, to_heads(): lax.all_to_all(columns, 'hid', split_axis=0, concat_axis=0, tiled=True)  26.5 us
    pallas_call x1, Pallas kernels, channel_inputs(): pl.pallas_call(partial(channel_kernel, places[:-1], steps), grid=(steps,)...  26 us
    pallas_call x1, Pallas kernels, prepare(): pl.pallas_call(prepare_kernel, grid_spec=pltpu.PrefetchScalarGridSpec(num...  25.4 us
    dot_general x3, matrix products, matmul(): return jnp.dot(a, b, preferred_element_type=F32)  18.6 us
    ppermute x16, starting transfers between devices, across(): return lax.ppermute(value, 'req', [(i, i ^ axis) for i in range(4)])  16.8 us
  transfers between devices with their start and end apart: 20, of which 13 were waited for; matrix products, arithmetic and copies ran while one was open for 10% of the time, Pallas kernels for 21%

profile of v3, /device:TPU:0, one launch (start us, length us, event | category | flops | bytes accessed | tf_op | source)
XLA Modules:
  0.0 446.5 jit_solution(12484562325546798696)
XLA Ops:
  7.2 6.8 %regroup.1 = bf16[8,384,512]{2,1,0:T(8,128)(2,1)} custom-call(f32[128,4096]{1,0:T(8,128)} %refs_0_.2, f32[128,4096]{1,0:T(8,128)} %refs_1_.1, f32[128,4096]{1,0:T(8,128)} %refs_2_.1), custom_call_target="tpu_custom_call" | custom-call | bytes 20971520 | tf_op jit(solution)/shard_map/regroup/pallas_call | solution.py:295
  14.0 6.3 %all-to-all-start = ((bf16[8,384,512]{2,1,0:T(8,128)(2,1)}), bf16[8,384,512]{2,1,0:T(8,128)(2,1)}, u32[]{:S(2)}, u32[]{:S(2)}) async-start(bf16[8,384,512]{2,1,0:T(8,128)(2,1)} %regroup.1), calls=%async_computation | async-start | bytes 6291456 | tf_op jit(solution)/shard_map/all_to_all | solution.py:581
  20.4 1.6 collective-permute-start
  22.0 1.5 collective-permute-start.1
  24.8 1.7 convert_select_fusion
  26.5 1.6 select_n.41
  31.6 25.4 %prepare.1 = (bf16[3,512,4096]{2,1,0:T(8,128)(2,1)}, bf16[512,4096]{1,0:T(8,128)(2,1)}, bf16[512,4096]{1,0:T(8,128)(2,1)}, f32[1,4096]{1,0:T(1,128)}) custom-call(s32[32]{0:T(128)} %pad_add_fusion.order_ref, s32[1]{0:T(128)S(6)} %copy.26.length_ref, bf16[512,4096]{1,0:T(8,128)(2,1)} %bitcast.29, f32[1,4096]{1,0:T(1,128)} %get-tuple-element.96.gain_ref, ...), custom_call_target="tpu_custom_call" | custom-call | flops 1048576 | bytes 81180000 | tf_op jit(solution)/shard_map/prepare/pallas_call | solution.py:262
  57.0 4.9 %fusion.1.refs_2_ = f32[512,512]{1,0:T(8,128)} fusion(bf16[128,512]{1,0:T(8,128)(2,1)S(1)} %copy-done.12, bf16[512,4096]{1,0:T(8,128)(2,1)} %get-tuple-element.48, bf16[4096,128]{1,0:T(8,128)(2,1)S(1)} %copy-done), kind=kOutput, calls=%fused_computation.2 | convolution fusion | flops 604045312 | bytes 6422528 | tf_op jit(solution)/shard_map/dot_general | solution.py:30
  61.9 6.8 %fusion.5.refs_3_ = f32[512,512]{1,0:T(8,128)} fusion(bf16[512,4096]{1,0:T(8,128)(2,1)} %get-tuple-element.49, bf16[4096,512]{1,0:T(8,128)(2,1)} %param.37), kind=kOutput, calls=%fused_computation.14 | convolution fusion | flops 2147483648 | bytes 9437184 | tf_op jit(solution)/shard_map/dot_general | solution.py:30
  68.7 1.7 reshape.63.refs_7_
  70.4 26.5 %all-to-all-done = bf16[8,384,512]{2,1,0:T(8,128)(2,1)} async-done(((bf16[8,384,512]{2,1,0:T(8,128)(2,1)}), bf16[8,384,512]{2,1,0:T(8,128)(2,1)}, u32[]{:S(2)}, u32[]{:S(2)}) %all-to-all-start) | async-done | bytes 3145760 | tf_op jit(solution)/shard_map/all_to_all | solution.py:581
  96.9 2.1 fusion.2
  99.0 3.5 collective-permute-done.refs_1_
  102.5 1.2 collective-permute-done.1.refs_2_
  104.3 1.5 collective-permute-start.3
  105.8 1.5 collective-permute-start.4
  107.8 2.5 slice.62
  110.3 1.9 slice.64
  112.2 1.4 slice.63
  113.6 1.9 slice.65
  115.5 25.6 %collective-permute-done.2.refs_2_ = bf16[4,3,128,512]{3,2,1,0:T(8,128)(2,1)S(1)} collective-permute-done((bf16[4,3,128,512]{3,2,1,0:T(8,128)(2,1)S(1)}, bf16[4,3,128,512]{3,2,1,0:T(8,128)(2,1)S(1)}, u32[]{:S(2)}, u32[]{:S(2)}) %collective-permute-start.2) | collective-permute-done | bytes 1572896 | tf_op jit(solution)/shard_map/ppermute | solution.py:42
  141.1 32.1 %collective-permute-done.3.refs_3_ = bf16[4,3,128,512]{3,2,1,0:T(8,128)(2,1)S(1)} collective-permute-done((bf16[4,3,128,512]{3,2,1,0:T(8,128)(2,1)S(1)}, bf16[4,3,128,512]{3,2,1,0:T(8,128)(2,1)S(1)}, u32[]{:S(2)}, u32[]{:S(2)}) %collective-permute-start.3) | collective-permute-done | bytes 1572896 | tf_op jit(solution)/shard_map/ppermute | solution.py:42
  173.2 1.6 collective-permute-done.5.refs_5_
  174.7 1.5 collective-permute-start.6
  176.9 13.5 %project.1.base_ref = f32[3,512,512]{2,1,0:T(8,128)} custom-call(bf16[3,512,4096]{2,1,0:T(8,128)(2,1)} %get-tuple-element.50.values_ref, bf16[4,3,128,512]{3,2,1,0:T(8,128)(2,1)} %bitcast.37, bf16[4,3,128,512]{3,2,1,0:T(8,128)(2,1)} %bitcast.34, bf16[4,3,128,512]{3,2,1,0:T(8,128)(2,1)} %copy-done.5, bf16[4,3,128,512]{3,2,1,0:T(8,128)(2,1)} %copy-done.6, ...), custom_call_target="tpu_custom_call" | custom-call | flops 1048576 | bytes 47970000 | tf_op jit(solution)/shard_map/project/pallas_call | solution.py:327
  190.4 18.9 %collective-permute-done.6.refs_0_ = bf16[4,3,128,512]{3,2,1,0:T(8,128)(2,1)} collective-permute-done((bf16[4,3,128,512]{3,2,1,0:T(8,128)(2,1)S(1)}, bf16[4,3,128,512]{3,2,1,0:T(8,128)(2,1)}, u32[]{:S(2)}, u32[]{:S(2)}) %collective-permute-start.6) | collective-permute-done | bytes 1572896 | tf_op jit(solution)/shard_map/ppermute | solution.py:42
  209.3 1.5 collective-permute-done.7.refs_1_
  210.7 0.8 collective-permute-start.8
  211.6 0.7 collective-permute-start.9
  212.2 30.0 %recurrence.1 = (bf16[512,4096]{1,0:T(8,128)(2,1)}, f32[8,64,64]{2,1,0:T(8,128)}) custom-call(s32[1]{0:T(128)S(6)} %copy.26.length_ref, f32[3,512,512]{2,1,0:T(8,128)} %project.1.base_ref, bf16[3,512,4096]{2,1,0:T(8,128)(2,1)} %get-tuple-element.50.values_ref, bf16[4,3,128,512]{3,2,1,0:T(8,128)(2,1)} %collective-permute-done.6.refs_0_, ...), custom_call_target="tpu_custom_call" | custom-call | flops 1048576 | bytes 88560000 | tf_op jit(solution)/shard_map/recurrence/pallas_call | solution.py:178
  242.3 1.4 collective-permute-start.10
  243.7 1.2 collective-permute-start.11
  244.9 0.8 collective-permute-start.12
  245.7 0.7 collective-permute-start.13
  246.5 78.5 %collective-permute-done.10.refs_1_ = bf16[448,4096]{1,0:T(8,128)(2,1)} collective-permute-done((bf16[448,4096]{1,0:T(8,128)(2,1)}, bf16[448,4096]{1,0:T(8,128)(2,1)}, u32[]{:S(2)}, u32[]{:S(2)}) %collective-permute-start.10) | collective-permute-done | bytes 3670048 | tf_op jit(solution)/shard_map/ppermute | solution.py:42
  325.0 3.0 slice.80
  327.9 3.0 slice.81
  330.9 3.4 collective-permute-done.12.refs_4_
  334.3 1.2 collective-permute-start.14
  336.8 6.2 %all-reduce.2.cloned.1.call-done.attended_ref = bf16[512,4096]{1,0:T(8,128)(2,1)} async-done(((bf16[512,4096]{1,0:T(8,128)(2,1)}), bf16[512,4096]{1,0:T(8,128)(2,1)}) %all-reduce.2.cloned.1.call-update) | async-done | bytes 4194320 | tf_op jit(solution)/shard_map/psum | solution.py:630
  343.0 26.0 %channel_inputs.1 = (bf16[4,512,448]{2,1,0:T(8,128)(2,1)}, bf16[512,4096]{1,0:T(8,128)(2,1)}, f32[1,4096]{1,0:T(1,128)}) custom-call(s32[1]{0:T(128)S(6)} %copy.26.length_ref, bf16[512,4096]{1,0:T(8,128)(2,1)} %bitcast.30, bf16[512,4096]{1,0:T(8,128)(2,1)} %all-reduce.2.cloned.1.call-done.attended_ref, f32[1,4096]{1,0:T(1,128)} %get-tuple-element.95.gain_ref, ...), custom_call_target="tpu_custom_call" | custom-call | flops 1048576 | bytes 81180000 | tf_op jit(solution)/shard_map/channel_inputs/pallas_call | solution.py:408
  369.0 3.1 collective-permute-done.14.refs_3_
  372.2 1.2 copy-done.4
  373.4 14.8 %exit_product.1 = bf16[512,4096]{1,0:T(8,128)(2,1)} custom-call(bf16[4,512,448]{2,1,0:T(8,128)(2,1)} %get-tuple-element.85.hidden_ref, bf16[448,4096]{1,0:T(8,128)(2,1)} %refs_0_.4, bf16[448,4096]{1,0:T(8,128)(2,1)} %collective-permute-done.10.refs_1_, bf16[448,4096]{1,0:T(8,128)(2,1)} %collective-permute-done.11.refs_2_, bf16[224,4096]{1,0:T(8,128)(2,1)} %copy-done.4, ...), custom_call_target="tpu_custom_call" | custom-call | flops 1048576 | bytes 25830000 | tf_op jit(solution)/shard_map/exit_product/pallas_call | solution.py:460
  388.2 0.7 copy-done.15
  389.6 6.9 %fusion.6.gate_ref = f32[512,512]{1,0:T(8,128)} fusion(bf16[512,4096]{1,0:T(8,128)(2,1)} %get-tuple-element.84, bf16[4096,512]{1,0:T(8,128)(2,1)} %param.43), kind=kOutput, calls=%fused_computation.15 | convolution fusion | flops 2147483648 | bytes 9437184 | tf_op jit(solution)/shard_map/dot_general | solution.py:30
  396.5 40.4 %reduce-scatter.5.cloned.1.call-done.refs_0_ = bf16[512,512]{1,0:T(8,128)(2,1)} async-done(((bf16[512,4096]{1,0:T(8,128)(2,1)}), bf16[512,512]{1,0:T(8,128)(2,1)}) %reduce-scatter.5.cloned.1.call-update) | async-done | bytes 524304 | tf_op jit(solution)/shard_map/reduce_scatter | solution.py:655
  436.9 3.1 combine.1
  (61 shorter events, 6.6 us)
Async XLA Ops:
  7.2 49.9 %copy-start = (bf16[4096,128]{1,0:T(8,128)(2,1)S(1)}, bf16[4096,128]{1,0:T(8,128)(2,1)}, u32[]{:S(2)}) copy-start(bf16[4096,128]{1,0:T(8,128)(2,1)} %param.33) | copy-start | bytes 3145732
  14.0 82.9 %all-to-all-start = ((bf16[8,384,512]{2,1,0:T(8,128)(2,1)}), bf16[8,384,512]{2,1,0:T(8,128)(2,1)}, u32[]{:S(2)}, u32[]{:S(2)}) async-start(bf16[8,384,512]{2,1,0:T(8,128)(2,1)} %regroup.1), calls=%async_computation | async-start | bytes 6291456 | tf_op jit(solution)/shard_map/all_to_all | solution.py:581
  20.3 7.9 %copy-start.14 = (bf16[1,2,4096]{2,1,0:T(2,128)(2,1)S(1)}, bf16[1,2,4096]{2,1,0:T(2,128)(2,1)}, u32[]{:S(2)}) copy-start(bf16[1,2,4096]{2,1,0:T(2,128)(2,1)} %param.40) | copy-start | bytes 49156
  20.4 8.6 %copy-start.11 = (bf16[7,4096]{1,0:T(8,128)(2,1)S(1)}, bf16[7,4096]{1,0:T(8,128)(2,1)}, u32[]{:S(2)}) copy-start(bf16[7,4096]{1,0:T(8,128)(2,1)} %param.31) | copy-start | bytes 172036
  20.4 9.2 %copy-start.17 = (s32[32]{0:T(128)S(1)}, s32[32]{0:T(128)}, u32[]{:S(2)}) copy-start(s32[32]{0:T(128)} %param.26) | copy-start | bytes 388
  20.4 10.0 %copy-start.13 = (bf16[2,4096]{1,0:T(2,128)(2,1)S(1)}, bf16[2,4096]{1,0:T(2,128)(2,1)}, u32[]{:S(2)}) copy-start(bf16[2,4096]{1,0:T(2,128)(2,1)} %param.30) | copy-start | bytes 49156
  20.4 48.3 %reduce-scatter.3.cloned.1.call-start = ((), (), s32[]{:S(2)}) async-start(), calls=%async_computation.3 | async-start | bytes 589824 | tf_op jit(solution)/shard_map/reduce_scatter | solution.py:547
  20.4 82.1 %collective-permute-start = (bf16[448,4096]{1,0:T(8,128)(2,1)}, bf16[448,4096]{1,0:T(8,128)(2,1)}, u32[]{:S(2)}, u32[]{:S(2)}) collective-permute-start(bf16[448,4096]{1,0:T(8,128)(2,1)} %refs_0_.3), channel_id=1, source_target_pairs={{0,8},{8,0},{16,24},{24,16},{1,9},{9,1},{17,25},{25,17},{2,10},{10... | collective-permute-start | bytes 11010056 | tf_op jit(solution)/shard_map/ppermute | solution.py:42
  22.0 81.8 %collective-permute-start.1 = (bf16[448,4096]{1,0:T(8,128)(2,1)}, bf16[448,4096]{1,0:T(8,128)(2,1)}, u32[]{:S(2)}, u32[]{:S(2)}) collective-permute-start(bf16[448,4096]{1,0:T(8,128)(2,1)} %refs_0_.3), channel_id=1, source_target_pairs={{0,16},{8,24},{16,0},{24,8},{1,17},{9,25},{17,1},{25,9},{2,18},{10... | collective-permute-start | bytes 11010056 | tf_op jit(solution)/shard_map/ppermute | solution.py:42
  26.5 30.5 %copy-start.12 = (bf16[128,512]{1,0:T(8,128)(2,1)S(1)}, bf16[128,512]{1,0:T(8,128)(2,1)}, u32[]{:S(2)}) copy-start(bf16[128,512]{1,0:T(8,128)(2,1)} %param.34) | copy-start | bytes 393220
  28.2 314.8 %all-reduce.2.cloned.1.call-start = ((), (), s32[]{:S(2)}) async-start(), calls=%async_computation.4 | async-start | bytes 8388608 | tf_op jit(solution)/shard_map/psum | solution.py:630
  99.0 16.5 %copy-start.2 = (bf16[4,384,512]{2,1,0:T(8,128)(2,1)}, bf16[4,384,512]{2,1,0:T(8,128)(2,1)S(1)}, u32[]{:S(2)}) copy-start(bf16[4,384,512]{2,1,0:T(8,128)(2,1)S(1)} %get-tuple-element.91) | copy-start | bytes 4718596
  99.0 16.5 %copy-start.3 = (bf16[4,384,512]{2,1,0:T(8,128)(2,1)}, bf16[4,384,512]{2,1,0:T(8,128)(2,1)S(1)}, u32[]{:S(2)}) copy-start(bf16[4,384,512]{2,1,0:T(8,128)(2,1)S(1)} %get-tuple-element.92) | copy-start | bytes 4718596
  103.8 37.3 %collective-permute-start.2 = (bf16[4,3,128,512]{3,2,1,0:T(8,128)(2,1)S(1)}, bf16[4,3,128,512]{3,2,1,0:T(8,128)(2,1)S(1)}, u32[]{:S(2)}, u32[]{:S(2)}) collective-permute-start(bf16[4,3,128,512]{3,2,1,0:T(8,128)(2,1)S(1)} %bitcast.35), channel_id=1, source_target_pairs={{0,8},{8,0},{16,24},{24,16},{1,9},{9,1},{17,25},{25,17},{2,10},{10... | collective-permute-start | bytes 4718600 | tf_op jit(solution)/shard_map/ppermute | solution.py:42
  104.3 68.9 %collective-permute-start.3 = (bf16[4,3,128,512]{3,2,1,0:T(8,128)(2,1)S(1)}, bf16[4,3,128,512]{3,2,1,0:T(8,128)(2,1)S(1)}, u32[]{:S(2)}, u32[]{:S(2)}) collective-permute-start(bf16[4,3,128,512]{3,2,1,0:T(8,128)(2,1)S(1)} %bitcast.32), channel_id=1, source_target_pairs={{0,8},{8,0},{16,24},{24,16},{1,9},{9,1},{17,25},{25,17},{2,10},{10... | collective-permute-start | bytes 4718600 | tf_op jit(solution)/shard_map/ppermute | solution.py:42
  105.8 67.4 %collective-permute-start.4 = (bf16[4,3,128,512]{3,2,1,0:T(8,128)(2,1)S(1)}, bf16[4,3,128,512]{3,2,1,0:T(8,128)(2,1)S(1)}, u32[]{:S(2)}, u32[]{:S(2)}) collective-permute-start(bf16[4,3,128,512]{3,2,1,0:T(8,128)(2,1)S(1)} %bitcast.36), channel_id=1, source_target_pairs={{0,16},{8,24},{16,0},{24,8},{1,17},{9,25},{17,1},{25,9},{2,18},{10... | collective-permute-start | bytes 4718600 | tf_op jit(solution)/shard_map/ppermute | solution.py:42
  107.3 67.4 %collective-permute-start.5 = (bf16[4,3,128,512]{3,2,1,0:T(8,128)(2,1)S(1)}, bf16[4,3,128,512]{3,2,1,0:T(8,128)(2,1)}, u32[]{:S(2)}, u32[]{:S(2)}) collective-permute-start(bf16[4,3,128,512]{3,2,1,0:T(8,128)(2,1)S(1)} %bitcast.33), channel_id=1, source_target_pairs={{0,16},{8,24},{16,0},{24,8},{1,17},{9,25},{17,1},{25,9},{2,18},{10... | collective-permute-start | bytes 4718600 | tf_op jit(solution)/shard_map/ppermute | solution.py:42
  141.1 35.8 %copy-start.5 = (bf16[4,3,128,512]{3,2,1,0:T(8,128)(2,1)}, bf16[4,3,128,512]{3,2,1,0:T(8,128)(2,1)S(1)}, u32[]{:S(2)}) copy-start(bf16[4,3,128,512]{3,2,1,0:T(8,128)(2,1)S(1)} %collective-permute-done.2.refs_2_) | copy-start | bytes 4718596
  173.2 1.6 copy-start.6
  173.2 3.1 copy-start.7
  174.7 34.5 %collective-permute-start.6 = (bf16[4,3,128,512]{3,2,1,0:T(8,128)(2,1)S(1)}, bf16[4,3,128,512]{3,2,1,0:T(8,128)(2,1)}, u32[]{:S(2)}, u32[]{:S(2)}) collective-permute-start(bf16[4,3,128,512]{3,2,1,0:T(8,128)(2,1)S(1)} %collective-permute-done.2.refs_2_), channel_id=1, source_target_pairs={{0,16},{8,24},{16,0},{24,8},{1,17},{9,25},{17,1},{25,9},{2,18},{10... | collective-permute-start | bytes 4718600 | tf_op jit(solution)/shard_map/ppermute | solution.py:42
  176.3 34.5 %collective-permute-start.7 = (bf16[4,3,128,512]{3,2,1,0:T(8,128)(2,1)}, bf16[4,3,128,512]{3,2,1,0:T(8,128)(2,1)}, u32[]{:S(2)}, u32[]{:S(2)}) collective-permute-start(bf16[4,3,128,512]{3,2,1,0:T(8,128)(2,1)} %collective-permute-done.5.refs_5_), channel_id=1, source_target_pairs={{0,8},{8,0},{16,24},{24,16},{1,9},{9,1},{17,25},{25,17},{2,10},{10... | collective-permute-start | bytes 4718600 | tf_op jit(solution)/shard_map/ppermute | solution.py:42
  210.7 31.6 %collective-permute-start.8 = (bf16[160,4096]{1,0:T(8,128)(2,1)}, bf16[160,4096]{1,0:T(8,128)(2,1)}, u32[]{:S(2)}, u32[]{:S(2)}) collective-permute-start(bf16[160,4096]{1,0:T(8,128)(2,1)} %slice.62), channel_id=1, source_target_pairs={{0,16},{8,24},{16,0},{24,8},{1,17},{9,25},{17,1},{25,9},{2,18},{10... | collective-permute-start | bytes 3932168 | tf_op jit(solution)/shard_map/ppermute | solution.py:42
  211.6 30.7 %collective-permute-start.9 = (bf16[160,4096]{1,0:T(8,128)(2,1)S(1)}, bf16[160,4096]{1,0:T(8,128)(2,1)}, u32[]{:S(2)}, u32[]{:S(2)}) collective-permute-start(bf16[160,4096]{1,0:T(8,128)(2,1)S(1)} %slice.63), channel_id=1, source_target_pairs={{0,8},{8,0},{16,24},{24,16},{1,9},{9,1},{17,25},{25,17},{2,10},{10... | collective-permute-start | bytes 3932168 | tf_op jit(solution)/shard_map/ppermute | solution.py:42
  212.2 33.5 %copy-start.10 = (bf16[64,4096]{1,0:T(8,128)(2,1)S(1)}, bf16[64,4096]{1,0:T(8,128)(2,1)}, u32[]{:S(2)}) copy-start(bf16[64,4096]{1,0:T(8,128)(2,1)} %slice.65) | copy-start | bytes 1572868
  242.3 82.7 %collective-permute-start.10 = (bf16[448,4096]{1,0:T(8,128)(2,1)}, bf16[448,4096]{1,0:T(8,128)(2,1)}, u32[]{:S(2)}, u32[]{:S(2)}) collective-permute-start(bf16[448,4096]{1,0:T(8,128)(2,1)} %refs_0_.4), channel_id=1, source_target_pairs={{0,8},{8,0},{16,24},{24,16},{1,9},{9,1},{17,25},{25,17},{2,10},{10... | collective-permute-start | bytes 11010056 | tf_op jit(solution)/shard_map/ppermute | solution.py:42
  243.7 84.2 %collective-permute-start.11 = (bf16[448,4096]{1,0:T(8,128)(2,1)}, bf16[448,4096]{1,0:T(8,128)(2,1)}, u32[]{:S(2)}, u32[]{:S(2)}) collective-permute-start(bf16[448,4096]{1,0:T(8,128)(2,1)} %refs_0_.4), channel_id=1, source_target_pairs={{0,16},{8,24},{16,0},{24,8},{1,17},{9,25},{17,1},{25,9},{2,18},{10... | collective-permute-start | bytes 11010056 | tf_op jit(solution)/shard_map/ppermute | solution.py:42
  244.9 89.4 %collective-permute-start.12 = (bf16[64,4096]{1,0:T(8,128)(2,1)}, bf16[64,4096]{1,0:T(8,128)(2,1)S(1)}, u32[]{:S(2)}, u32[]{:S(2)}) collective-permute-start(bf16[64,4096]{1,0:T(8,128)(2,1)} %slice.64), channel_id=1, source_target_pairs={{0,16},{8,24},{16,0},{24,8},{1,17},{9,25},{17,1},{25,9},{2,18},{10... | collective-permute-start | bytes 1572872 | tf_op jit(solution)/shard_map/ppermute | solution.py:42
  245.7 88.5 %collective-permute-start.13 = (bf16[64,4096]{1,0:T(8,128)(2,1)S(1)}, bf16[64,4096]{1,0:T(8,128)(2,1)S(1)}, u32[]{:S(2)}, u32[]{:S(2)}) collective-permute-start(bf16[64,4096]{1,0:T(8,128)(2,1)S(1)} %copy-done.10), channel_id=1, source_target_pairs={{0,8},{8,0},{16,24},{24,16},{1,9},{9,1},{17,25},{25,17},{2,10},{10... | collective-permute-start | bytes 1572872 | tf_op jit(solution)/shard_map/ppermute | solution.py:42
  246.4 190.5 %reduce-scatter.5.cloned.1.call-start = ((), (), s32[]{:S(2)}) async-start(), calls=%async_computation.5 | async-start | bytes 4718592 | tf_op jit(solution)/shard_map/reduce_scatter | solution.py:655
  334.3 8.7 %copy-start.8 = (bf16[64,4096]{1,0:T(8,128)(2,1)}, bf16[64,4096]{1,0:T(8,128)(2,1)S(1)}, u32[]{:S(2)}) copy-start(bf16[64,4096]{1,0:T(8,128)(2,1)S(1)} %collective-permute-done.12.refs_4_) | copy-start | bytes 1572868
  334.3 8.7 %copy-start.9 = (bf16[64,4096]{1,0:T(8,128)(2,1)}, bf16[64,4096]{1,0:T(8,128)(2,1)S(1)}, u32[]{:S(2)}) copy-start(bf16[64,4096]{1,0:T(8,128)(2,1)S(1)} %collective-permute-done.13.refs_6_) | copy-start | bytes 1572868
  334.3 37.9 %collective-permute-start.14 = (bf16[224,4096]{1,0:T(8,128)(2,1)}, bf16[224,4096]{1,0:T(8,128)(2,1)S(1)}, u32[]{:S(2)}, u32[]{:S(2)}) collective-permute-start(bf16[224,4096]{1,0:T(8,128)(2,1)} %slice.80), channel_id=1, source_target_pairs={{0,16},{8,24},{16,0},{24,8},{1,17},{9,25},{17,1},{25,9},{2,18},{10... | collective-permute-start | bytes 5505032 | tf_op jit(solution)/shard_map/ppermute | solution.py:42
  335.5 36.6 %collective-permute-start.15 = (bf16[224,4096]{1,0:T(8,128)(2,1)}, bf16[224,4096]{1,0:T(8,128)(2,1)}, u32[]{:S(2)}, u32[]{:S(2)}) collective-permute-start(bf16[224,4096]{1,0:T(8,128)(2,1)} %slice.81), channel_id=1, source_target_pairs={{0,8},{8,0},{16,24},{24,16},{1,9},{9,1},{17,25},{25,17},{2,10},{10... | collective-permute-start | bytes 5505032 | tf_op jit(solution)/shard_map/ppermute | solution.py:42
  372.1 1.2 copy-start.4
  388.2 0.7 copy-start.15
  388.2 0.7 copy-start.16
  436.9 3.1 copy-start.1
Sparse Core Ops, SparseCore 0:
  28.3 33.8 reduce-scatter.2
  246.6 96.3 all-reduce.1
  388.3 48.5 reduce-scatter.4

commit v4 on v3

--- a/solution.py
+++ b/solution.py
@@ -198,7 +198,7 @@
             pltpu.VMEM((tokens, lanes), BF16),
             pltpu.VMEM((tokens, out_width), F32),
         ],
-        compiler_params=pltpu.CompilerParams(vmem_limit_bytes=VMEM_BYTES),
+        compiler_params=pltpu.CompilerParams(vmem_limit_bytes=44 << 20),
         cost_estimate=pl.CostEstimate(
             flops=1 << 20, bytes_accessed=24 * MICROSECOND, transcendentals=0
         ),
@@ -284,19 +284,23 @@
 def regroup_kernel(*refs):
     out_ref = refs[-1]
     rows = refs[0].shape[0]
+    count, _, wide = out_ref.shape
     for at, piece_ref in enumerate(refs[:-1]):
-        out_ref[0, at * rows : (at + 1) * rows, :] = piece_ref[...].astype(BF16)
+        for h in range(count):
+            block = piece_ref[:, h * wide : (h + 1) * wide]
+            out_ref[h, at * rows : (at + 1) * rows, :] = block.astype(BF16)
 
 
 def regroup(pieces, hid):
     rows, width = pieces[0].shape
     wide = width // hid
     tall = rows * len(pieces)
+    steps = 4
     return pl.pallas_call(
         regroup_kernel,
-        grid=(hid,),
-        in_specs=[pl.BlockSpec((rows, wide), lambda h: (0, h))] * len(pieces),
-        out_specs=pl.BlockSpec((1, tall, wide), lambda h: (h, 0, 0)),
+        grid=(steps,),
+        in_specs=[pl.BlockSpec((rows, width // steps), lambda h: (0, h))] * len(pieces),
+        out_specs=pl.BlockSpec((hid // steps, tall, wide), lambda h: (h, 0, 0)),
         out_shape=jax.ShapeDtypeStruct((hid, tall, wide), BF16),
         compiler_params=pltpu.CompilerParams(vmem_limit_bytes=VMEM_BYTES),
         cost_estimate=pl.CostEstimate(flops=0, bytes_accessed=20 << 20, transcendentals=0),
@@ -381,26 +385,25 @@
 
     @pl.when(step == steps - 1)
     def _():
-        blocks, _, units = hidden_ref.shape
+        units = hidden_ref.shape[1]
         ready = 0
-        for at in range(blocks):
-            while ready < count and places[ready] < (at + 1) * units:
+        for first in range(0, units, 256):
+            end = min(first + 256, units)
+            while ready < count and places[ready] < end:
                 copies[ready].wait()
                 ready += 1
-            inner = matmul_nt(mixed[...], taken[at * units : (at + 1) * units, :])
-            inner = jnp.maximum(inner, 0.0)
-            hidden_ref[at] = (inner * inner).astype(BF16)
-
-
-def channel_inputs(length, tokens, attended, gain, first, mixes, rows, units):
+            inner = jnp.maximum(matmul_nt(mixed[...], taken[first:end, :]), 0.0)
+            hidden_ref[:, first:end] = (inner * inner).astype(BF16)
+
+
+def channel_inputs(length, tokens, attended, gain, first, mixes, rows):
     seq_len, width = tokens.shape
-    tall = min(64, seq_len)
+    tall = min(128, seq_len)
     steps = seq_len // tall
     by_rows = pl.BlockSpec((tall, width), lambda i: (i, 0))
     places = [0]
     for block in rows:
         places.append(places[-1] + block.shape[0])
-    blocks = places[-1] // units
 
     def wide(number):
         return pl.BlockSpec((number, width), lambda i: (0, 0))
@@ -418,12 +421,12 @@
         ]
         + [pl.BlockSpec(memory_space=pl.ANY)] * len(rows),
         out_specs=[
-            pl.BlockSpec((blocks, seq_len, units), lambda i: (0, 0, 0)),
+            pl.BlockSpec((seq_len, places[-1]), lambda i: (0, 0)),
             by_rows,
             wide(1),
         ],
         out_shape=[
-            jax.ShapeDtypeStruct((blocks, seq_len, units), BF16),
+            jax.ShapeDtypeStruct((seq_len, places[-1]), BF16),
             jax.ShapeDtypeStruct((seq_len, width), BF16),
             jax.ShapeDtypeStruct((1, width), F32),
         ],
@@ -442,25 +445,18 @@
 
 
 def exit_kernel(hidden_ref, *refs):
-    values, out_ref = refs[:-1], refs[-1]
-    units = hidden_ref.shape[2]
-    total, at, blocks = 0.0, 0, []
-    for values_ref in values:
-        blocks.append(values_ref[...])
-        if sum(block.shape[0] for block in blocks) == units:
-            total = total + matmul(hidden_ref[at], jnp.concatenate(blocks, axis=0))
-            at, blocks = at + 1, []
-    out_ref[...] = total.astype(BF16)
+    values = jnp.concatenate([ref[...] for ref in refs[:-1]], axis=0)
+    refs[-1][...] = matmul(hidden_ref[...], values).astype(BF16)
 
 
 def exit_product(hidden, values):
-    tokens = hidden.shape[1]
+    tokens = hidden.shape[0]
     width = values[0].shape[1]
-    tile = min(512, width)
+    tile = min(1024, width)
     return pl.pallas_call(
         exit_kernel,
         grid=(width // tile,),
-        in_specs=[pl.BlockSpec(hidden.shape, lambda n: (0, 0, 0))]
+        in_specs=[pl.BlockSpec(hidden.shape, lambda n: (0, 0))]
         + [pl.BlockSpec((v.shape[0], tile), lambda n: (0, n)) for v in values],
         out_specs=pl.BlockSpec((tokens, tile), lambda n: (0, n)),
         out_shape=jax.ShapeDtypeStruct((tokens, width), BF16),
@@ -648,7 +644,6 @@
         carried[1:],
         mix_rows[5:],
         key_rows,
-        units,
     )
     accept = matmul(accept_in, feedforward_accept_proj)
     terms = exit_product(hidden, value_rows)

time: 448 us -> 444 us (level)
  Pallas kernels: 120 us -> 114 us
  transfers between devices with their start and end apart: 20 -> 20, of which waited for: 13 -> 13; matrix products, arithmetic and copies ran while one was open for 10% -> 9% of each run, Pallas kernels for 21% -> 21%
where the time goes in v4:
time: 444 us; the launch traced here: 443 us
  waiting for transfers between devices  244 us (55%)
  Pallas kernels  114 us (26%)
  local copies, waits for them, and re-layouts  26.1 us (6%)
  starting transfers between devices  23.3 us (5%)
  matrix products  16.5 us (4%)
  between operations  15.9 us (4%)
    ppermute x16, waiting for transfers between devices, across(): return lax.ppermute(value, 'req', [(i, i ^ axis) for i in range(4)])  168 us
    reduce_scatter x1, waiting for transfers between devices, local(): summed = lax.psum_scatter(terms, 'hid', scatter_dimension=1, tiled=True)  40.5 us
    all_to_all x1, waiting for transfers between devices, to_heads(): lax.all_to_all(columns, 'hid', split_axis=0, concat_axis=0, tiled=True)  29.3 us
    pallas_call x1, Pallas kernels, recurrence(): pl.pallas_call(partial(recurrence_kernel, steps, len(far)), grid=(steps,)...  28.5 us
    pallas_call x1, Pallas kernels, channel_inputs(): pl.pallas_call(partial(channel_kernel, places[:-1], steps), grid=(steps,)...  25.8 us
    pallas_call x1, Pallas kernels, prepare(): pl.pallas_call(prepare_kernel, grid_spec=pltpu.PrefetchScalarGridSpec(num...  25.4 us
    ppermute x16, starting transfers between devices, across(): return lax.ppermute(value, 'req', [(i, i ^ axis) for i in range(4)])  16.8 us
    dot_general x3, matrix products, matmul(): return jnp.dot(a, b, preferred_element_type=F32)  16.5 us
  transfers between devices with their start and end apart: 20, of which 13 were waited for; matrix products, arithmetic and copies ran while one was open for 9% of the time, Pallas kernels for 21%

profile of v4, /device:TPU:0, one launch (start us, length us, event | category | flops | bytes accessed | tf_op | source)
XLA Modules:
  0.0 443.4 jit_solution(7291429043547845887)
XLA Ops:
  7.2 5.0 %regroup.1 = bf16[8,384,512]{2,1,0:T(8,128)(2,1)} custom-call(f32[128,4096]{1,0:T(8,128)} %refs_0_.2, f32[128,4096]{1,0:T(8,128)} %refs_1_.1, f32[128,4096]{1,0:T(8,128)} %refs_2_.1), custom_call_target="tpu_custom_call" | custom-call | bytes 20971520 | tf_op jit(solution)/shard_map/regroup/pallas_call | solution.py:299
  12.2 6.3 %all-to-all-start = ((bf16[8,384,512]{2,1,0:T(8,128)(2,1)}), bf16[8,384,512]{2,1,0:T(8,128)(2,1)}, u32[]{:S(2)}, u32[]{:S(2)}) async-start(bf16[8,384,512]{2,1,0:T(8,128)(2,1)} %regroup.1), calls=%async_computation | async-start | bytes 6291456 | tf_op jit(solution)/shard_map/all_to_all | solution.py:577
  18.6 1.6 collective-permute-start
  20.1 1.5 collective-permute-start.1
  23.0 1.7 convert_select_fusion
  24.7 1.6 select_n.41
  29.7 25.4 %prepare.1 = (bf16[3,512,4096]{2,1,0:T(8,128)(2,1)}, bf16[512,4096]{1,0:T(8,128)(2,1)}, bf16[512,4096]{1,0:T(8,128)(2,1)}, f32[1,4096]{1,0:T(1,128)}) custom-call(s32[32]{0:T(128)} %pad_add_fusion.order_ref, s32[1]{0:T(128)S(6)} %copy.26.length_ref, bf16[512,4096]{1,0:T(8,128)(2,1)} %bitcast.32, f32[1,4096]{1,0:T(1,128)} %get-tuple-element.96.gain_ref, ...), custom_call_target="tpu_custom_call" | custom-call | flops 1048576 | bytes 81180000 | tf_op jit(solution)/shard_map/prepare/pallas_call | solution.py:262
  55.1 3.8 fusion.1.refs_2_
  58.9 5.8 %fusion.5.refs_3_ = f32[512,512]{1,0:T(8,128)S(1)} fusion(bf16[512,4096]{1,0:T(8,128)(2,1)} %get-tuple-element.49, bf16[4096,512]{1,0:T(8,128)(2,1)} %param.37), kind=kOutput, calls=%fused_computation.14 | convolution fusion | flops 2147483648 | bytes 9437184 | tf_op jit(solution)/shard_map/dot_general | solution.py:30
  64.7 1.0 reshape.63.refs_7_
  65.8 29.3 %all-to-all-done = bf16[8,384,512]{2,1,0:T(8,128)(2,1)} async-done(((bf16[8,384,512]{2,1,0:T(8,128)(2,1)}), bf16[8,384,512]{2,1,0:T(8,128)(2,1)}, u32[]{:S(2)}, u32[]{:S(2)}) %all-to-all-start) | async-done | bytes 3145760 | tf_op jit(solution)/shard_map/all_to_all | solution.py:577
  95.0 2.1 fusion.2
  97.2 3.5 collective-permute-done.refs_1_
  100.7 1.2 collective-permute-done.1.refs_2_
  102.4 1.5 collective-permute-start.3
  103.9 1.5 collective-permute-start.4
  106.0 2.5 slice.62
  108.5 1.9 slice.64
  110.3 2.6 slice.63
  112.9 1.9 slice.65
  114.8 24.5 %collective-permute-done.2.refs_2_ = bf16[4,3,128,512]{3,2,1,0:T(8,128)(2,1)} collective-permute-done((bf16[4,3,128,512]{3,2,1,0:T(8,128)(2,1)S(1)}, bf16[4,3,128,512]{3,2,1,0:T(8,128)(2,1)}, u32[]{:S(2)}, u32[]{:S(2)}) %collective-permute-start.2) | collective-permute-done | bytes 1572896 | tf_op jit(solution)/shard_map/ppermute | solution.py:42
  139.3 32.0 %collective-permute-done.3.refs_3_ = bf16[4,3,128,512]{3,2,1,0:T(8,128)(2,1)S(1)} collective-permute-done((bf16[4,3,128,512]{3,2,1,0:T(8,128)(2,1)S(1)}, bf16[4,3,128,512]{3,2,1,0:T(8,128)(2,1)S(1)}, u32[]{:S(2)}, u32[]{:S(2)}) %collective-permute-start.3) | collective-permute-done | bytes 1572896 | tf_op jit(solution)/shard_map/ppermute | solution.py:42
  171.3 1.6 collective-permute-done.5.refs_5_
  172.9 1.5 collective-permute-start.6
  175.0 13.5 %project.1.base_ref = f32[3,512,512]{2,1,0:T(8,128)} custom-call(bf16[3,512,4096]{2,1,0:T(8,128)(2,1)} %get-tuple-element.50.values_ref, bf16[4,3,128,512]{3,2,1,0:T(8,128)(2,1)} %bitcast.40, bf16[4,3,128,512]{3,2,1,0:T(8,128)(2,1)} %bitcast.37, bf16[4,3,128,512]{3,2,1,0:T(8,128)(2,1)} %collective-permute-done.2.refs_2_, bf16[4,3,128,512]{3,2,1,0:T(8,128)(2,1)} %copy-done.9, ...), custom_call_target="tpu_custom_call" | custom-call | flops 1048576 | bytes 47970000 | tf_op jit(solution)/shard_map/project/pallas_call | solution.py:331
  188.5 19.1 %collective-permute-done.6.refs_0_ = bf16[4,3,128,512]{3,2,1,0:T(8,128)(2,1)S(1)} collective-permute-done((bf16[4,3,128,512]{3,2,1,0:T(8,128)(2,1)}, bf16[4,3,128,512]{3,2,1,0:T(8,128)(2,1)S(1)}, u32[]{:S(2)}, u32[]{:S(2)}) %collective-permute-start.6) | collective-permute-done | bytes 1572896 | tf_op jit(solution)/shard_map/ppermute | solution.py:42
  207.5 1.3 collective-permute-done.7.refs_1_
  208.9 0.8 collective-permute-start.8
  210.4 1.9 copy-done.2
  212.3 28.5 %recurrence.1 = (bf16[512,4096]{1,0:T(8,128)(2,1)}, f32[8,64,64]{2,1,0:T(8,128)}) custom-call(s32[1]{0:T(128)S(6)} %copy.26.length_ref, f32[3,512,512]{2,1,0:T(8,128)S(1)} %copy-done.2, bf16[3,512,4096]{2,1,0:T(8,128)(2,1)} %get-tuple-element.50.values_ref, bf16[4,3,128,512]{3,2,1,0:T(8,128)(2,1)S(1)} %collective-permute-done.6.refs_0_, ...), custom_call_target="tpu_custom_call" | custom-call | flops 1048576 | bytes 88560000 | tf_op jit(solution)/shard_map/recurrence/pallas_call | solution.py:178
  240.8 1.4 collective-permute-start.10
  242.3 1.2 collective-permute-start.11
  243.5 0.8 collective-permute-start.12
  245.0 78.5 %collective-permute-done.10.refs_1_ = bf16[448,4096]{1,0:T(8,128)(2,1)} collective-permute-done((bf16[448,4096]{1,0:T(8,128)(2,1)}, bf16[448,4096]{1,0:T(8,128)(2,1)}, u32[]{:S(2)}, u32[]{:S(2)}) %collective-permute-start.10) | collective-permute-done | bytes 3670048 | tf_op jit(solution)/shard_map/ppermute | solution.py:42
  323.5 3.0 slice.80
  326.4 3.0 slice.81
  329.4 3.4 collective-permute-done.12.refs_4_
  332.8 1.3 collective-permute-start.14
  334.1 0.7 collective-permute-start.15
  335.4 6.2 %all-reduce.2.cloned.1.call-done.attended_ref = bf16[512,4096]{1,0:T(8,128)(2,1)} async-done(((bf16[512,4096]{1,0:T(8,128)(2,1)}), bf16[512,4096]{1,0:T(8,128)(2,1)}) %all-reduce.2.cloned.1.call-update) | async-done | bytes 4194320 | tf_op jit(solution)/shard_map/psum | solution.py:626
  341.6 25.8 %channel_inputs.1 = (bf16[512,1792]{1,0:T(8,128)(2,1)}, bf16[512,4096]{1,0:T(8,128)(2,1)}, f32[1,4096]{1,0:T(1,128)}) custom-call(s32[1]{0:T(128)S(6)} %copy.26.length_ref, bf16[512,4096]{1,0:T(8,128)(2,1)} %bitcast.33, bf16[512,4096]{1,0:T(8,128)(2,1)} %all-reduce.2.cloned.1.call-done.attended_ref, f32[1,4096]{1,0:T(1,128)} %get-tuple-element.95.gain_ref, ...), custom_call_target="tpu_custom_call" | custom-call | flops 1048576 | bytes 81180000 | tf_op jit(solution)/shard_map/channel_inputs/pallas_call | solution.py:411
  367.4 3.3 collective-permute-done.14.refs_3_
  370.7 1.3 copy-done.8
  372.0 13.0 %exit_product.1 = bf16[512,4096]{1,0:T(8,128)(2,1)} custom-call(bf16[512,1792]{1,0:T(8,128)(2,1)} %get-tuple-element.85.hidden_ref, bf16[448,4096]{1,0:T(8,128)(2,1)} %refs_0_.4, bf16[448,4096]{1,0:T(8,128)(2,1)} %collective-permute-done.10.refs_1_, bf16[448,4096]{1,0:T(8,128)(2,1)} %collective-permute-done.11.refs_2_, bf16[224,4096]{1,0:T(8,128)(2,1)} %copy-done.8, ...), custom_call_target="tpu_custom_call" | custom-call | flops 1048576 | bytes 25830000 | tf_op jit(solution)/shard_map/exit_product/pallas_call | solution.py:456
  385.0 0.7 copy-done.17
  386.4 6.9 %fusion.6.gate_ref = f32[512,512]{1,0:T(8,128)} fusion(bf16[512,4096]{1,0:T(8,128)(2,1)} %get-tuple-element.84, bf16[4096,512]{1,0:T(8,128)(2,1)} %param.43), kind=kOutput, calls=%fused_computation.15 | convolution fusion | flops 2147483648 | bytes 9437184 | tf_op jit(solution)/shard_map/dot_general | solution.py:30
  393.3 40.5 %reduce-scatter.5.cloned.1.call-done.refs_0_ = bf16[512,512]{1,0:T(8,128)(2,1)} async-done(((bf16[512,4096]{1,0:T(8,128)(2,1)}), bf16[512,512]{1,0:T(8,128)(2,1)}) %reduce-scatter.5.cloned.1.call-update) | async-done | bytes 524304 | tf_op jit(solution)/shard_map/reduce_scatter | solution.py:650
  433.8 3.1 combine.1
  (65 shorter events, 7.2 us)
Async XLA Ops:
  7.2 47.9 %copy-start = (bf16[4096,128]{1,0:T(8,128)(2,1)S(1)}, bf16[4096,128]{1,0:T(8,128)(2,1)}, u32[]{:S(2)}) copy-start(bf16[4096,128]{1,0:T(8,128)(2,1)} %param.33) | copy-start | bytes 3145732
  12.2 82.9 %all-to-all-start = ((bf16[8,384,512]{2,1,0:T(8,128)(2,1)}), bf16[8,384,512]{2,1,0:T(8,128)(2,1)}, u32[]{:S(2)}, u32[]{:S(2)}) async-start(bf16[8,384,512]{2,1,0:T(8,128)(2,1)} %regroup.1), calls=%async_computation | async-start | bytes 6291456 | tf_op jit(solution)/shard_map/all_to_all | solution.py:577
  18.5 7.9 %copy-start.16 = (bf16[1,2,4096]{2,1,0:T(2,128)(2,1)S(1)}, bf16[1,2,4096]{2,1,0:T(2,128)(2,1)}, u32[]{:S(2)}) copy-start(bf16[1,2,4096]{2,1,0:T(2,128)(2,1)} %param.40) | copy-start | bytes 49156
  18.5 8.6 %copy-start.13 = (bf16[7,4096]{1,0:T(8,128)(2,1)S(1)}, bf16[7,4096]{1,0:T(8,128)(2,1)}, u32[]{:S(2)}) copy-start(bf16[7,4096]{1,0:T(8,128)(2,1)} %param.31) | copy-start | bytes 172036
  18.5 9.2 %copy-start.19 = (s32[32]{0:T(128)S(1)}, s32[32]{0:T(128)}, u32[]{:S(2)}) copy-start(s32[32]{0:T(128)} %param.26) | copy-start | bytes 388
  18.5 9.9 %copy-start.15 = (bf16[2,4096]{1,0:T(2,128)(2,1)S(1)}, bf16[2,4096]{1,0:T(2,128)(2,1)}, u32[]{:S(2)}) copy-start(bf16[2,4096]{1,0:T(2,128)(2,1)} %param.30) | copy-start | bytes 49156
  18.5 46.2 %reduce-scatter.3.cloned.1.call-start = ((), (), s32[]{:S(2)}) async-start(), calls=%async_computation.3 | async-start | bytes 589824 | tf_op jit(solution)/shard_map/reduce_scatter | solution.py:543
  18.6 82.1 %collective-permute-start = (bf16[448,4096]{1,0:T(8,128)(2,1)}, bf16[448,4096]{1,0:T(8,128)(2,1)}, u32[]{:S(2)}, u32[]{:S(2)}) collective-permute-start(bf16[448,4096]{1,0:T(8,128)(2,1)} %refs_0_.3), channel_id=1, source_target_pairs={{0,8},{8,0},{16,24},{24,16},{1,9},{9,1},{17,25},{25,17},{2,10},{10... | collective-permute-start | bytes 11010056 | tf_op jit(solution)/shard_map/ppermute | solution.py:42
  20.1 81.8 %collective-permute-start.1 = (bf16[448,4096]{1,0:T(8,128)(2,1)}, bf16[448,4096]{1,0:T(8,128)(2,1)}, u32[]{:S(2)}, u32[]{:S(2)}) collective-permute-start(bf16[448,4096]{1,0:T(8,128)(2,1)} %refs_0_.3), channel_id=1, source_target_pairs={{0,16},{8,24},{16,0},{24,8},{1,17},{9,25},{17,1},{25,9},{2,18},{10... | collective-permute-start | bytes 11010056 | tf_op jit(solution)/shard_map/ppermute | solution.py:42
  24.7 30.4 %copy-start.14 = (bf16[128,512]{1,0:T(8,128)(2,1)S(1)}, bf16[128,512]{1,0:T(8,128)(2,1)}, u32[]{:S(2)}) copy-start(bf16[128,512]{1,0:T(8,128)(2,1)} %param.34) | copy-start | bytes 393220
  26.3 315.3 %all-reduce.2.cloned.1.call-start = ((), (), s32[]{:S(2)}) async-start(), calls=%async_computation.4 | async-start | bytes 8388608 | tf_op jit(solution)/shard_map/psum | solution.py:626
  97.1 17.7 %copy-start.6 = (bf16[4,384,512]{2,1,0:T(8,128)(2,1)}, bf16[4,384,512]{2,1,0:T(8,128)(2,1)S(1)}, u32[]{:S(2)}) copy-start(bf16[4,384,512]{2,1,0:T(8,128)(2,1)S(1)} %get-tuple-element.91) | copy-start | bytes 4718596
  97.1 17.7 %copy-start.7 = (bf16[4,384,512]{2,1,0:T(8,128)(2,1)}, bf16[4,384,512]{2,1,0:T(8,128)(2,1)S(1)}, u32[]{:S(2)}) copy-start(bf16[4,384,512]{2,1,0:T(8,128)(2,1)S(1)} %get-tuple-element.92) | copy-start | bytes 4718596
  101.9 37.4 %collective-permute-start.2 = (bf16[4,3,128,512]{3,2,1,0:T(8,128)(2,1)S(1)}, bf16[4,3,128,512]{3,2,1,0:T(8,128)(2,1)}, u32[]{:S(2)}, u32[]{:S(2)}) collective-permute-start(bf16[4,3,128,512]{3,2,1,0:T(8,128)(2,1)S(1)} %bitcast.38), channel_id=1, source_target_pairs={{0,8},{8,0},{16,24},{24,16},{1,9},{9,1},{17,25},{25,17},{2,10},{10... | collective-permute-start | bytes 4718600 | tf_op jit(solution)/shard_map/ppermute | solution.py:42
  102.4 68.9 %collective-permute-start.3 = (bf16[4,3,128,512]{3,2,1,0:T(8,128)(2,1)S(1)}, bf16[4,3,128,512]{3,2,1,0:T(8,128)(2,1)S(1)}, u32[]{:S(2)}, u32[]{:S(2)}) collective-permute-start(bf16[4,3,128,512]{3,2,1,0:T(8,128)(2,1)S(1)} %bitcast.35), channel_id=1, source_target_pairs={{0,8},{8,0},{16,24},{24,16},{1,9},{9,1},{17,25},{25,17},{2,10},{10... | collective-permute-start | bytes 4718600 | tf_op jit(solution)/shard_map/ppermute | solution.py:42
  103.9 67.4 %collective-permute-start.4 = (bf16[4,3,128,512]{3,2,1,0:T(8,128)(2,1)S(1)}, bf16[4,3,128,512]{3,2,1,0:T(8,128)(2,1)S(1)}, u32[]{:S(2)}, u32[]{:S(2)}) collective-permute-start(bf16[4,3,128,512]{3,2,1,0:T(8,128)(2,1)S(1)} %bitcast.39), channel_id=1, source_target_pairs={{0,16},{8,24},{16,0},{24,8},{1,17},{9,25},{17,1},{25,9},{2,18},{10... | collective-permute-start | bytes 4718600 | tf_op jit(solution)/shard_map/ppermute | solution.py:42
  105.4 67.4 %collective-permute-start.5 = (bf16[4,3,128,512]{3,2,1,0:T(8,128)(2,1)S(1)}, bf16[4,3,128,512]{3,2,1,0:T(8,128)(2,1)}, u32[]{:S(2)}, u32[]{:S(2)}) collective-permute-start(bf16[4,3,128,512]{3,2,1,0:T(8,128)(2,1)S(1)} %bitcast.36), channel_id=1, source_target_pairs={{0,16},{8,24},{16,0},{24,8},{1,17},{9,25},{17,1},{25,9},{2,18},{10... | collective-permute-start | bytes 4718600 | tf_op jit(solution)/shard_map/ppermute | solution.py:42
  114.8 95.6 %copy-start.3 = (f32[512]{0:T(512)S(1)}, f32[512]{0:T(512)}, u32[]{:S(2)}) copy-start(f32[512]{0:T(512)} %param.32) | copy-start | bytes 6148
  114.8 95.6 %copy-start.4 = (f32[512]{0:T(512)S(1)}, f32[512]{0:T(512)}, u32[]{:S(2)}) copy-start(f32[512]{0:T(512)} %param.35) | copy-start | bytes 6148
  114.8 95.6 %copy-start.5 = (f32[512]{0:T(512)S(1)}, f32[512]{0:T(512)}, u32[]{:S(2)}) copy-start(f32[512]{0:T(512)} %param.36) | copy-start | bytes 6148
  171.3 1.6 copy-start.9
  171.3 3.1 copy-start.10
  172.9 34.7 %collective-permute-start.6 = (bf16[4,3,128,512]{3,2,1,0:T(8,128)(2,1)}, bf16[4,3,128,512]{3,2,1,0:T(8,128)(2,1)S(1)}, u32[]{:S(2)}, u32[]{:S(2)}) collective-permute-start(bf16[4,3,128,512]{3,2,1,0:T(8,128)(2,1)} %collective-permute-done.2.refs_2_), channel_id=1, source_target_pairs={{0,16},{8,24},{16,0},{24,8},{1,17},{9,25},{17,1},{25,9},{2,18},{10... | collective-permute-start | bytes 4718600 | tf_op jit(solution)/shard_map/ppermute | solution.py:42
  174.4 34.5 %collective-permute-start.7 = (bf16[4,3,128,512]{3,2,1,0:T(8,128)(2,1)}, bf16[4,3,128,512]{3,2,1,0:T(8,128)(2,1)}, u32[]{:S(2)}, u32[]{:S(2)}) collective-permute-start(bf16[4,3,128,512]{3,2,1,0:T(8,128)(2,1)} %collective-permute-done.5.refs_5_), channel_id=1, source_target_pairs={{0,8},{8,0},{16,24},{24,16},{1,9},{9,1},{17,25},{25,17},{2,10},{10... | collective-permute-start | bytes 4718600 | tf_op jit(solution)/shard_map/ppermute | solution.py:42
  208.9 31.9 %collective-permute-start.8 = (bf16[160,4096]{1,0:T(8,128)(2,1)}, bf16[160,4096]{1,0:T(8,128)(2,1)}, u32[]{:S(2)}, u32[]{:S(2)}) collective-permute-start(bf16[160,4096]{1,0:T(8,128)(2,1)} %slice.62), channel_id=1, source_target_pairs={{0,16},{8,24},{16,0},{24,8},{1,17},{9,25},{17,1},{25,9},{2,18},{10... | collective-permute-start | bytes 3932168 | tf_op jit(solution)/shard_map/ppermute | solution.py:42
  209.7 31.1 %collective-permute-start.9 = (bf16[160,4096]{1,0:T(8,128)(2,1)}, bf16[160,4096]{1,0:T(8,128)(2,1)}, u32[]{:S(2)}, u32[]{:S(2)}) collective-permute-start(bf16[160,4096]{1,0:T(8,128)(2,1)} %slice.63), channel_id=1, source_target_pairs={{0,8},{8,0},{16,24},{24,16},{1,9},{9,1},{17,25},{25,17},{2,10},{10... | collective-permute-start | bytes 3932168 | tf_op jit(solution)/shard_map/ppermute | solution.py:42
  210.4 1.9 copy-start.2
  240.8 82.7 %collective-permute-start.10 = (bf16[448,4096]{1,0:T(8,128)(2,1)}, bf16[448,4096]{1,0:T(8,128)(2,1)}, u32[]{:S(2)}, u32[]{:S(2)}) collective-permute-start(bf16[448,4096]{1,0:T(8,128)(2,1)} %refs_0_.4), channel_id=1, source_target_pairs={{0,8},{8,0},{16,24},{24,16},{1,9},{9,1},{17,25},{25,17},{2,10},{10... | collective-permute-start | bytes 11010056 | tf_op jit(solution)/shard_map/ppermute | solution.py:42
  242.3 84.2 %collective-permute-start.11 = (bf16[448,4096]{1,0:T(8,128)(2,1)}, bf16[448,4096]{1,0:T(8,128)(2,1)}, u32[]{:S(2)}, u32[]{:S(2)}) collective-permute-start(bf16[448,4096]{1,0:T(8,128)(2,1)} %refs_0_.4), channel_id=1, source_target_pairs={{0,16},{8,24},{16,0},{24,8},{1,17},{9,25},{17,1},{25,9},{2,18},{10... | collective-permute-start | bytes 11010056 | tf_op jit(solution)/shard_map/ppermute | solution.py:42
  243.5 89.3 %collective-permute-start.12 = (bf16[64,4096]{1,0:T(8,128)(2,1)}, bf16[64,4096]{1,0:T(8,128)(2,1)S(1)}, u32[]{:S(2)}, u32[]{:S(2)}) collective-permute-start(bf16[64,4096]{1,0:T(8,128)(2,1)} %slice.64), channel_id=1, source_target_pairs={{0,16},{8,24},{16,0},{24,8},{1,17},{9,25},{17,1},{25,9},{2,18},{10... | collective-permute-start | bytes 1572872 | tf_op jit(solution)/shard_map/ppermute | solution.py:42
  244.3 88.5 %collective-permute-start.13 = (bf16[64,4096]{1,0:T(8,128)(2,1)}, bf16[64,4096]{1,0:T(8,128)(2,1)S(1)}, u32[]{:S(2)}, u32[]{:S(2)}) collective-permute-start(bf16[64,4096]{1,0:T(8,128)(2,1)} %slice.65), channel_id=1, source_target_pairs={{0,8},{8,0},{16,24},{24,16},{1,9},{9,1},{17,25},{25,17},{2,10},{10... | collective-permute-start | bytes 1572872 | tf_op jit(solution)/shard_map/ppermute | solution.py:42
  245.0 188.8 %reduce-scatter.5.cloned.1.call-start = ((), (), s32[]{:S(2)}) async-start(), calls=%async_computation.5 | async-start | bytes 4718592 | tf_op jit(solution)/shard_map/reduce_scatter | solution.py:650
  332.8 8.8 %copy-start.11 = (bf16[64,4096]{1,0:T(8,128)(2,1)}, bf16[64,4096]{1,0:T(8,128)(2,1)S(1)}, u32[]{:S(2)}) copy-start(bf16[64,4096]{1,0:T(8,128)(2,1)S(1)} %collective-permute-done.12.refs_4_) | copy-start | bytes 1572868
  332.8 8.7 %copy-start.12 = (bf16[64,4096]{1,0:T(8,128)(2,1)}, bf16[64,4096]{1,0:T(8,128)(2,1)S(1)}, u32[]{:S(2)}) copy-start(bf16[64,4096]{1,0:T(8,128)(2,1)S(1)} %collective-permute-done.13.refs_6_) | copy-start | bytes 1572868
  332.8 37.9 %collective-permute-start.14 = (bf16[224,4096]{1,0:T(8,128)(2,1)}, bf16[224,4096]{1,0:T(8,128)(2,1)S(1)}, u32[]{:S(2)}, u32[]{:S(2)}) collective-permute-start(bf16[224,4096]{1,0:T(8,128)(2,1)} %slice.80), channel_id=1, source_target_pairs={{0,16},{8,24},{16,0},{24,8},{1,17},{9,25},{17,1},{25,9},{2,18},{10... | collective-permute-start | bytes 5505032 | tf_op jit(solution)/shard_map/ppermute | solution.py:42
  334.1 36.6 %collective-permute-start.15 = (bf16[224,4096]{1,0:T(8,128)(2,1)}, bf16[224,4096]{1,0:T(8,128)(2,1)}, u32[]{:S(2)}, u32[]{:S(2)}) collective-permute-start(bf16[224,4096]{1,0:T(8,128)(2,1)} %slice.81), channel_id=1, source_target_pairs={{0,8},{8,0},{16,24},{24,16},{1,9},{9,1},{17,25},{25,17},{2,10},{10... | collective-permute-start | bytes 5505032 | tf_op jit(solution)/shard_map/ppermute | solution.py:42
  370.7 1.3 copy-start.8
  385.0 0.7 copy-start.17
  385.0 0.7 copy-start.18
  433.8 3.1 copy-start.1
Sparse Core Ops, SparseCore 0:
  26.4 33.8 reduce-scatter.2
  245.1 96.4 all-reduce.1
  385.2 48.5 reduce-scatter.4

commit v5 on v4

--- a/solution.py
+++ b/solution.py
@@ -585,7 +585,7 @@
     hold = lax.optimization_barrier
     if req == 4:
         half = units // 2
-        cut = half * 5 // 7 // 16 * 16
+        cut = half * 11 // 14 // 16 * 16
         key_mine, value_mine = feedforward_entry_proj, feedforward_exit_proj
         key_x, key_y = across(key_mine, 1), across(key_mine, 2)
         mine = to_heads(columns)
@@ -619,12 +619,9 @@
         start,
         mixing_exit_projection,
     )
-    if req == 4:
-        head_terms, value_mine, second, key_far = hold(
-            (head_terms, value_mine, second, key_far)
-        )
     attended = lax.psum(head_terms, "hid")
     if req == 4:
+        new_state, value_mine, second, key_far = hold((new_state, value_mine, second, key_far))
         value_x, value_y = across(value_mine, 1), across(value_mine, 2)
         key_far.insert(1, across(second[0], 2))
         key_far.append(across(second[1], 1))

time: 444 us -> 442 us (level)
    ppermute x16, waiting for transfers between devices: 168 us -> 163 us  [across(): return lax.ppermute(value, 'req', [(i, i ^ axis) for i in range(4)])]
where the time goes in v5:
time: 442 us
  waiting for transfers between devices  243 us (55%)
  Pallas kernels  114 us (26%)
  local copies, waits for them, and re-layouts  26.1 us (6%)
  starting transfers between devices  23.3 us (5%)
  matrix products  16.4 us (4%)
  between operations  15.9 us (4%)
    ppermute x16, waiting for transfers between devices, across(): return lax.ppermute(value, 'req', [(i, i ^ axis) for i in range(4)])  163 us
    reduce_scatter x1, waiting for transfers between devices, local(): summed = lax.psum_scatter(terms, 'hid', scatter_dimension=1, tiled=True)  41.7 us
    all_to_all x1, waiting for transfers between devices, to_heads(): lax.all_to_all(columns, 'hid', split_axis=0, concat_axis=0, tiled=True)  29.3 us
    pallas_call x1, Pallas kernels, recurrence(): pl.pallas_call(partial(recurrence_kernel, steps, len(far)), grid=(steps,)...  28.5 us
    pallas_call x1, Pallas kernels, channel_inputs(): pl.pallas_call(partial(channel_kernel, places[:-1], steps), grid=(steps,)...  25.6 us
    pallas_call x1, Pallas kernels, prepare(): pl.pallas_call(prepare_kernel, grid_spec=pltpu.PrefetchScalarGridSpec(num...  25.4 us
    ppermute x16, starting transfers between devices, across(): return lax.ppermute(value, 'req', [(i, i ^ axis) for i in range(4)])  16.8 us
    dot_general x3, matrix products, matmul(): return jnp.dot(a, b, preferred_element_type=F32)  16.4 us
  transfers between devices with their start and end apart: 20, of which 13 were waited for; matrix products, arithmetic and copies ran while one was open for 9% of the time, Pallas kernels for 21%

profile of v5, /device:TPU:0, one launch (start us, length us, event | category | flops | bytes accessed | tf_op | source)
XLA Modules:
  0.0 441.5 jit_solution(1933855542231293837)
XLA Ops:
  7.2 5.0 %regroup.1 = bf16[8,384,512]{2,1,0:T(8,128)(2,1)} custom-call(f32[128,4096]{1,0:T(8,128)} %refs_0_.2, f32[128,4096]{1,0:T(8,128)} %refs_1_.1, f32[128,4096]{1,0:T(8,128)} %refs_2_.1), custom_call_target="tpu_custom_call" | custom-call | bytes 20971520 | tf_op jit(solution)/shard_map/regroup/pallas_call | solution.py:299
  12.2 6.3 %all-to-all-start = ((bf16[8,384,512]{2,1,0:T(8,128)(2,1)}), bf16[8,384,512]{2,1,0:T(8,128)(2,1)}, u32[]{:S(2)}, u32[]{:S(2)}) async-start(bf16[8,384,512]{2,1,0:T(8,128)(2,1)} %regroup.1), calls=%async_computation | async-start | bytes 6291456 | tf_op jit(solution)/shard_map/all_to_all | solution.py:577
  18.6 1.6 collective-permute-start
  20.1 1.5 collective-permute-start.1
  23.0 1.7 convert_select_fusion
  24.7 1.6 select_n.41
  29.7 25.4 %prepare.1 = (bf16[3,512,4096]{2,1,0:T(8,128)(2,1)}, bf16[512,4096]{1,0:T(8,128)(2,1)}, bf16[512,4096]{1,0:T(8,128)(2,1)}, f32[1,4096]{1,0:T(1,128)}) custom-call(s32[32]{0:T(128)} %pad_add_fusion.order_ref, s32[1]{0:T(128)S(6)} %copy.26.length_ref, bf16[512,4096]{1,0:T(8,128)(2,1)} %bitcast.32, f32[1,4096]{1,0:T(1,128)} %get-tuple-element.96.gain_ref, ...), custom_call_target="tpu_custom_call" | custom-call | flops 1048576 | bytes 81180000 | tf_op jit(solution)/shard_map/prepare/pallas_call | solution.py:262
  55.0 3.8 fusion.1.refs_2_
  58.9 5.8 %fusion.5.refs_3_ = f32[512,512]{1,0:T(8,128)S(1)} fusion(bf16[512,4096]{1,0:T(8,128)(2,1)} %get-tuple-element.49, bf16[4096,512]{1,0:T(8,128)(2,1)} %param.37), kind=kOutput, calls=%fused_computation.14 | convolution fusion | flops 2147483648 | bytes 9437184 | tf_op jit(solution)/shard_map/dot_general | solution.py:30
  64.7 1.0 reshape.63.refs_7_
  65.7 29.3 %all-to-all-done = bf16[8,384,512]{2,1,0:T(8,128)(2,1)} async-done(((bf16[8,384,512]{2,1,0:T(8,128)(2,1)}), bf16[8,384,512]{2,1,0:T(8,128)(2,1)}, u32[]{:S(2)}, u32[]{:S(2)}) %all-to-all-start) | async-done | bytes 3145760 | tf_op jit(solution)/shard_map/all_to_all | solution.py:577
  95.0 2.1 fusion.2
  97.2 3.5 collective-permute-done.refs_1_
  100.7 1.2 collective-permute-done.1.refs_2_
  102.4 1.5 collective-permute-start.3
  103.9 1.5 collective-permute-start.4
  106.0 2.7 slice.62
  108.6 1.8 slice.64
  110.4 2.7 slice.63
  113.1 1.8 slice.65
  114.9 24.5 %collective-permute-done.2.refs_2_ = bf16[4,3,128,512]{3,2,1,0:T(8,128)(2,1)} collective-permute-done((bf16[4,3,128,512]{3,2,1,0:T(8,128)(2,1)S(1)}, bf16[4,3,128,512]{3,2,1,0:T(8,128)(2,1)}, u32[]{:S(2)}, u32[]{:S(2)}) %collective-permute-start.2) | collective-permute-done | bytes 1572896 | tf_op jit(solution)/shard_map/ppermute | solution.py:42
  139.3 32.0 %collective-permute-done.3.refs_3_ = bf16[4,3,128,512]{3,2,1,0:T(8,128)(2,1)S(1)} collective-permute-done((bf16[4,3,128,512]{3,2,1,0:T(8,128)(2,1)S(1)}, bf16[4,3,128,512]{3,2,1,0:T(8,128)(2,1)S(1)}, u32[]{:S(2)}, u32[]{:S(2)}) %collective-permute-start.3) | collective-permute-done | bytes 1572896 | tf_op jit(solution)/shard_map/ppermute | solution.py:42
  171.3 1.6 collective-permute-done.5.refs_5_
  172.9 1.5 collective-permute-start.6
  175.0 13.5 %project.1.base_ref = f32[3,512,512]{2,1,0:T(8,128)} custom-call(bf16[3,512,4096]{2,1,0:T(8,128)(2,1)} %get-tuple-element.50.values_ref, bf16[4,3,128,512]{3,2,1,0:T(8,128)(2,1)} %bitcast.40, bf16[4,3,128,512]{3,2,1,0:T(8,128)(2,1)} %bitcast.37, bf16[4,3,128,512]{3,2,1,0:T(8,128)(2,1)} %collective-permute-done.2.refs_2_, bf16[4,3,128,512]{3,2,1,0:T(8,128)(2,1)} %copy-done.9, ...), custom_call_target="tpu_custom_call" | custom-call | flops 1048576 | bytes 47970000 | tf_op jit(solution)/shard_map/project/pallas_call | solution.py:331
  188.5 19.1 %collective-permute-done.6.refs_0_ = bf16[4,3,128,512]{3,2,1,0:T(8,128)(2,1)S(1)} collective-permute-done((bf16[4,3,128,512]{3,2,1,0:T(8,128)(2,1)}, bf16[4,3,128,512]{3,2,1,0:T(8,128)(2,1)S(1)}, u32[]{:S(2)}, u32[]{:S(2)}) %collective-permute-start.6) | collective-permute-done | bytes 1572896 | tf_op jit(solution)/shard_map/ppermute | solution.py:42
  207.6 1.3 collective-permute-done.7.refs_1_
  208.9 0.7 collective-permute-start.8
  209.6 0.7 collective-permute-start.9
  210.3 1.9 copy-done.2
  212.2 28.5 %recurrence.1 = (bf16[512,4096]{1,0:T(8,128)(2,1)}, f32[8,64,64]{2,1,0:T(8,128)}) custom-call(s32[1]{0:T(128)S(6)} %copy.26.length_ref, f32[3,512,512]{2,1,0:T(8,128)S(1)} %copy-done.2, bf16[3,512,4096]{2,1,0:T(8,128)(2,1)} %get-tuple-element.50.values_ref, bf16[4,3,128,512]{3,2,1,0:T(8,128)(2,1)S(1)} %collective-permute-done.6.refs_0_, ...), custom_call_target="tpu_custom_call" | custom-call | flops 1048576 | bytes 88560000 | tf_op jit(solution)/shard_map/recurrence/pallas_call | solution.py:178
  240.7 1.4 collective-permute-start.10
  242.1 1.3 collective-permute-start.11
  243.5 0.7 collective-permute-start.12
  244.2 0.7 collective-permute-start.13
  244.9 78.3 %collective-permute-done.10.refs_1_ = bf16[448,4096]{1,0:T(8,128)(2,1)} collective-permute-done((bf16[448,4096]{1,0:T(8,128)(2,1)}, bf16[448,4096]{1,0:T(8,128)(2,1)}, u32[]{:S(2)}, u32[]{:S(2)}) %collective-permute-start.10) | collective-permute-done | bytes 3670048 | tf_op jit(solution)/shard_map/ppermute | solution.py:42
  323.2 2.9 slice.80
  326.2 3.0 slice.81
  329.2 0.7 collective-permute-done.12.refs_4_
  329.9 1.4 collective-permute-start.14
  332.6 9.0 %all-reduce.2.cloned.1.call-done.attended_ref = bf16[512,4096]{1,0:T(8,128)(2,1)} async-done(((bf16[512,4096]{1,0:T(8,128)(2,1)}), bf16[512,4096]{1,0:T(8,128)(2,1)}) %all-reduce.2.cloned.1.call-update) | async-done | bytes 4194320 | tf_op jit(solution)/shard_map/psum | solution.py:622
  341.6 25.6 %channel_inputs.1 = (bf16[512,1792]{1,0:T(8,128)(2,1)}, bf16[512,4096]{1,0:T(8,128)(2,1)}, f32[1,4096]{1,0:T(1,128)}) custom-call(s32[1]{0:T(128)S(6)} %copy.26.length_ref, bf16[512,4096]{1,0:T(8,128)(2,1)} %bitcast.33, bf16[512,4096]{1,0:T(8,128)(2,1)} %all-reduce.2.cloned.1.call-done.attended_ref, f32[1,4096]{1,0:T(1,128)} %get-tuple-element.95.gain_ref, ...), custom_call_target="tpu_custom_call" | custom-call | flops 1048576 | bytes 81180000 | tf_op jit(solution)/shard_map/channel_inputs/pallas_call | solution.py:411
  367.7 1.3 copy-done.8
  369.0 13.0 %exit_product.1 = bf16[512,4096]{1,0:T(8,128)(2,1)} custom-call(bf16[512,1792]{1,0:T(8,128)(2,1)} %get-tuple-element.85.hidden_ref, bf16[448,4096]{1,0:T(8,128)(2,1)} %refs_0_.4, bf16[448,4096]{1,0:T(8,128)(2,1)} %collective-permute-done.10.refs_1_, bf16[448,4096]{1,0:T(8,128)(2,1)} %collective-permute-done.11.refs_2_, bf16[224,4096]{1,0:T(8,128)(2,1)} %copy-done.8, ...), custom_call_target="tpu_custom_call" | custom-call | flops 1048576 | bytes 25830000 | tf_op jit(solution)/shard_map/exit_product/pallas_call | solution.py:456
  382.0 0.7 copy-done.17
  383.4 6.8 %fusion.6.gate_ref = f32[512,512]{1,0:T(8,128)} fusion(bf16[512,4096]{1,0:T(8,128)(2,1)} %get-tuple-element.84, bf16[4096,512]{1,0:T(8,128)(2,1)} %param.43), kind=kOutput, calls=%fused_computation.15 | convolution fusion | flops 2147483648 | bytes 9437184 | tf_op jit(solution)/shard_map/dot_general | solution.py:30
  390.2 41.7 %reduce-scatter.5.cloned.1.call-done.refs_0_ = bf16[512,512]{1,0:T(8,128)(2,1)} async-done(((bf16[512,4096]{1,0:T(8,128)(2,1)}), bf16[512,512]{1,0:T(8,128)(2,1)}) %reduce-scatter.5.cloned.1.call-update) | async-done | bytes 524304 | tf_op jit(solution)/shard_map/reduce_scatter | solution.py:647
  431.9 3.1 combine.1
  (65 shorter events, 7.1 us)
Async XLA Ops:
  7.2 47.9 %copy-start = (bf16[4096,128]{1,0:T(8,128)(2,1)S(1)}, bf16[4096,128]{1,0:T(8,128)(2,1)}, u32[]{:S(2)}) copy-start(bf16[4096,128]{1,0:T(8,128)(2,1)} %param.33) | copy-start | bytes 3145732
  12.2 82.9 %all-to-all-start = ((bf16[8,384,512]{2,1,0:T(8,128)(2,1)}), bf16[8,384,512]{2,1,0:T(8,128)(2,1)}, u32[]{:S(2)}, u32[]{:S(2)}) async-start(bf16[8,384,512]{2,1,0:T(8,128)(2,1)} %regroup.1), calls=%async_computation | async-start | bytes 6291456 | tf_op jit(solution)/shard_map/all_to_all | solution.py:577
  18.5 7.9 %copy-start.16 = (bf16[1,2,4096]{2,1,0:T(2,128)(2,1)S(1)}, bf16[1,2,4096]{2,1,0:T(2,128)(2,1)}, u32[]{:S(2)}) copy-start(bf16[1,2,4096]{2,1,0:T(2,128)(2,1)} %param.40) | copy-start | bytes 49156
  18.5 8.6 %copy-start.11 = (bf16[7,4096]{1,0:T(8,128)(2,1)S(1)}, bf16[7,4096]{1,0:T(8,128)(2,1)}, u32[]{:S(2)}) copy-start(bf16[7,4096]{1,0:T(8,128)(2,1)} %param.31) | copy-start | bytes 172036
  18.5 9.2 %copy-start.19 = (s32[32]{0:T(128)S(1)}, s32[32]{0:T(128)}, u32[]{:S(2)}) copy-start(s32[32]{0:T(128)} %param.26) | copy-start | bytes 388
  18.5 9.9 %copy-start.15 = (bf16[2,4096]{1,0:T(2,128)(2,1)S(1)}, bf16[2,4096]{1,0:T(2,128)(2,1)}, u32[]{:S(2)}) copy-start(bf16[2,4096]{1,0:T(2,128)(2,1)} %param.30) | copy-start | bytes 49156
  18.5 46.2 %reduce-scatter.3.cloned.1.call-start = ((), (), s32[]{:S(2)}) async-start(), calls=%async_computation.3 | async-start | bytes 589824 | tf_op jit(solution)/shard_map/reduce_scatter | solution.py:543
  18.6 82.1 %collective-permute-start = (bf16[448,4096]{1,0:T(8,128)(2,1)}, bf16[448,4096]{1,0:T(8,128)(2,1)}, u32[]{:S(2)}, u32[]{:S(2)}) collective-permute-start(bf16[448,4096]{1,0:T(8,128)(2,1)} %refs_0_.3), channel_id=1, source_target_pairs={{0,8},{8,0},{16,24},{24,16},{1,9},{9,1},{17,25},{25,17},{2,10},{10... | collective-permute-start | bytes 11010056 | tf_op jit(solution)/shard_map/ppermute | solution.py:42
  20.1 81.8 %collective-permute-start.1 = (bf16[448,4096]{1,0:T(8,128)(2,1)}, bf16[448,4096]{1,0:T(8,128)(2,1)}, u32[]{:S(2)}, u32[]{:S(2)}) collective-permute-start(bf16[448,4096]{1,0:T(8,128)(2,1)} %refs_0_.3), channel_id=1, source_target_pairs={{0,16},{8,24},{16,0},{24,8},{1,17},{9,25},{17,1},{25,9},{2,18},{10... | collective-permute-start | bytes 11010056 | tf_op jit(solution)/shard_map/ppermute | solution.py:42
  24.7 30.4 %copy-start.14 = (bf16[128,512]{1,0:T(8,128)(2,1)S(1)}, bf16[128,512]{1,0:T(8,128)(2,1)}, u32[]{:S(2)}) copy-start(bf16[128,512]{1,0:T(8,128)(2,1)} %param.34) | copy-start | bytes 393220
  26.3 315.2 %all-reduce.2.cloned.1.call-start = ((), (), s32[]{:S(2)}) async-start(), calls=%async_computation.4 | async-start | bytes 8388608 | tf_op jit(solution)/shard_map/psum | solution.py:622
  97.1 17.7 %copy-start.6 = (bf16[4,384,512]{2,1,0:T(8,128)(2,1)}, bf16[4,384,512]{2,1,0:T(8,128)(2,1)S(1)}, u32[]{:S(2)}) copy-start(bf16[4,384,512]{2,1,0:T(8,128)(2,1)S(1)} %get-tuple-element.91) | copy-start | bytes 4718596
  97.1 17.7 %copy-start.7 = (bf16[4,384,512]{2,1,0:T(8,128)(2,1)}, bf16[4,384,512]{2,1,0:T(8,128)(2,1)S(1)}, u32[]{:S(2)}) copy-start(bf16[4,384,512]{2,1,0:T(8,128)(2,1)S(1)} %get-tuple-element.92) | copy-start | bytes 4718596
  101.9 37.4 %collective-permute-start.2 = (bf16[4,3,128,512]{3,2,1,0:T(8,128)(2,1)S(1)}, bf16[4,3,128,512]{3,2,1,0:T(8,128)(2,1)}, u32[]{:S(2)}, u32[]{:S(2)}) collective-permute-start(bf16[4,3,128,512]{3,2,1,0:T(8,128)(2,1)S(1)} %bitcast.38), channel_id=1, source_target_pairs={{0,8},{8,0},{16,24},{24,16},{1,9},{9,1},{17,25},{25,17},{2,10},{10... | collective-permute-start | bytes 4718600 | tf_op jit(solution)/shard_map/ppermute | solution.py:42
  102.4 68.9 %collective-permute-start.3 = (bf16[4,3,128,512]{3,2,1,0:T(8,128)(2,1)S(1)}, bf16[4,3,128,512]{3,2,1,0:T(8,128)(2,1)S(1)}, u32[]{:S(2)}, u32[]{:S(2)}) collective-permute-start(bf16[4,3,128,512]{3,2,1,0:T(8,128)(2,1)S(1)} %bitcast.35), channel_id=1, source_target_pairs={{0,8},{8,0},{16,24},{24,16},{1,9},{9,1},{17,25},{25,17},{2,10},{10... | collective-permute-start | bytes 4718600 | tf_op jit(solution)/shard_map/ppermute | solution.py:42
  103.9 67.4 %collective-permute-start.4 = (bf16[4,3,128,512]{3,2,1,0:T(8,128)(2,1)S(1)}, bf16[4,3,128,512]{3,2,1,0:T(8,128)(2,1)S(1)}, u32[]{:S(2)}, u32[]{:S(2)}) collective-permute-start(bf16[4,3,128,512]{3,2,1,0:T(8,128)(2,1)S(1)} %bitcast.39), channel_id=1, source_target_pairs={{0,16},{8,24},{16,0},{24,8},{1,17},{9,25},{17,1},{25,9},{2,18},{10... | collective-permute-start | bytes 4718600 | tf_op jit(solution)/shard_map/ppermute | solution.py:42
  105.4 67.4 %collective-permute-start.5 = (bf16[4,3,128,512]{3,2,1,0:T(8,128)(2,1)S(1)}, bf16[4,3,128,512]{3,2,1,0:T(8,128)(2,1)}, u32[]{:S(2)}, u32[]{:S(2)}) collective-permute-start(bf16[4,3,128,512]{3,2,1,0:T(8,128)(2,1)S(1)} %bitcast.36), channel_id=1, source_target_pairs={{0,16},{8,24},{16,0},{24,8},{1,17},{9,25},{17,1},{25,9},{2,18},{10... | collective-permute-start | bytes 4718600 | tf_op jit(solution)/shard_map/ppermute | solution.py:42
  114.8 95.4 %copy-start.3 = (f32[512]{0:T(512)S(1)}, f32[512]{0:T(512)}, u32[]{:S(2)}) copy-start(f32[512]{0:T(512)} %param.32) | copy-start | bytes 6148
  114.8 95.5 %copy-start.4 = (f32[512]{0:T(512)S(1)}, f32[512]{0:T(512)}, u32[]{:S(2)}) copy-start(f32[512]{0:T(512)} %param.35) | copy-start | bytes 6148
  114.9 95.4 %copy-start.5 = (f32[512]{0:T(512)S(1)}, f32[512]{0:T(512)}, u32[]{:S(2)}) copy-start(f32[512]{0:T(512)} %param.36) | copy-start | bytes 6148
  171.3 1.6 copy-start.9
  171.3 3.1 copy-start.10
  172.9 34.7 %collective-permute-start.6 = (bf16[4,3,128,512]{3,2,1,0:T(8,128)(2,1)}, bf16[4,3,128,512]{3,2,1,0:T(8,128)(2,1)S(1)}, u32[]{:S(2)}, u32[]{:S(2)}) collective-permute-start(bf16[4,3,128,512]{3,2,1,0:T(8,128)(2,1)} %collective-permute-done.2.refs_2_), channel_id=1, source_target_pairs={{0,16},{8,24},{16,0},{24,8},{1,17},{9,25},{17,1},{25,9},{2,18},{10... | collective-permute-start | bytes 4718600 | tf_op jit(solution)/shard_map/ppermute | solution.py:42
  174.4 34.5 %collective-permute-start.7 = (bf16[4,3,128,512]{3,2,1,0:T(8,128)(2,1)}, bf16[4,3,128,512]{3,2,1,0:T(8,128)(2,1)}, u32[]{:S(2)}, u32[]{:S(2)}) collective-permute-start(bf16[4,3,128,512]{3,2,1,0:T(8,128)(2,1)} %collective-permute-done.5.refs_5_), channel_id=1, source_target_pairs={{0,8},{8,0},{16,24},{24,16},{1,9},{9,1},{17,25},{25,17},{2,10},{10... | collective-permute-start | bytes 4718600 | tf_op jit(solution)/shard_map/ppermute | solution.py:42
  208.9 31.8 %collective-permute-start.8 = (bf16[176,4096]{1,0:T(8,128)(2,1)}, bf16[176,4096]{1,0:T(8,128)(2,1)}, u32[]{:S(2)}, u32[]{:S(2)}) collective-permute-start(bf16[176,4096]{1,0:T(8,128)(2,1)} %slice.62), channel_id=1, source_target_pairs={{0,16},{8,24},{16,0},{24,8},{1,17},{9,25},{17,1},{25,9},{2,18},{10... | collective-permute-start | bytes 4325384 | tf_op jit(solution)/shard_map/ppermute | solution.py:42
  209.6 31.1 %collective-permute-start.9 = (bf16[176,4096]{1,0:T(8,128)(2,1)}, bf16[176,4096]{1,0:T(8,128)(2,1)}, u32[]{:S(2)}, u32[]{:S(2)}) collective-permute-start(bf16[176,4096]{1,0:T(8,128)(2,1)} %slice.63), channel_id=1, source_target_pairs={{0,8},{8,0},{16,24},{24,16},{1,9},{9,1},{17,25},{25,17},{2,10},{10... | collective-permute-start | bytes 4325384 | tf_op jit(solution)/shard_map/ppermute | solution.py:42
  210.3 1.9 copy-start.2
  240.7 82.5 %collective-permute-start.10 = (bf16[448,4096]{1,0:T(8,128)(2,1)}, bf16[448,4096]{1,0:T(8,128)(2,1)}, u32[]{:S(2)}, u32[]{:S(2)}) collective-permute-start(bf16[448,4096]{1,0:T(8,128)(2,1)} %refs_0_.4), channel_id=1, source_target_pairs={{0,8},{8,0},{16,24},{24,16},{1,9},{9,1},{17,25},{25,17},{2,10},{10... | collective-permute-start | bytes 11010056 | tf_op jit(solution)/shard_map/ppermute | solution.py:42
  242.1 84.1 %collective-permute-start.11 = (bf16[448,4096]{1,0:T(8,128)(2,1)}, bf16[448,4096]{1,0:T(8,128)(2,1)}, u32[]{:S(2)}, u32[]{:S(2)}) collective-permute-start(bf16[448,4096]{1,0:T(8,128)(2,1)} %refs_0_.4), channel_id=1, source_target_pairs={{0,16},{8,24},{16,0},{24,8},{1,17},{9,25},{17,1},{25,9},{2,18},{10... | collective-permute-start | bytes 11010056 | tf_op jit(solution)/shard_map/ppermute | solution.py:42
  243.5 86.4 %collective-permute-start.12 = (bf16[48,4096]{1,0:T(8,128)(2,1)}, bf16[48,4096]{1,0:T(8,128)(2,1)S(1)}, u32[]{:S(2)}, u32[]{:S(2)}) collective-permute-start(bf16[48,4096]{1,0:T(8,128)(2,1)} %slice.64), channel_id=1, source_target_pairs={{0,16},{8,24},{16,0},{24,8},{1,17},{9,25},{17,1},{25,9},{2,18},{10... | collective-permute-start | bytes 1179656 | tf_op jit(solution)/shard_map/ppermute | solution.py:42
  244.2 85.7 %collective-permute-start.13 = (bf16[48,4096]{1,0:T(8,128)(2,1)}, bf16[48,4096]{1,0:T(8,128)(2,1)S(1)}, u32[]{:S(2)}, u32[]{:S(2)}) collective-permute-start(bf16[48,4096]{1,0:T(8,128)(2,1)} %slice.65), channel_id=1, source_target_pairs={{0,8},{8,0},{16,24},{24,16},{1,9},{9,1},{17,25},{25,17},{2,10},{10... | collective-permute-start | bytes 1179656 | tf_op jit(solution)/shard_map/ppermute | solution.py:42
  244.9 187.0 %reduce-scatter.5.cloned.1.call-start = ((), (), s32[]{:S(2)}) async-start(), calls=%async_computation.5 | async-start | bytes 4718592 | tf_op jit(solution)/shard_map/reduce_scatter | solution.py:647
  329.9 11.7 %copy-start.12 = (bf16[48,4096]{1,0:T(8,128)(2,1)}, bf16[48,4096]{1,0:T(8,128)(2,1)S(1)}, u32[]{:S(2)}) copy-start(bf16[48,4096]{1,0:T(8,128)(2,1)S(1)} %collective-permute-done.12.refs_4_) | copy-start | bytes 1179652
  329.9 11.7 %copy-start.13 = (bf16[48,4096]{1,0:T(8,128)(2,1)}, bf16[48,4096]{1,0:T(8,128)(2,1)S(1)}, u32[]{:S(2)}) copy-start(bf16[48,4096]{1,0:T(8,128)(2,1)S(1)} %collective-permute-done.13.refs_6_) | copy-start | bytes 1179652
  329.9 37.8 %collective-permute-start.14 = (bf16[224,4096]{1,0:T(8,128)(2,1)}, bf16[224,4096]{1,0:T(8,128)(2,1)S(1)}, u32[]{:S(2)}, u32[]{:S(2)}) collective-permute-start(bf16[224,4096]{1,0:T(8,128)(2,1)} %slice.80), channel_id=1, source_target_pairs={{0,16},{8,24},{16,0},{24,8},{1,17},{9,25},{17,1},{25,9},{2,18},{10... | collective-permute-start | bytes 5505032 | tf_op jit(solution)/shard_map/ppermute | solution.py:42
  331.3 36.4 %collective-permute-start.15 = (bf16[224,4096]{1,0:T(8,128)(2,1)}, bf16[224,4096]{1,0:T(8,128)(2,1)}, u32[]{:S(2)}, u32[]{:S(2)}) collective-permute-start(bf16[224,4096]{1,0:T(8,128)(2,1)} %slice.81), channel_id=1, source_target_pairs={{0,8},{8,0},{16,24},{24,16},{1,9},{9,1},{17,25},{25,17},{2,10},{10... | collective-permute-start | bytes 5505032 | tf_op jit(solution)/shard_map/ppermute | solution.py:42
  367.7 1.3 copy-start.8
  382.0 0.7 copy-start.17
  382.0 0.7 copy-start.18
  431.9 3.1 copy-start.1
Sparse Core Ops, SparseCore 0:
  26.4 33.8 reduce-scatter.2
  245.0 96.5 all-reduce.1
  382.1 49.7 reduce-scatter.4

commit v6 on v5

--- a/solution.py
+++ b/solution.py
@@ -468,39 +468,6 @@
     )(hidden, *values)
 
 
-def combine_kernel(slot_ref, length_ref, tokens_ref, attended_ref, gate_ref, *refs):
-    out_ref = refs[-1]
-    present = lax.broadcasted_iota(jnp.int32, gate_ref.shape, 0) < length_ref[0]
-    summed = jnp.concatenate([ref[...] for ref in refs[:-1]], axis=1).astype(F32)
-    accept = 1.0 / (1.0 + jnp.exp(-gate_ref[...]))
-    middle = (tokens_ref[...].astype(F32) + attended_ref[...].astype(F32)).astype(BF16)
-    combined = middle.astype(F32) + accept * summed
-    out_ref[...] = jnp.where(present, combined, 0.0).astype(BF16)
-
-
-def combine(slot, length, tokens, attended, gate, summed):
-    seq_len, wide = gate.shape
-    whole = pl.BlockSpec((seq_len, wide), lambda i, *_: (0, 0))
-    parts = [pl.BlockSpec(part.shape, lambda i, *_: (0, 0)) for part in summed]
-    return pl.pallas_call(
-        combine_kernel,
-        grid_spec=pltpu.PrefetchScalarGridSpec(
-            num_scalar_prefetch=2,
-            grid=(1,),
-            in_specs=[pl.BlockSpec((seq_len, wide), lambda i, slot, *_: (0, slot[0]))] * 2
-            + [whole]
-            + parts,
-            out_specs=whole,
-        ),
-        out_shape=jax.ShapeDtypeStruct((seq_len, wide), BF16),
-        compiler_params=pltpu.CompilerParams(vmem_limit_bytes=VMEM_BYTES),
-        cost_estimate=pl.CostEstimate(
-            flops=1 << 20, bytes_accessed=3 * MICROSECOND, transcendentals=0
-        ),
-        name="combine",
-    )(slot, length, tokens, attended, gate, *summed)
-
-
 def local(
     input_activations,
     prompt_extents,
@@ -645,9 +612,14 @@
     accept = matmul(accept_in, feedforward_accept_proj)
     terms = exit_product(hidden, value_rows)
     summed = lax.psum_scatter(terms, "hid", scatter_dimension=1, tiled=True)
-    layer_out = combine(
-        slot[None], prompt_extents, token_rows, attended, accept, [summed]
-    )[None]
+    present = (jnp.arange(seq_len) < length)[:, None]
+    first_column = slot * local_width
+    middle = lax.dynamic_slice_in_dim(token_rows, first_column, local_width, 1).astype(F32)
+    middle += lax.dynamic_slice_in_dim(attended, first_column, local_width, 1).astype(F32)
+    middle = jnp.where(present, middle.astype(BF16), 0)
+    accept = jnp.where(present, jax.nn.sigmoid(accept), 0.0)
+    middle, accept = hold((middle, accept))
+    layer_out = (middle.astype(F32) + accept * summed.astype(F32)).astype(BF16)[None]
     shift_out = jnp.concatenate([last_in, last_chan]).astype(BF16)[None]
     return (layer_out, new_state[None], shift_out)
 

time: 442 us -> 441 us (level)
  transfers between devices with their start and end apart: 20 -> 20, of which waited for: 13 -> 13; matrix products, arithmetic and copies ran while one was open for 9% -> 10% of each run, Pallas kernels for 21% -> 21%
where the time goes in v6:
time: 441 us; the launch traced here: 440 us
  waiting for transfers between devices  242 us (55%)
  Pallas kernels  111 us (25%)
  local copies, waits for them, and re-layouts  26.1 us (6%)
  starting transfers between devices  23.3 us (5%)
  between operations  16 us (4%)
  matrix products  15.7 us (4%)
  other arithmetic  6.39 us (1%)
    ppermute x16, waiting for transfers between devices, across(): return lax.ppermute(value, 'req', [(i, i ^ axis) for i in range(4)])  163 us
    reduce_scatter x1, waiting for transfers between devices, local(): summed = lax.psum_scatter(terms, 'hid', scatter_dimension=1, tiled=True)  40.8 us
    all_to_all x1, waiting for transfers between devices, to_heads(): lax.all_to_all(columns, 'hid', split_axis=0, concat_axis=0, tiled=True)  29.2 us
    pallas_call x1, Pallas kernels, recurrence(): pl.pallas_call(partial(recurrence_kernel, steps, len(far)), grid=(steps,)...  28.5 us
    pallas_call x1, Pallas kernels, channel_inputs(): pl.pallas_call(partial(channel_kernel, places[:-1], steps), grid=(steps,)...  25.8 us
    pallas_call x1, Pallas kernels, prepare(): pl.pallas_call(prepare_kernel, grid_spec=pltpu.PrefetchScalarGridSpec(num...  25.4 us
    ppermute x16, starting transfers between devices, across(): return lax.ppermute(value, 'req', [(i, i ^ axis) for i in range(4)])  16.8 us
    dot_general x3, matrix products, matmul(): return jnp.dot(a, b, preferred_element_type=F32)  15.7 us
  transfers between devices with their start and end apart: 20, of which 13 were waited for; matrix products, arithmetic and copies ran while one was open for 10% of the time, Pallas kernels for 21%

profile of v6, /device:TPU:0, one launch (start us, length us, event | category | flops | bytes accessed | tf_op | source)
XLA Modules:
  0.0 440.3 jit_solution(11110419206944648051)
XLA Ops:
  7.2 5.0 %regroup.1 = bf16[8,384,512]{2,1,0:T(8,128)(2,1)} custom-call(f32[128,4096]{1,0:T(8,128)} %refs_0_.2, f32[128,4096]{1,0:T(8,128)} %refs_1_.1, f32[128,4096]{1,0:T(8,128)} %refs_2_.1), custom_call_target="tpu_custom_call" | custom-call | bytes 20971520 | tf_op jit(solution)/shard_map/regroup/pallas_call | solution.py:299
  12.2 6.3 %all-to-all-start = ((bf16[8,384,512]{2,1,0:T(8,128)(2,1)}), bf16[8,384,512]{2,1,0:T(8,128)(2,1)}, u32[]{:S(2)}, u32[]{:S(2)}) async-start(bf16[8,384,512]{2,1,0:T(8,128)(2,1)} %regroup.1), calls=%async_computation | async-start | bytes 6291456 | tf_op jit(solution)/shard_map/all_to_all | solution.py:544
  18.6 1.6 collective-permute-start
  20.1 1.5 collective-permute-start.1
  23.0 1.7 convert_select_fusion
  24.7 1.6 select_n.54
  29.7 25.4 %prepare.1 = (bf16[3,512,4096]{2,1,0:T(8,128)(2,1)}, bf16[512,4096]{1,0:T(8,128)(2,1)}, bf16[512,4096]{1,0:T(8,128)(2,1)}, f32[1,4096]{1,0:T(1,128)}) custom-call(s32[32]{0:T(128)} %pad_add_fusion.order_ref, s32[1]{0:T(128)} %copy.26.length_ref, bf16[512,4096]{1,0:T(8,128)(2,1)} %bitcast.37, f32[1,4096]{1,0:T(1,128)} %get-tuple-element.100.gain_ref, ...), custom_call_target="tpu_custom_call" | custom-call | flops 1048576 | bytes 81180000 | tf_op jit(solution)/shard_map/prepare/pallas_call | solution.py:262
  55.1 3.8 fusion.5.refs_2_
  58.9 5.8 %fusion.12.refs_3_ = f32[512,512]{1,0:T(8,128)S(1)} fusion(bf16[512,4096]{1,0:T(8,128)(2,1)} %get-tuple-element.51, bf16[4096,512]{1,0:T(8,128)(2,1)} %param.37), kind=kOutput, calls=%fused_computation.25 | convolution fusion | flops 2147483648 | bytes 9437184 | tf_op jit(solution)/shard_map/dot_general | solution.py:30
  64.8 1.0 reshape.71.refs_7_
  65.8 29.2 %all-to-all-done = bf16[8,384,512]{2,1,0:T(8,128)(2,1)} async-done(((bf16[8,384,512]{2,1,0:T(8,128)(2,1)}), bf16[8,384,512]{2,1,0:T(8,128)(2,1)}, u32[]{:S(2)}, u32[]{:S(2)}) %all-to-all-start) | async-done | bytes 3145760 | tf_op jit(solution)/shard_map/all_to_all | solution.py:544
  95.0 2.1 fusion.9
  97.2 3.5 collective-permute-done.refs_1_
  100.7 1.2 collective-permute-done.1.refs_2_
  102.4 1.5 collective-permute-start.3
  103.9 1.5 collective-permute-start.4
  106.0 2.7 slice.62
  108.6 1.8 slice.64
  110.4 2.7 slice.63
  113.1 1.8 slice.65
  114.9 24.5 %collective-permute-done.2.refs_2_ = bf16[4,3,128,512]{3,2,1,0:T(8,128)(2,1)} collective-permute-done((bf16[4,3,128,512]{3,2,1,0:T(8,128)(2,1)S(1)}, bf16[4,3,128,512]{3,2,1,0:T(8,128)(2,1)}, u32[]{:S(2)}, u32[]{:S(2)}) %collective-permute-start.2) | collective-permute-done | bytes 1572896 | tf_op jit(solution)/shard_map/ppermute | solution.py:42
  139.3 32.0 %collective-permute-done.3.refs_3_ = bf16[4,3,128,512]{3,2,1,0:T(8,128)(2,1)S(1)} collective-permute-done((bf16[4,3,128,512]{3,2,1,0:T(8,128)(2,1)S(1)}, bf16[4,3,128,512]{3,2,1,0:T(8,128)(2,1)S(1)}, u32[]{:S(2)}, u32[]{:S(2)}) %collective-permute-start.3) | collective-permute-done | bytes 1572896 | tf_op jit(solution)/shard_map/ppermute | solution.py:42
  171.3 1.6 collective-permute-done.5.refs_5_
  172.9 1.5 collective-permute-start.6
  175.0 13.5 %project.1.base_ref = f32[3,512,512]{2,1,0:T(8,128)} custom-call(bf16[3,512,4096]{2,1,0:T(8,128)(2,1)} %get-tuple-element.52.values_ref, bf16[4,3,128,512]{3,2,1,0:T(8,128)(2,1)} %bitcast.44, bf16[4,3,128,512]{3,2,1,0:T(8,128)(2,1)} %bitcast.41, bf16[4,3,128,512]{3,2,1,0:T(8,128)(2,1)} %collective-permute-done.2.refs_2_, bf16[4,3,128,512]{3,2,1,0:T(8,128)(2,1)} %copy-done.9, ...), custom_call_target="tpu_custom_call" | custom-call | flops 1048576 | bytes 47970000 | tf_op jit(solution)/shard_map/project/pallas_call | solution.py:331
  188.5 19.1 %collective-permute-done.6.refs_0_ = bf16[4,3,128,512]{3,2,1,0:T(8,128)(2,1)S(1)} collective-permute-done((bf16[4,3,128,512]{3,2,1,0:T(8,128)(2,1)}, bf16[4,3,128,512]{3,2,1,0:T(8,128)(2,1)S(1)}, u32[]{:S(2)}, u32[]{:S(2)}) %collective-permute-start.6) | collective-permute-done | bytes 1572896 | tf_op jit(solution)/shard_map/ppermute | solution.py:42
  207.6 1.3 collective-permute-done.7.refs_1_
  208.9 0.7 collective-permute-start.8
  209.6 0.7 collective-permute-start.9
  210.3 1.9 copy-done.2
  212.2 28.5 %recurrence.1 = (bf16[512,4096]{1,0:T(8,128)(2,1)}, f32[8,64,64]{2,1,0:T(8,128)}) custom-call(s32[1]{0:T(128)} %copy.26.length_ref, f32[3,512,512]{2,1,0:T(8,128)S(1)} %copy-done.2, bf16[3,512,4096]{2,1,0:T(8,128)(2,1)} %get-tuple-element.52.values_ref, bf16[4,3,128,512]{3,2,1,0:T(8,128)(2,1)S(1)} %collective-permute-done.6.refs_0_, ...), custom_call_target="tpu_custom_call" | custom-call | flops 1048576 | bytes 88560000 | tf_op jit(solution)/shard_map/recurrence/pallas_call | solution.py:178
  240.7 1.4 collective-permute-start.10
  242.1 1.3 collective-permute-start.11
  243.5 0.7 collective-permute-start.12
  244.2 0.7 collective-permute-start.13
  244.9 78.3 %collective-permute-done.10.refs_1_ = bf16[448,4096]{1,0:T(8,128)(2,1)} collective-permute-done((bf16[448,4096]{1,0:T(8,128)(2,1)}, bf16[448,4096]{1,0:T(8,128)(2,1)}, u32[]{:S(2)}, u32[]{:S(2)}) %collective-permute-start.10) | collective-permute-done | bytes 3670048 | tf_op jit(solution)/shard_map/ppermute | solution.py:42
  323.2 2.9 slice.80
  326.2 3.0 slice.81
  329.2 0.7 collective-permute-done.12.refs_4_
  329.9 1.4 collective-permute-start.14
  332.6 9.0 %all-reduce.2.cloned.1.call-done.attended_ref = bf16[512,4096]{1,0:T(8,128)(2,1)} async-done(((bf16[512,4096]{1,0:T(8,128)(2,1)}), bf16[512,4096]{1,0:T(8,128)(2,1)}) %all-reduce.2.cloned.1.call-update) | async-done | bytes 4194320 | tf_op jit(solution)/shard_map/psum | solution.py:589
  341.6 25.8 %channel_inputs.1 = (bf16[512,1792]{1,0:T(8,128)(2,1)}, bf16[512,4096]{1,0:T(8,128)(2,1)}, f32[1,4096]{1,0:T(1,128)}) custom-call(s32[1]{0:T(128)} %copy.26.length_ref, bf16[512,4096]{1,0:T(8,128)(2,1)} %bitcast.38, bf16[512,4096]{1,0:T(8,128)(2,1)} %all-reduce.2.cloned.1.call-done.attended_ref, f32[1,4096]{1,0:T(1,128)} %get-tuple-element.99.gain_ref, ...), custom_call_target="tpu_custom_call" | custom-call | flops 1048576 | bytes 81180000 | tf_op jit(solution)/shard_map/channel_inputs/pallas_call | solution.py:411
  367.7 1.3 copy-done.8
  369.0 13.0 %exit_product.1 = bf16[512,4096]{1,0:T(8,128)(2,1)} custom-call(bf16[512,1792]{1,0:T(8,128)(2,1)} %get-tuple-element.89.hidden_ref, bf16[448,4096]{1,0:T(8,128)(2,1)} %refs_0_.4, bf16[448,4096]{1,0:T(8,128)(2,1)} %collective-permute-done.10.refs_1_, bf16[448,4096]{1,0:T(8,128)(2,1)} %collective-permute-done.11.refs_2_, bf16[224,4096]{1,0:T(8,128)(2,1)} %copy-done.8, ...), custom_call_target="tpu_custom_call" | custom-call | flops 1048576 | bytes 25830000 | tf_op jit(solution)/shard_map/exit_product/pallas_call | solution.py:456
  382.7 1.4 fusion.8
  384.1 6.0 %fusion.3 = f32[512,512]{1,0:T(8,128)S(1)} fusion(bf16[512,4096]{1,0:T(8,128)(2,1)} %get-tuple-element.86, bf16[4096,512]{1,0:T(8,128)(2,1)} %param.43, pred[512]{0:T(512)(128)(4,1)S(1)} %iota_compare_fusion), kind=kOutput, calls=%fused_computation.4 | convolution fusion | flops 2148532224 | bytes 9437696 | tf_op jit(solution)/shard_map/dot_general | solution.py:30
  390.9 40.8 %reduce-scatter.5.cloned.1.call-done = bf16[512,512]{1,0:T(8,128)(2,1)} async-done(((bf16[512,4096]{1,0:T(8,128)(2,1)}), bf16[512,512]{1,0:T(8,128)(2,1)}) %reduce-scatter.5.cloned.1.call-update) | async-done | bytes 524304 | tf_op jit(solution)/shard_map/reduce_scatter | solution.py:614
  431.7 2.0 fusion.7
  (67 shorter events, 7.5 us)
Async XLA Ops:
  7.2 47.9 %copy-start = (bf16[4096,128]{1,0:T(8,128)(2,1)S(1)}, bf16[4096,128]{1,0:T(8,128)(2,1)}, u32[]{:S(2)}) copy-start(bf16[4096,128]{1,0:T(8,128)(2,1)} %param.33) | copy-start | bytes 3145732
  12.2 82.9 %all-to-all-start = ((bf16[8,384,512]{2,1,0:T(8,128)(2,1)}), bf16[8,384,512]{2,1,0:T(8,128)(2,1)}, u32[]{:S(2)}, u32[]{:S(2)}) async-start(bf16[8,384,512]{2,1,0:T(8,128)(2,1)} %regroup.1), calls=%async_computation | async-start | bytes 6291456 | tf_op jit(solution)/shard_map/all_to_all | solution.py:544
  18.5 7.9 %copy-start.16 = (bf16[1,2,4096]{2,1,0:T(2,128)(2,1)S(1)}, bf16[1,2,4096]{2,1,0:T(2,128)(2,1)}, u32[]{:S(2)}) copy-start(bf16[1,2,4096]{2,1,0:T(2,128)(2,1)} %param.40) | copy-start | bytes 49156
  18.5 8.6 %copy-start.11 = (bf16[7,4096]{1,0:T(8,128)(2,1)S(1)}, bf16[7,4096]{1,0:T(8,128)(2,1)}, u32[]{:S(2)}) copy-start(bf16[7,4096]{1,0:T(8,128)(2,1)} %param.31) | copy-start | bytes 172036
  18.5 9.2 %copy-start.19 = (s32[32]{0:T(128)S(1)}, s32[32]{0:T(128)}, u32[]{:S(2)}) copy-start(s32[32]{0:T(128)} %param.26) | copy-start | bytes 388
  18.5 9.9 %copy-start.15 = (bf16[2,4096]{1,0:T(2,128)(2,1)S(1)}, bf16[2,4096]{1,0:T(2,128)(2,1)}, u32[]{:S(2)}) copy-start(bf16[2,4096]{1,0:T(2,128)(2,1)} %param.30) | copy-start | bytes 49156
  18.5 46.2 %reduce-scatter.3.cloned.1.call-start = ((), (), s32[]{:S(2)}) async-start(), calls=%async_computation.3 | async-start | bytes 589824 | tf_op jit(solution)/shard_map/reduce_scatter | solution.py:510
  18.6 82.1 %collective-permute-start = (bf16[448,4096]{1,0:T(8,128)(2,1)}, bf16[448,4096]{1,0:T(8,128)(2,1)}, u32[]{:S(2)}, u32[]{:S(2)}) collective-permute-start(bf16[448,4096]{1,0:T(8,128)(2,1)} %refs_0_.3), channel_id=1, source_target_pairs={{0,8},{8,0},{16,24},{24,16},{1,9},{9,1},{17,25},{25,17},{2,10},{10... | collective-permute-start | bytes 11010056 | tf_op jit(solution)/shard_map/ppermute | solution.py:42
  20.1 81.8 %collective-permute-start.1 = (bf16[448,4096]{1,0:T(8,128)(2,1)}, bf16[448,4096]{1,0:T(8,128)(2,1)}, u32[]{:S(2)}, u32[]{:S(2)}) collective-permute-start(bf16[448,4096]{1,0:T(8,128)(2,1)} %refs_0_.3), channel_id=1, source_target_pairs={{0,16},{8,24},{16,0},{24,8},{1,17},{9,25},{17,1},{25,9},{2,18},{10... | collective-permute-start | bytes 11010056 | tf_op jit(solution)/shard_map/ppermute | solution.py:42
  24.7 30.4 %copy-start.14 = (bf16[128,512]{1,0:T(8,128)(2,1)S(1)}, bf16[128,512]{1,0:T(8,128)(2,1)}, u32[]{:S(2)}) copy-start(bf16[128,512]{1,0:T(8,128)(2,1)} %param.34) | copy-start | bytes 393220
  26.3 315.2 %all-reduce.2.cloned.1.call-start = ((), (), s32[]{:S(2)}) async-start(), calls=%async_computation.4 | async-start | bytes 8388608 | tf_op jit(solution)/shard_map/psum | solution.py:589
  97.1 17.7 %copy-start.6 = (bf16[4,384,512]{2,1,0:T(8,128)(2,1)}, bf16[4,384,512]{2,1,0:T(8,128)(2,1)S(1)}, u32[]{:S(2)}) copy-start(bf16[4,384,512]{2,1,0:T(8,128)(2,1)S(1)} %get-tuple-element.95) | copy-start | bytes 4718596
  97.1 17.7 %copy-start.7 = (bf16[4,384,512]{2,1,0:T(8,128)(2,1)}, bf16[4,384,512]{2,1,0:T(8,128)(2,1)S(1)}, u32[]{:S(2)}) copy-start(bf16[4,384,512]{2,1,0:T(8,128)(2,1)S(1)} %get-tuple-element.96) | copy-start | bytes 4718596
  101.9 37.4 %collective-permute-start.2 = (bf16[4,3,128,512]{3,2,1,0:T(8,128)(2,1)S(1)}, bf16[4,3,128,512]{3,2,1,0:T(8,128)(2,1)}, u32[]{:S(2)}, u32[]{:S(2)}) collective-permute-start(bf16[4,3,128,512]{3,2,1,0:T(8,128)(2,1)S(1)} %bitcast.42), channel_id=1, source_target_pairs={{0,8},{8,0},{16,24},{24,16},{1,9},{9,1},{17,25},{25,17},{2,10},{10... | collective-permute-start | bytes 4718600 | tf_op jit(solution)/shard_map/ppermute | solution.py:42
  102.4 68.9 %collective-permute-start.3 = (bf16[4,3,128,512]{3,2,1,0:T(8,128)(2,1)S(1)}, bf16[4,3,128,512]{3,2,1,0:T(8,128)(2,1)S(1)}, u32[]{:S(2)}, u32[]{:S(2)}) collective-permute-start(bf16[4,3,128,512]{3,2,1,0:T(8,128)(2,1)S(1)} %bitcast.39), channel_id=1, source_target_pairs={{0,8},{8,0},{16,24},{24,16},{1,9},{9,1},{17,25},{25,17},{2,10},{10... | collective-permute-start | bytes 4718600 | tf_op jit(solution)/shard_map/ppermute | solution.py:42
  103.9 67.4 %collective-permute-start.4 = (bf16[4,3,128,512]{3,2,1,0:T(8,128)(2,1)S(1)}, bf16[4,3,128,512]{3,2,1,0:T(8,128)(2,1)S(1)}, u32[]{:S(2)}, u32[]{:S(2)}) collective-permute-start(bf16[4,3,128,512]{3,2,1,0:T(8,128)(2,1)S(1)} %bitcast.43), channel_id=1, source_target_pairs={{0,16},{8,24},{16,0},{24,8},{1,17},{9,25},{17,1},{25,9},{2,18},{10... | collective-permute-start | bytes 4718600 | tf_op jit(solution)/shard_map/ppermute | solution.py:42
  105.4 67.4 %collective-permute-start.5 = (bf16[4,3,128,512]{3,2,1,0:T(8,128)(2,1)S(1)}, bf16[4,3,128,512]{3,2,1,0:T(8,128)(2,1)}, u32[]{:S(2)}, u32[]{:S(2)}) collective-permute-start(bf16[4,3,128,512]{3,2,1,0:T(8,128)(2,1)S(1)} %bitcast.40), channel_id=1, source_target_pairs={{0,16},{8,24},{16,0},{24,8},{1,17},{9,25},{17,1},{25,9},{2,18},{10... | collective-permute-start | bytes 4718600 | tf_op jit(solution)/shard_map/ppermute | solution.py:42
  114.8 95.4 %copy-start.3 = (f32[512]{0:T(512)S(1)}, f32[512]{0:T(512)}, u32[]{:S(2)}) copy-start(f32[512]{0:T(512)} %param.32) | copy-start | bytes 6148
  114.8 95.5 %copy-start.4 = (f32[512]{0:T(512)S(1)}, f32[512]{0:T(512)}, u32[]{:S(2)}) copy-start(f32[512]{0:T(512)} %param.35) | copy-start | bytes 6148
  114.9 95.4 %copy-start.5 = (f32[512]{0:T(512)S(1)}, f32[512]{0:T(512)}, u32[]{:S(2)}) copy-start(f32[512]{0:T(512)} %param.36) | copy-start | bytes 6148
  171.3 1.6 copy-start.9
  171.3 3.1 copy-start.10
  172.9 34.7 %collective-permute-start.6 = (bf16[4,3,128,512]{3,2,1,0:T(8,128)(2,1)}, bf16[4,3,128,512]{3,2,1,0:T(8,128)(2,1)S(1)}, u32[]{:S(2)}, u32[]{:S(2)}) collective-permute-start(bf16[4,3,128,512]{3,2,1,0:T(8,128)(2,1)} %collective-permute-done.2.refs_2_), channel_id=1, source_target_pairs={{0,16},{8,24},{16,0},{24,8},{1,17},{9,25},{17,1},{25,9},{2,18},{10... | collective-permute-start | bytes 4718600 | tf_op jit(solution)/shard_map/ppermute | solution.py:42
  174.4 34.5 %collective-permute-start.7 = (bf16[4,3,128,512]{3,2,1,0:T(8,128)(2,1)}, bf16[4,3,128,512]{3,2,1,0:T(8,128)(2,1)}, u32[]{:S(2)}, u32[]{:S(2)}) collective-permute-start(bf16[4,3,128,512]{3,2,1,0:T(8,128)(2,1)} %collective-permute-done.5.refs_5_), channel_id=1, source_target_pairs={{0,8},{8,0},{16,24},{24,16},{1,9},{9,1},{17,25},{25,17},{2,10},{10... | collective-permute-start | bytes 4718600 | tf_op jit(solution)/shard_map/ppermute | solution.py:42
  208.9 31.8 %collective-permute-start.8 = (bf16[176,4096]{1,0:T(8,128)(2,1)}, bf16[176,4096]{1,0:T(8,128)(2,1)}, u32[]{:S(2)}, u32[]{:S(2)}) collective-permute-start(bf16[176,4096]{1,0:T(8,128)(2,1)} %slice.62), channel_id=1, source_target_pairs={{0,16},{8,24},{16,0},{24,8},{1,17},{9,25},{17,1},{25,9},{2,18},{10... | collective-permute-start | bytes 4325384 | tf_op jit(solution)/shard_map/ppermute | solution.py:42
  209.6 31.1 %collective-permute-start.9 = (bf16[176,4096]{1,0:T(8,128)(2,1)}, bf16[176,4096]{1,0:T(8,128)(2,1)}, u32[]{:S(2)}, u32[]{:S(2)}) collective-permute-start(bf16[176,4096]{1,0:T(8,128)(2,1)} %slice.63), channel_id=1, source_target_pairs={{0,8},{8,0},{16,24},{24,16},{1,9},{9,1},{17,25},{25,17},{2,10},{10... | collective-permute-start | bytes 4325384 | tf_op jit(solution)/shard_map/ppermute | solution.py:42
  210.3 1.9 copy-start.2
  240.7 82.5 %collective-permute-start.10 = (bf16[448,4096]{1,0:T(8,128)(2,1)}, bf16[448,4096]{1,0:T(8,128)(2,1)}, u32[]{:S(2)}, u32[]{:S(2)}) collective-permute-start(bf16[448,4096]{1,0:T(8,128)(2,1)} %refs_0_.4), channel_id=1, source_target_pairs={{0,8},{8,0},{16,24},{24,16},{1,9},{9,1},{17,25},{25,17},{2,10},{10... | collective-permute-start | bytes 11010056 | tf_op jit(solution)/shard_map/ppermute | solution.py:42
  242.1 84.1 %collective-permute-start.11 = (bf16[448,4096]{1,0:T(8,128)(2,1)}, bf16[448,4096]{1,0:T(8,128)(2,1)}, u32[]{:S(2)}, u32[]{:S(2)}) collective-permute-start(bf16[448,4096]{1,0:T(8,128)(2,1)} %refs_0_.4), channel_id=1, source_target_pairs={{0,16},{8,24},{16,0},{24,8},{1,17},{9,25},{17,1},{25,9},{2,18},{10... | collective-permute-start | bytes 11010056 | tf_op jit(solution)/shard_map/ppermute | solution.py:42
  243.5 86.4 %collective-permute-start.12 = (bf16[48,4096]{1,0:T(8,128)(2,1)}, bf16[48,4096]{1,0:T(8,128)(2,1)S(1)}, u32[]{:S(2)}, u32[]{:S(2)}) collective-permute-start(bf16[48,4096]{1,0:T(8,128)(2,1)} %slice.64), channel_id=1, source_target_pairs={{0,16},{8,24},{16,0},{24,8},{1,17},{9,25},{17,1},{25,9},{2,18},{10... | collective-permute-start | bytes 1179656 | tf_op jit(solution)/shard_map/ppermute | solution.py:42
  244.2 85.7 %collective-permute-start.13 = (bf16[48,4096]{1,0:T(8,128)(2,1)}, bf16[48,4096]{1,0:T(8,128)(2,1)S(1)}, u32[]{:S(2)}, u32[]{:S(2)}) collective-permute-start(bf16[48,4096]{1,0:T(8,128)(2,1)} %slice.65), channel_id=1, source_target_pairs={{0,8},{8,0},{16,24},{24,16},{1,9},{9,1},{17,25},{25,17},{2,10},{10... | collective-permute-start | bytes 1179656 | tf_op jit(solution)/shard_map/ppermute | solution.py:42
  244.9 186.8 %reduce-scatter.5.cloned.1.call-start = ((), (), s32[]{:S(2)}) async-start(), calls=%async_computation.5 | async-start | bytes 4718592 | tf_op jit(solution)/shard_map/reduce_scatter | solution.py:614
  329.9 11.7 %copy-start.12 = (bf16[48,4096]{1,0:T(8,128)(2,1)}, bf16[48,4096]{1,0:T(8,128)(2,1)S(1)}, u32[]{:S(2)}) copy-start(bf16[48,4096]{1,0:T(8,128)(2,1)S(1)} %collective-permute-done.12.refs_4_) | copy-start | bytes 1179652
  329.9 11.7 %copy-start.13 = (bf16[48,4096]{1,0:T(8,128)(2,1)}, bf16[48,4096]{1,0:T(8,128)(2,1)S(1)}, u32[]{:S(2)}) copy-start(bf16[48,4096]{1,0:T(8,128)(2,1)S(1)} %collective-permute-done.13.refs_6_) | copy-start | bytes 1179652
  329.9 37.8 %collective-permute-start.14 = (bf16[224,4096]{1,0:T(8,128)(2,1)}, bf16[224,4096]{1,0:T(8,128)(2,1)S(1)}, u32[]{:S(2)}, u32[]{:S(2)}) collective-permute-start(bf16[224,4096]{1,0:T(8,128)(2,1)} %slice.80), channel_id=1, source_target_pairs={{0,16},{8,24},{16,0},{24,8},{1,17},{9,25},{17,1},{25,9},{2,18},{10... | collective-permute-start | bytes 5505032 | tf_op jit(solution)/shard_map/ppermute | solution.py:42
  331.3 36.4 %collective-permute-start.15 = (bf16[224,4096]{1,0:T(8,128)(2,1)}, bf16[224,4096]{1,0:T(8,128)(2,1)}, u32[]{:S(2)}, u32[]{:S(2)}) collective-permute-start(bf16[224,4096]{1,0:T(8,128)(2,1)} %slice.81), channel_id=1, source_target_pairs={{0,8},{8,0},{16,24},{24,16},{1,9},{9,1},{17,25},{25,17},{2,10},{10... | collective-permute-start | bytes 5505032 | tf_op jit(solution)/shard_map/ppermute | solution.py:42
  367.7 1.3 copy-start.8
  382.0 0.7 copy-start.17
  384.1 6.1 %copy-start.18 = (f32[1,4096]{1,0:T(1,128)S(1)}, f32[1,4096]{1,0:T(1,128)}, u32[]{:S(2)}) copy-start(f32[1,4096]{1,0:T(1,128)} %get-tuple-element.94) | copy-start | bytes 49156
  384.1 49.6 %copy-start.1 = (bf16[4096,128]{1,0:T(8,128)(2,1)S(1)}, bf16[4096,128]{1,0:T(8,128)(2,1)}, u32[]{:S(2)}) copy-start(bf16[4096,128]{1,0:T(8,128)(2,1)} %param.33) | copy-start | bytes 3145732
Sparse Core Ops, SparseCore 0:
  26.4 33.8 reduce-scatter.2
  245.0 96.5 all-reduce.1
  382.1 49.4 reduce-scatter.4
